TPU v7x, 256 devices: a whole 4x4x8 slice. The times are simulated.
256 devices in a mesh: dp: 64 (over x, z, y_lo), head: 4 (over y_hi, core).
Axes of the slice: x: 4, y: 4 (y_hi: 2, y_lo: 2; y = y_hi * 2 + y_lo), z: 8, core: 2. Of those that a mesh axis runs over, the one named last changes fastest.
Arguments:
- vision_tokens: bfloat16 [512, 256, 1536], P('dp', 'head'), may hold values from -6 to 6
- memory_projector: bfloat16 [1536, 2, 1536], P(None, None, 'head'), may hold values from -0.15625 to 0.15625
- query_vectors: bfloat16 [16, 96], P('head'), may hold values from -4 to 4
- final_projector: bfloat16 [1536, 1536], P('head'), may hold values from -0.89304314 to 0.89304314
- caption_vectors: bfloat16 [512, 1536], P('dp'), may hold values from -40 to 40
- logit_multiplier: float32 [], replicated, may hold values from 8 to 16
- logit_shift: float32 [], replicated, may hold values from -4 to -2
Outputs:
- image_grad: float32 [512, 1536], P(('dp', 'head'))
- text_grad: float32 [512, 1536], P(('dp', 'head'))
All inputs are finite; a program needn't handle non-finite values.
Results may differ from a plain program's by a relative error of at most 0.0055.
Values may be sent and summed in bfloat16 or wider, within the bound.
No kernel may reach another device: no remote copies, remote signals or barrier semaphores. Data moves between devices by JAX's collectives and lax.ppermute only.
A program may use at most 64 MiB of HBM per device.

v0:
```python
import math

import jax
import jax.numpy as jnp
from jax import lax
from jax.sharding import PartitionSpec as P


def unit_rows(values):
    widened = values.astype(jnp.float32)
    return (widened * lax.rsqrt(jnp.sum(widened * widened, -1, keepdims=True) + 1e-06)).astype(
        jnp.bfloat16
    )


def per_device(
    vision_tokens,
    memory_projector,
    query_vectors,
    final_projector,
    caption_vectors,
    logit_multiplier,
    logit_shift,
):
    image_count = vision_tokens.shape[0]
    heads_here = query_vectors.shape[0]
    head_size = query_vectors.shape[1]
    projection = memory_projector.reshape(memory_projector.shape[0], -1)
    key_width = projection.shape[1] // 2
    token_piece = lax.all_gather(vision_tokens, "head", axis=1, tiled=True)
    token_rows = token_piece.shape[1]
    flattened = token_piece.reshape(image_count * token_rows, token_piece.shape[2])
    projected = jnp.dot(flattened, projection, preferred_element_type=jnp.float32).astype(
        jnp.bfloat16
    )
    keys_values = projected.reshape(image_count, token_rows, projection.shape[1])
    token_total = keys_values.shape[1]
    key_rows = keys_values[:, :, :key_width].reshape(
        image_count, token_total, heads_here, head_size
    )
    value_rows = keys_values[:, :, key_width:].reshape(
        image_count, token_total, heads_here, head_size
    )
    scores = jnp.einsum(
        "bphe,he->bhp", key_rows, query_vectors, preferred_element_type=jnp.float32
    ) / math.sqrt(head_size)
    raised = jnp.exp(scores)
    weights = (raised / jnp.sum(raised, -1, keepdims=True)).astype(jnp.bfloat16)
    pooled = jnp.einsum("bhp,bphe->bhe", weights, value_rows, preferred_element_type=jnp.float32)
    pooled = pooled.astype(jnp.bfloat16).reshape(image_count, heads_here * head_size)
    share_rows = image_count // lax.axis_size("head")
    quarter_start = lax.axis_index("head") * share_rows
    partial_embed = jnp.dot(pooled, final_projector, preferred_element_type=jnp.float32)
    embedding = lax.psum(partial_embed, "head")
    first_row = lax.axis_index("dp") * image_count
    picture_unitlength = unit_rows(embedding)
    caption_unitlength = unit_rows(caption_vectors)
    row_count = picture_unitlength.shape[0]
    image_ids = first_row + jnp.arange(row_count, dtype=jnp.int32)
    text_piece = lax.all_gather(caption_unitlength, "dp", axis=0, tiled=True)
    span_rows = text_piece.shape[0]
    similarity_matrix = lax.dot_general(
        picture_unitlength, text_piece, (((1,), (1,)), ((), ())), preferred_element_type=jnp.float32
    )
    match_scores = logit_multiplier * similarity_matrix + logit_shift
    text_ids = jnp.arange(span_rows, dtype=jnp.int32)
    target_signs = (image_ids[:, None] == text_ids[None, :]).astype(jnp.float32)
    objective_factor = (logit_multiplier * (jax.nn.sigmoid(match_scores) - target_signs)).astype(
        jnp.bfloat16
    )
    grad_rows = jnp.dot(objective_factor, text_piece, preferred_element_type=jnp.float32)
    coefficients = objective_factor
    coefficients, grad_rows = (coefficients, grad_rows)
    image_grad = lax.dynamic_slice_in_dim(grad_rows, quarter_start, share_rows, 0)
    own_images = lax.dynamic_slice_in_dim(picture_unitlength, quarter_start, share_rows, 0)
    own_coefficients = lax.dynamic_slice_in_dim(coefficients, quarter_start, share_rows, 0)
    text_grad = lax.psum_scatter(
        lax.dot_general(
            own_coefficients,
            own_images,
            (((0,), (0,)), ((), ())),
            preferred_element_type=jnp.float32,
        ),
        ("dp", "head"),
        scatter_dimension=0,
        tiled=True,
    )
    return (image_grad, text_grad)


def solution(mesh):
    in_specs = (
        P("dp", "head", None),
        P(None, None, "head"),
        P("head", None),
        P("head", None),
        P("dp", None),
        P(),
        P(),
    )
    out_specs = (P(("dp", "head"), None), P(("dp", "head"), None))
    return jax.shard_map(
        per_device, mesh=mesh, in_specs=in_specs, out_specs=out_specs, check_vma=False
    )
```

profile of v0, /device:TPU:2, one launch (start us, length us, event | category | flops | bytes accessed | tf_op | source)
XLA Modules:
  0.0 641.0 jit_solution(8589704932940047597)
XLA Ops:
  7.2 0.7 all-gather.3.cloned.1.call-update
  8.0 0.1 fusion.14
  8.1 0.7 fusion.15
  8.9 2.1 copy.22
  12.4 53.5 %all-gather.3.cloned.1.call-done = bf16[8,256,1536]{2,1,0:T(8,128)(2,1)} async-done(((bf16[8,64,1536]{2,1,0:T(8,128)(2,1)}), bf16[8,256,1536]{2,1,0:T(8,128)(2,1)}) %all-gather.3.cloned.1.call-update) | async-done | bytes 6291472 | tf_op jit(solution)/shard_map/all_gather | solution.py:30
  65.8 8.2 %convolution_convert_fusion = bf16[2048,768]{1,0:T(8,128)(2,1)S(1)} fusion(bf16[2048,1536]{1,0:T(8,128)(2,1)} %bitcast.39, bf16[1536,768]{1,0:T(8,128)(2,1)S(1)} %bitcast.36), kind=kOutput, calls=%fused_computation.1 | convolution fusion | flops 4833411072 | bytes 11796480 | tf_op jit(solution)/shard_map/dot_general | solution.py:33
  74.0 1.5 fusion.28
  75.5 1.6 copy.20
  77.2 1.7 copy.21
  78.9 1.7 fusion.1
  80.6 0.1 fusion.12
  80.7 0.5 fusion.18
  81.2 0.1 reshape.44
  81.3 0.3 fusion.29
  81.6 14.9 %psum.7 = f32[8,1536]{1,0:T(8,128)S(1)} all-reduce(f32[8,1536]{1,0:T(8,128)S(1)} %fusion.29), channel_id=1, replica_groups=mesh['dp'=64,'head'=4] {'head'}, use_global_device_ids=true, to_apply=%region_1.0 | all-reduce | flops 12288 | bytes 98304 | tf_op jit(solution)/shard_map/psum | solution.py:54
  96.5 0.1 multiply_reduce_fusion
  96.7 246.6 %all-gather.5.cloned.1.call-done = bf16[512,1536]{1,0:T(8,128)(2,1)} async-done(((bf16[8,1536]{1,0:T(8,128)(2,1)}), bf16[512,1536]{1,0:T(8,128)(2,1)}) %all-gather.5.cloned.1.call-update) | async-done | bytes 1572880 | tf_op jit(solution)/shard_map/all_gather | solution.py:60
  343.4 1.9 fusion.13
  345.3 2.3 fusion.22
  347.7 1.4 copy-done.1
  349.0 0.3 fusion.30
  349.3 0.6 constant_dynamic-slice_fusion
  350.0 283.1 %all-reduce.3.cloned.1.call-done = f32[512,1536]{1,0:T(8,128)} async-done(((f32[512,1536]{1,0:T(8,128)}), f32[512,1536]{1,0:T(8,128)}) %all-reduce.3.cloned.1.call-update) | async-done | bytes 3145744
  633.1 1.4 constant_dynamic-slice_fusion.1
  (17 shorter events, 0.3 us)
Async XLA Ops:
  7.2 74.2 %copy-start = (bf16[384,1536]{1,0:T(8,128)(2,1)S(1)}, bf16[384,1536]{1,0:T(8,128)(2,1)}, u32[]{:S(2)}) copy-start(bf16[384,1536]{1,0:T(8,128)(2,1)} %param.10) | copy-start | bytes 3538948
  7.2 0.8 copy-start.2
  7.2 58.6 %all-gather.3.cloned.1.call-start = ((), (), s32[]{:S(2)}) async-start(), calls=%async_computation | async-start | bytes 7864320 | tf_op jit(solution)/shard_map/all_gather | solution.py:30
  7.9 335.4 %all-gather.5.cloned.1.call-start = ((), (), s32[]{:S(2)}) async-start(), calls=%async_computation.1 | async-start | bytes 1597440 | tf_op jit(solution)/shard_map/all_gather | solution.py:60
  8.8 624.2 %all-reduce.3.cloned.1.call-start = ((), (), s32[]{:S(2)}) async-start(), calls=%async_computation.2 | async-start | bytes 6291456
  77.2 1.7 copy-start.3
  347.6 1.4 copy-start.1
Sparse Core Ops, SparseCore 0:
  9.8 55.9 all-gather.2
  67.6 275.7 all-gather.4
  348.8 284.2 all-reduce.2
where the time goes:
time: 641 us
  waiting for transfers between devices  584 us (91%)
  matrix products  15.3 us (2%)
  between operations  15.1 us (2%)
  blocking collectives  14.9 us (2%)
  local copies, waits for them, and re-layouts  10.5 us (2%)
    unnamed x4, waiting for transfers between devices  284 us
    all_gather x1, waiting for transfers between devices, per_device(): text_piece = lax.all_gather(caption_unitlength, 'dp', axis=0, tiled=True)  247 us
    all_gather x1, waiting for transfers between devices, per_device(): token_piece = lax.all_gather(vision_tokens, 'head', axis=1, tiled=True)  53.5 us
    psum x1, blocking collectives, per_device(): embedding = lax.psum(partial_embed, 'head')  14.9 us
  transfers between devices with their start and end apart: 3, of which 3 were waited for; matrix products, arithmetic and copies ran while one was open for 3% of the time, Pallas kernels for 0%

commit v1 on v0

v1 whole, which is shorter than its diff:
```python
import math

import jax
import jax.numpy as jnp
from jax import lax
from jax.sharding import PartitionSpec as P

F32 = jnp.float32
BF16 = jnp.bfloat16


def unit_rows(values):
    widened = values.astype(F32)
    return (widened * lax.rsqrt(jnp.sum(widened * widened, -1, keepdims=True) + 1e-06)).astype(BF16)


def split_two(values):
    high = values.astype(BF16)
    return high, (values - high.astype(F32)).astype(BF16)


def split_three(values):
    high = values.astype(BF16)
    rest = values - high.astype(F32)
    middle = rest.astype(BF16)
    return high, middle, (rest - middle.astype(F32)).astype(BF16)


def peers(piece_of):
    parts = [piece_of(0)]
    for step in (1, 2, 3):
        parts.append(lax.ppermute(piece_of(step), "head", [(i, i ^ step) for i in range(4)]))
    return parts


def per_device(tokens, projector, queries, final, captions, multiplier, shift):
    images, tokens_here, width = tokens.shape
    heads, head_size = queries.shape
    n_dp = lax.axis_size("dp")
    share = images // 4
    dp = lax.axis_index("dp")
    head = lax.axis_index("head")

    text_unit = unit_rows(lax.dynamic_slice_in_dim(captions, head * share, share, 0))
    texts = lax.all_to_all(
        jnp.broadcast_to(text_unit[None], (n_dp, share, width)), "dp", 0, 0, tiled=False
    ).reshape(n_dp * share, width)

    key_part = projector[:, 0, :].reshape(width, heads, head_size)
    key_query = jnp.einsum("ihe,he->hi", key_part, queries, preferred_element_type=F32)
    key_query = key_query / math.sqrt(head_size)
    high, low = split_two(key_query)
    packed = jnp.concatenate([high, low], 0)
    gathered = peers(lambda s: packed)
    high = jnp.concatenate([part[:heads] for part in gathered], 0)
    low = jnp.concatenate([part[heads:] for part in gathered], 0)
    both = jnp.concatenate([high, low], 0)
    rows = tokens.reshape(images * tokens_here, width)
    raw = lax.dot_general(rows, both, (((1,), (1,)), ((), ())), preferred_element_type=F32)
    scores = (raw[:, : 4 * heads] + raw[:, 4 * heads :]).reshape(images, tokens_here, 4 * heads)
    top = jnp.max(scores, 1, keepdims=True)
    raised = jnp.exp(scores - top)
    total = jnp.sum(raised, 1, keepdims=True)
    weights = (raised / total).astype(BF16)
    mixed = jnp.einsum("nph,npi->hni", weights, tokens, preferred_element_type=F32).astype(BF16)
    log_total = (top + jnp.log(total))[:, 0, :].T
    pieces = jnp.stack(split_three(log_total), -1)
    message = jnp.concatenate(
        [mixed, jnp.pad(pieces, ((0, 0), (0, 0), (0, 125)))], -1
    ).reshape(4, heads * images, width + 128)
    parts = peers(lambda s: message[s])
    logs = [jnp.sum(part[:, width : width + 3].astype(F32), -1, keepdims=True) for part in parts]
    peak = jnp.maximum(jnp.maximum(logs[0], logs[1]), jnp.maximum(logs[2], logs[3]))
    shares = [jnp.exp(entry - peak) for entry in logs]
    whole = shares[0] + shares[1] + shares[2] + shares[3]
    token_mix = sum(s / whole * part[:, :width].astype(F32) for s, part in zip(shares, parts))
    token_mix = token_mix.astype(BF16).reshape(heads, images, width)
    value_part = projector[:, 1, :].reshape(width, heads, head_size)
    pooled = jnp.einsum("hni,ihe->nhe", token_mix, value_part, preferred_element_type=F32)
    pooled = pooled.astype(BF16).reshape(images, heads * head_size)
    partial = jnp.dot(pooled, final, preferred_element_type=F32)
    embeds = peers(lambda s: partial)
    image_unit = unit_rows((embeds[0] + embeds[1]) + (embeds[2] + embeds[3]))

    similarity = lax.dot_general(
        image_unit, texts, (((1,), (1,)), ((), ())), preferred_element_type=F32
    )
    logits = multiplier * similarity + shift
    image_ids = dp * images + jnp.arange(images, dtype=jnp.int32)
    column = jnp.arange(n_dp * share, dtype=jnp.int32)
    text_ids = column // share * images + head * share + column % share
    matched = (image_ids[:, None] == text_ids[None, :]).astype(F32)
    coefficient = (multiplier * (jax.nn.sigmoid(logits) - matched)).astype(BF16)

    text_part = lax.dot_general(
        coefficient, image_unit, (((0,), (0,)), ((), ())), preferred_element_type=F32
    )
    text_part = text_part.astype(BF16).reshape(n_dp, share, width)
    text_grad = jnp.sum(
        lax.all_to_all(text_part, "dp", 0, 0, tiled=False).astype(F32), 0
    )
    image_part = jnp.dot(coefficient, texts, preferred_element_type=F32)
    grads = peers(
        lambda s: lax.dynamic_slice_in_dim(image_part, (head ^ s) * share, share, 0)
    )
    image_grad = (grads[0] + grads[1]) + (grads[2] + grads[3])
    return image_grad, text_grad


def solution(mesh):
    in_specs = (
        P("dp", "head", None),
        P(None, None, "head"),
        P("head", None),
        P("head", None),
        P("dp", None),
        P(),
        P(),
    )
    out_specs = (P(("dp", "head"), None), P(("dp", "head"), None))
    return jax.shard_map(
        per_device, mesh=mesh, in_specs=in_specs, out_specs=out_specs, check_vma=False
    )
```

time: 641 us -> 90.3 us (0.14)
  waiting for transfers between devices: 584 us -> 18.2 us
  starting transfers between devices: 0.12 us -> 37.9 us
  blocking collectives: 14.9 us -> 0 us
  between operations: 15.1 us -> 2.22 us
  local copies, waits for them, and re-layouts: 10.5 us -> 22.4 us
  matrix products: 15.3 us -> 4.62 us
    all_gather x2 -> x0, waiting for transfers between devices: 300 us -> none  [the longest x1 247 us: per_device(): text_piece = lax.all_gather(caption_unitlength, 'dp', axis=0, tiled=True)]
    unnamed x4 -> x0, waiting for transfers between devices: 284 us -> none
    all_to_all x0 -> x2, starting transfers between devices: none -> 23.7 us  [the longest x1 13 us: per_device(): lax.all_to_all(jnp.broadcast_to(text_unit[None], (n_dp, share, width)), '...]
    psum x1 -> x0, blocking collectives: 14.9 us -> none  [per_device(): embedding = lax.psum(partial_embed, 'head')]
    ppermute x0 -> x12, starting transfers between devices: none -> 14.2 us  [peers(): lax.ppermute(piece_of(step), 'head', [(i, i ^ step) for i in range(4)])]
    slice x1 -> x10, local copies, waits for them, and re-layouts: 1.49 us -> 13.7 us  [the longest x1 7.99 us: per_device(): key_part = projector[:, 0, :].reshape(width, heads, head_size)]
    ppermute x0 -> x12, waiting for transfers between devices: none -> 11.5 us  [peers(): lax.ppermute(piece_of(step), 'head', [(i, i ^ step) for i in range(4)])]
    dot_general x7 -> x8, matrix products: 15.3 us -> 4.62 us  [the longest x1 1.53 us: per_device(): partial = jnp.dot(pooled, final, preferred_element_type=F32)]
  transfers between devices with their start and end apart: 3 -> 14, of which waited for: 3 -> 7; matrix products, arithmetic and copies ran while one was open for 3% -> 17% of each run, Pallas kernels for 0% -> 0%
where the time goes in v1:
time: 90.3 us; the launch traced here: 89.5 us
  starting transfers between devices  37.9 us (42%)
  local copies, waits for them, and re-layouts  22.4 us (25%)
  waiting for transfers between devices  18.2 us (20%)
  matrix products  4.62 us (5%)
  other arithmetic  4.23 us (5%)
  between operations  2.22 us (2%)
    ppermute x12, starting transfers between devices, peers(): lax.ppermute(piece_of(step), 'head', [(i, i ^ step) for i in range(4)])  14.2 us
    all_to_all x1, starting transfers between devices, per_device(): lax.all_to_all(jnp.broadcast_to(text_unit[None], (n_dp, share, width)), '...  13 us
    ppermute x12, waiting for transfers between devices, peers(): lax.ppermute(piece_of(step), 'head', [(i, i ^ step) for i in range(4)])  11.5 us
    all_to_all x1, starting transfers between devices, per_device(): lax.all_to_all(text_part, 'dp', 0, 0, tiled=False).astype(F32)  10.6 us
    slice x1, local copies, waits for them, and re-layouts, per_device(): key_part = projector[:, 0, :].reshape(width, heads, head_size)  7.99 us
    all_to_all x1, waiting for transfers between devices, per_device(): lax.all_to_all(text_part, 'dp', 0, 0, tiled=False).astype(F32)  6.65 us
    unnamed x7, local copies, waits for them, and re-layouts  5.51 us
    slice x1, local copies, waits for them, and re-layouts, per_device(): value_part = projector[:, 1, :].reshape(width, heads, head_size)  5.48 us
  transfers between devices with their start and end apart: 14, of which 7 were waited for; matrix products, arithmetic and copies ran while one was open for 17% of the time, Pallas kernels for 0%

profile of v1, /device:TPU:2, one launch (start us, length us, event | category | flops | bytes accessed | tf_op | source)
XLA Modules:
  0.0 89.5 jit_solution(13681603451434897165)
XLA Ops:
  0.6 8.0 %fusion.40 = (bf16[1536,1,384]{2,1,0:T(2,128)(2,1)}, bf16[1536,1,384]{2,1,0:T(2,128)(2,1)}) fusion(bf16[1536,2,384]{2,1,0:T(2,128)(2,1)} %param.8), kind=kLoop, calls=%fused_computation.89 | loop fusion | bytes 4718592 | tf_op jit(solution)/shard_map/slice | solution.py:49
  8.6 5.5 %copy.61 = bf16[1536,1,384]{0,2,1:T(8,128)(2,1)S(1)} copy(bf16[1536,1,384]{2,1,0:T(2,128)(2,1)} %get-tuple-element.7) | data formatting | bytes 2359296
  14.5 2.7 %collective-permute-start.2 = (bf16[8,1536]{1,0:T(8,128)(2,1)S(1)}, bf16[8,1536]{1,0:T(8,128)(2,1)S(1)}, u32[]{:S(2)}, u32[]{:S(2)}) collective-permute-start(bf16[8,1536]{1,0:T(8,128)(2,1)S(1)} %pad_maximum_fusion), channel_id=1, source_target_pairs={{0,3},{1,2},{2,1},{3,0},{4,7},{5,6},{6,5},{7,4},{8,11},{9,10},{10,... | collective-permute-start | bytes 73736 | tf_op jit(solution)/shard_map/ppermute | solution.py:32
  18.1 1.0 %broadcast_in_dim.2 = bf16[64,2,1536]{2,1,0:T(2,128)(2,1)} broadcast(bf16[2,1536]{1,0:T(2,128)(2,1)S(1)} %fusion.26), dimensions={1,2} | broadcast | bytes 399360 | tf_op jit(solution)/shard_map/broadcast_in_dim | solution.py:46
  19.1 13.0 %all-to-all-start = ((bf16[64,2,1536]{2,1,0:T(2,128)(2,1)}), bf16[64,2,1536]{2,1,0:T(2,128)(2,1)S(1)}, u32[]{:S(2)}, u32[]{:S(2)}) async-start(bf16[64,2,1536]{2,1,0:T(2,128)(2,1)} %broadcast_in_dim.2), calls=%async_computation | async-start | bytes 786432 | tf_op jit(solution)/shard_map/all_to_all | solution.py:45
  32.2 5.5 %copy.57 = bf16[1536,1,384]{0,2,1:T(8,128)(2,1)S(1)} copy(bf16[1536,1,384]{2,1,0:T(2,128)(2,1)} %get-tuple-element.8) | data formatting | bytes 2359296 | tf_op jit(solution)/shard_map/slice | solution.py:78
  39.7 1.1 %fusion = bf16[16,8,1536]{2,0,1:T(8,128)(2,1)S(1)} fusion(bf16[8,64,1536]{2,1,0:T(8,128)(2,1)S(1)} %copy-done, bf16[8,64,16]{1,0,2:T(8,128)(2,1)} %divide_convert_fusion), kind=kOutput, calls=%fused_computation.2 | convolution fusion | flops 25362432 | bytes 1982464 | tf_op jit(solution)/shard_map/nph,npi->hni/dot_general | solution.py:65
  42.5 2.1 %collective-permute-start.5 = (bf16[32,1664]{1,0:T(8,128)(2,1)S(1)}, bf16[32,1664]{1,0:T(8,128)(2,1)S(1)}, u32[]{:S(2)}, u32[]{:S(2)}) collective-permute-start(bf16[32,1664]{1,0:T(8,128)(2,1)S(1)} %bitcast.76), channel_id=1, source_target_pairs={{0,3},{1,2},{2,1},{3,0},{4,7},{5,6},{6,5},{7,4},{8,11},{9,10},{10,... | collective-permute-start | bytes 319496 | tf_op jit(solution)/shard_map/ppermute | solution.py:32
  44.6 0.9 %collective-permute-start.4 = (bf16[32,1664]{1,0:T(8,128)(2,1)S(1)}, bf16[32,1664]{1,0:T(8,128)(2,1)S(1)}, u32[]{:S(2)}, u32[]{:S(2)}) collective-permute-start(bf16[32,1664]{1,0:T(8,128)(2,1)S(1)} %bitcast.77), channel_id=1, source_target_pairs={{0,2},{1,3},{2,0},{3,1},{4,6},{5,7},{6,4},{7,5},{8,10},{9,11},{10,... | collective-permute-start | bytes 319496 | tf_op jit(solution)/shard_map/ppermute | solution.py:32
  46.3 3.2 %collective-permute-done.5 = bf16[32,1664]{1,0:T(8,128)(2,1)S(1)} collective-permute-done((bf16[32,1664]{1,0:T(8,128)(2,1)S(1)}, bf16[32,1664]{1,0:T(8,128)(2,1)S(1)}, u32[]{:S(2)}, u32[]{:S(2)}) %collective-permute-start.5) | collective-permute-done | bytes 106528 | tf_op jit(solution)/shard_map/ppermute | solution.py:32
  49.5 2.5 %collective-permute-done.4 = bf16[32,1664]{1,0:T(8,128)(2,1)S(1)} collective-permute-done((bf16[32,1664]{1,0:T(8,128)(2,1)S(1)}, bf16[32,1664]{1,0:T(8,128)(2,1)S(1)}, u32[]{:S(2)}, u32[]{:S(2)}) %collective-permute-start.4) | collective-permute-done | bytes 106528 | tf_op jit(solution)/shard_map/ppermute | solution.py:32
  52.9 1.5 %fusion.45 = f32[8,1536]{1,0:T(8,128)S(1)} fusion(bf16[8,384]{1,0:T(8,128)(2,1)S(1)} %reshape.148, bf16[384,1536]{1,0:T(8,128)(2,1)} %param.10), kind=kOutput, calls=%fused_computation.94 | convolution fusion | flops 9437184 | bytes 1234944 | tf_op jit(solution)/shard_map/dot_general | solution.py:81
  54.5 2.0 %collective-permute-start.7 = (f32[8,1536]{1,0:T(8,128)S(1)}, f32[8,1536]{1,0:T(8,128)S(1)}, u32[]{:S(2)}, u32[]{:S(2)}) collective-permute-start(f32[8,1536]{1,0:T(8,128)S(1)} %fusion.45), channel_id=1, source_target_pairs={{0,2},{1,3},{2,0},{3,1},{4,6},{5,7},{6,4},{7,5},{8,10},{9,11},{10,... | collective-permute-start | bytes 147464 | tf_op jit(solution)/shard_map/ppermute | solution.py:32
  56.5 1.3 %collective-permute-start.8 = (f32[8,1536]{1,0:T(8,128)S(1)}, f32[8,1536]{1,0:T(8,128)S(1)}, u32[]{:S(2)}, u32[]{:S(2)}) collective-permute-start(f32[8,1536]{1,0:T(8,128)S(1)} %fusion.45), channel_id=1, source_target_pairs={{0,3},{1,2},{2,1},{3,0},{4,7},{5,6},{6,5},{7,4},{8,11},{9,10},{10,... | collective-permute-start | bytes 147464 | tf_op jit(solution)/shard_map/ppermute | solution.py:32
  59.2 1.0 %collective-permute-done.7 = f32[8,1536]{1,0:T(8,128)S(1)} collective-permute-done((f32[8,1536]{1,0:T(8,128)S(1)}, f32[8,1536]{1,0:T(8,128)S(1)}, u32[]{:S(2)}, u32[]{:S(2)}) %collective-permute-start.7) | collective-permute-done | bytes 49184 | tf_op jit(solution)/shard_map/ppermute | solution.py:32
  60.1 1.7 %collective-permute-done.8 = f32[8,1536]{1,0:T(8,128)S(1)} collective-permute-done((f32[8,1536]{1,0:T(8,128)S(1)}, f32[8,1536]{1,0:T(8,128)S(1)}, u32[]{:S(2)}, u32[]{:S(2)}) %collective-permute-start.8) | collective-permute-done | bytes 49184 | tf_op jit(solution)/shard_map/ppermute | solution.py:32
  62.7 0.9 %reshape.150 = bf16[64,2,1536]{2,1,0:T(2,128)(2,1)} reshape(bf16[128,1536]{1,0:T(8,128)(2,1)S(1)} %convolution_convert_fusion) | data formatting | bytes 786432 | tf_op jit(solution)/shard_map/reshape | solution.py:98
  63.6 10.6 %all-to-all-start.1 = ((bf16[64,2,1536]{2,1,0:T(2,128)(2,1)}), bf16[64,2,1536]{2,1,0:T(2,128)(2,1)S(1)}, u32[]{:S(2)}, u32[]{:S(2)}) async-start(bf16[64,2,1536]{2,1,0:T(2,128)(2,1)} %reshape.150), calls=%async_computation.1 | async-start | bytes 786432 | tf_op jit(solution)/shard_map/all_to_all | solution.py:100
  74.4 2.2 %collective-permute-start.10 = (f32[2,1536]{1,0:T(2,128)S(1)}, f32[2,1536]{1,0:T(2,128)S(1)}, u32[]{:S(2)}, u32[]{:S(2)}) collective-permute-start(f32[2,1536]{1,0:T(2,128)S(1)} %get-tuple-element.15), channel_id=1, source_target_pairs={{0,2},{1,3},{2,0},{3,1},{4,6},{5,7},{6,4},{7,5},{8,10},{9,11},{10,... | collective-permute-start | bytes 36872 | tf_op jit(solution)/shard_map/ppermute | solution.py:32
  76.9 1.2 %collective-permute-start.9 = (f32[2,1536]{1,0:T(2,128)S(1)}, f32[2,1536]{1,0:T(2,128)S(1)}, u32[]{:S(2)}, u32[]{:S(2)}) collective-permute-start(f32[2,1536]{1,0:T(2,128)S(1)} %get-tuple-element.13), channel_id=1, source_target_pairs={{0,1},{1,0},{2,3},{3,2},{4,5},{5,4},{6,7},{7,6},{8,9},{9,8},{10,11... | collective-permute-start | bytes 36872 | tf_op jit(solution)/shard_map/ppermute | solution.py:32
  78.2 1.7 %collective-permute-done.10 = f32[2,1536]{1,0:T(2,128)S(1)} collective-permute-done((f32[2,1536]{1,0:T(2,128)S(1)}, f32[2,1536]{1,0:T(2,128)S(1)}, u32[]{:S(2)}, u32[]{:S(2)}) %collective-permute-start.10) | collective-permute-done | bytes 12320 | tf_op jit(solution)/shard_map/ppermute | solution.py:32
  79.8 1.5 %collective-permute-done.11 = f32[2,1536]{1,0:T(2,128)S(1)} collective-permute-done((f32[2,1536]{1,0:T(2,128)S(1)}, f32[2,1536]{1,0:T(2,128)S(1)}, u32[]{:S(2)}, u32[]{:S(2)}) %collective-permute-start.11) | collective-permute-done | bytes 12320 | tf_op jit(solution)/shard_map/ppermute | solution.py:32
  81.9 6.7 %all-to-all-done.1 = bf16[64,2,1536]{2,1,0:T(2,128)(2,1)S(1)} async-done(((bf16[64,2,1536]{2,1,0:T(2,128)(2,1)}), bf16[64,2,1536]{2,1,0:T(2,128)(2,1)S(1)}, u32[]{:S(2)}, u32[]{:S(2)}) %all-to-all-start.1) | async-done | bytes 393248 | tf_op jit(solution)/shard_map/all_to_all | solution.py:100
  88.6 0.9 %convert_reduce_fusion = f32[2,1536]{1,0:T(2,128)} fusion(bf16[64,2,1536]{2,1,0:T(2,128)(2,1)S(1)} %all-to-all-done.1), kind=kLoop, calls=%fused_computation.17 | loop fusion | flops 390144 | bytes 405504 | tf_op jit(solution)/shard_map/reduce_sum | solution.py:99
  (65 shorter events, 8.6 us)
Async XLA Ops:
  0.6 37.2 %copy-start = (bf16[8,64,1536]{2,1,0:T(8,128)(2,1)S(1)}, bf16[8,64,1536]{2,1,0:T(8,128)(2,1)}, u32[]{:S(2)}) copy-start(bf16[8,64,1536]{2,1,0:T(8,128)(2,1)} %param.7) | copy-start | bytes 4718596
  8.6 5.5 %copy-start.2 = (bf16[4,96]{1,0:T(4,128)(2,1)S(1)}, bf16[4,96]{1,0:T(4,128)(2,1)}, u32[]{:S(2)}) copy-start(bf16[4,96]{1,0:T(4,128)(2,1)} %param.9) | copy-start | bytes 2308
  8.6 9.3 %copy-start.1 = (bf16[8,1536]{1,0:T(8,128)(2,1)S(1)}, bf16[8,1536]{1,0:T(8,128)(2,1)}, u32[]{:S(2)}) copy-start(bf16[8,1536]{1,0:T(8,128)(2,1)} %param.11) | copy-start | bytes 73732
  14.5 23.2 %collective-permute-start.2 = (bf16[8,1536]{1,0:T(8,128)(2,1)S(1)}, bf16[8,1536]{1,0:T(8,128)(2,1)S(1)}, u32[]{:S(2)}, u32[]{:S(2)}) collective-permute-start(bf16[8,1536]{1,0:T(8,128)(2,1)S(1)} %pad_maximum_fusion), channel_id=1, source_target_pairs={{0,3},{1,2},{2,1},{3,0},{4,7},{5,6},{6,5},{7,4},{8,11},{9,10},{10,... | collective-permute-start | bytes 73736 | tf_op jit(solution)/shard_map/ppermute | solution.py:32
  17.2 20.5 %collective-permute-start.1 = (bf16[8,1536]{1,0:T(8,128)(2,1)S(1)}, bf16[8,1536]{1,0:T(8,128)(2,1)S(1)}, u32[]{:S(2)}, u32[]{:S(2)}) collective-permute-start(bf16[8,1536]{1,0:T(8,128)(2,1)S(1)} %pad_maximum_fusion), channel_id=1, source_target_pairs={{0,2},{1,3},{2,0},{3,1},{4,6},{5,7},{6,4},{7,5},{8,10},{9,11},{10,... | collective-permute-start | bytes 73736 | tf_op jit(solution)/shard_map/ppermute | solution.py:32
  17.8 19.9 %collective-permute-start = (bf16[8,1536]{1,0:T(8,128)(2,1)S(1)}, bf16[8,1536]{1,0:T(8,128)(2,1)S(1)}, u32[]{:S(2)}, u32[]{:S(2)}) collective-permute-start(bf16[8,1536]{1,0:T(8,128)(2,1)S(1)} %pad_maximum_fusion), channel_id=1, source_target_pairs={{0,1},{1,0},{2,3},{3,2},{4,5},{5,4},{6,7},{7,6},{8,9},{9,8},{10,11... | collective-permute-start | bytes 73736 | tf_op jit(solution)/shard_map/ppermute | solution.py:32
  19.1 42.8 %all-to-all-start = ((bf16[64,2,1536]{2,1,0:T(2,128)(2,1)}), bf16[64,2,1536]{2,1,0:T(2,128)(2,1)S(1)}, u32[]{:S(2)}, u32[]{:S(2)}) async-start(bf16[64,2,1536]{2,1,0:T(2,128)(2,1)} %broadcast_in_dim.2), calls=%async_computation | async-start | bytes 786432 | tf_op jit(solution)/shard_map/all_to_all | solution.py:45
  42.5 7.0 %collective-permute-start.5 = (bf16[32,1664]{1,0:T(8,128)(2,1)S(1)}, bf16[32,1664]{1,0:T(8,128)(2,1)S(1)}, u32[]{:S(2)}, u32[]{:S(2)}) collective-permute-start(bf16[32,1664]{1,0:T(8,128)(2,1)S(1)} %bitcast.76), channel_id=1, source_target_pairs={{0,3},{1,2},{2,1},{3,0},{4,7},{5,6},{6,5},{7,4},{8,11},{9,10},{10,... | collective-permute-start | bytes 319496 | tf_op jit(solution)/shard_map/ppermute | solution.py:32
  44.6 7.4 %collective-permute-start.4 = (bf16[32,1664]{1,0:T(8,128)(2,1)S(1)}, bf16[32,1664]{1,0:T(8,128)(2,1)S(1)}, u32[]{:S(2)}, u32[]{:S(2)}) collective-permute-start(bf16[32,1664]{1,0:T(8,128)(2,1)S(1)} %bitcast.77), channel_id=1, source_target_pairs={{0,2},{1,3},{2,0},{3,1},{4,6},{5,7},{6,4},{7,5},{8,10},{9,11},{10,... | collective-permute-start | bytes 319496 | tf_op jit(solution)/shard_map/ppermute | solution.py:32
  45.6 6.6 %collective-permute-start.3 = (bf16[32,1664]{1,0:T(8,128)(2,1)S(1)}, bf16[32,1664]{1,0:T(8,128)(2,1)S(1)}, u32[]{:S(2)}, u32[]{:S(2)}) collective-permute-start(bf16[32,1664]{1,0:T(8,128)(2,1)S(1)} %bitcast.78), channel_id=1, source_target_pairs={{0,1},{1,0},{2,3},{3,2},{4,5},{5,4},{6,7},{7,6},{8,9},{9,8},{10,11... | collective-permute-start | bytes 319496 | tf_op jit(solution)/shard_map/ppermute | solution.py:32
  54.4 4.7 %collective-permute-start.6 = (f32[8,1536]{1,0:T(8,128)S(1)}, f32[8,1536]{1,0:T(8,128)S(1)}, u32[]{:S(2)}, u32[]{:S(2)}) collective-permute-start(f32[8,1536]{1,0:T(8,128)S(1)} %fusion.45), channel_id=1, source_target_pairs={{0,1},{1,0},{2,3},{3,2},{4,5},{5,4},{6,7},{7,6},{8,9},{9,8},{10,11... | collective-permute-start | bytes 147464 | tf_op jit(solution)/shard_map/ppermute | solution.py:32
  54.5 5.6 %collective-permute-start.7 = (f32[8,1536]{1,0:T(8,128)S(1)}, f32[8,1536]{1,0:T(8,128)S(1)}, u32[]{:S(2)}, u32[]{:S(2)}) collective-permute-start(f32[8,1536]{1,0:T(8,128)S(1)} %fusion.45), channel_id=1, source_target_pairs={{0,2},{1,3},{2,0},{3,1},{4,6},{5,7},{6,4},{7,5},{8,10},{9,11},{10,... | collective-permute-start | bytes 147464 | tf_op jit(solution)/shard_map/ppermute | solution.py:32
  56.5 5.3 %collective-permute-start.8 = (f32[8,1536]{1,0:T(8,128)S(1)}, f32[8,1536]{1,0:T(8,128)S(1)}, u32[]{:S(2)}, u32[]{:S(2)}) collective-permute-start(f32[8,1536]{1,0:T(8,128)S(1)} %fusion.45), channel_id=1, source_target_pairs={{0,3},{1,2},{2,1},{3,0},{4,7},{5,6},{6,5},{7,4},{8,11},{9,10},{10,... | collective-permute-start | bytes 147464 | tf_op jit(solution)/shard_map/ppermute | solution.py:32
  63.6 25.0 %all-to-all-start.1 = ((bf16[64,2,1536]{2,1,0:T(2,128)(2,1)}), bf16[64,2,1536]{2,1,0:T(2,128)(2,1)S(1)}, u32[]{:S(2)}, u32[]{:S(2)}) async-start(bf16[64,2,1536]{2,1,0:T(2,128)(2,1)} %reshape.150), calls=%async_computation.1 | async-start | bytes 786432 | tf_op jit(solution)/shard_map/all_to_all | solution.py:100
  74.4 5.4 %collective-permute-start.10 = (f32[2,1536]{1,0:T(2,128)S(1)}, f32[2,1536]{1,0:T(2,128)S(1)}, u32[]{:S(2)}, u32[]{:S(2)}) collective-permute-start(f32[2,1536]{1,0:T(2,128)S(1)} %get-tuple-element.15), channel_id=1, source_target_pairs={{0,2},{1,3},{2,0},{3,1},{4,6},{5,7},{6,4},{7,5},{8,10},{9,11},{10,... | collective-permute-start | bytes 36872 | tf_op jit(solution)/shard_map/ppermute | solution.py:32
  76.6 4.7 %collective-permute-start.11 = (f32[2,1536]{1,0:T(2,128)S(1)}, f32[2,1536]{1,0:T(2,128)S(1)}, u32[]{:S(2)}, u32[]{:S(2)}) collective-permute-start(f32[2,1536]{1,0:T(2,128)S(1)} %get-tuple-element.14), channel_id=1, source_target_pairs={{0,3},{1,2},{2,1},{3,0},{4,7},{5,6},{6,5},{7,4},{8,11},{9,10},{10,... | collective-permute-start | bytes 36872 | tf_op jit(solution)/shard_map/ppermute | solution.py:32
  76.9 4.4 %collective-permute-start.9 = (f32[2,1536]{1,0:T(2,128)S(1)}, f32[2,1536]{1,0:T(2,128)S(1)}, u32[]{:S(2)}, u32[]{:S(2)}) collective-permute-start(f32[2,1536]{1,0:T(2,128)S(1)} %get-tuple-element.13), channel_id=1, source_target_pairs={{0,1},{1,0},{2,3},{3,2},{4,5},{5,4},{6,7},{7,6},{8,9},{9,8},{10,11... | collective-permute-start | bytes 36872 | tf_op jit(solution)/shard_map/ppermute | solution.py:32

commit v2 on v1

v2 whole, which is shorter than its diff:
```python
import math

import jax
import jax.numpy as jnp
from jax import lax
from jax.experimental import pallas as pl
from jax.experimental.pallas import tpu as pltpu
from jax.sharding import PartitionSpec as P

F32 = jnp.float32
BF16 = jnp.bfloat16
NT = (((1,), (1,)), ((), ()))
TN = (((0,), (0,)), ((), ()))
VMEM = pl.BlockSpec(memory_space=pltpu.VMEM)
ANY = pl.BlockSpec(memory_space=pl.ANY)
SMEM = pl.BlockSpec(memory_space=pltpu.SMEM)


def call(kernel, outs, specs, flops, moved):
    return pl.pallas_call(
        kernel,
        grid=(1,),
        out_shape=outs,
        in_specs=specs,
        out_specs=jax.tree.map(lambda _: VMEM, outs),
        compiler_params=pltpu.CompilerParams(vmem_limit_bytes=10 << 20),
        cost_estimate=pl.CostEstimate(flops=flops, bytes_accessed=moved, transcendentals=0),
    )


def unit_rows(values):
    widened = values.astype(F32)
    return (widened * lax.rsqrt(jnp.sum(widened * widened, -1, keepdims=True) + 1e-06)).astype(BF16)


def peers(pieces):
    return [pieces[0]] + [
        lax.ppermute(pieces[s], "head", [(i, i ^ s) for i in range(4)]) for s in (1, 2, 3)
    ]


def key_query_kernel(spread_ref, key_ref, out_ref, *, scale):
    out_ref[...] = (
        lax.dot_general(spread_ref[...], key_ref[...], NT, preferred_element_type=F32) * scale
    )


def mix_kernel(tokens_ref, q0, q1, q2, q3, m0, m1, m2, m3, *, images):
    count, here, width = tokens_ref.shape
    rows = tokens_ref[...].reshape(count * here, width)
    heads = q0.shape[0]
    spread = jnp.concatenate(
        [
            jnp.broadcast_to(ref[h : h + 1, :], (images, width))
            for ref in (q0, q1, q2, q3)
            for h in range(heads)
        ],
        0,
    )
    columns = spread.shape[0]
    high = spread.astype(BF16)
    low = (spread - high.astype(F32)).astype(BF16)
    raw = lax.dot_general(rows, jnp.concatenate([high, low], 0), NT, preferred_element_type=F32)
    scores = raw[:, :columns] + raw[:, columns:]
    row_image = lax.broadcasted_iota(jnp.int32, scores.shape, 0) // here
    column_image = lax.broadcasted_iota(jnp.int32, scores.shape, 1) % images
    mine = row_image == column_image
    top = jnp.max(jnp.where(mine, scores, -jnp.inf), 0, keepdims=True)
    raised = jnp.exp(jnp.where(mine, scores - top, -jnp.inf))
    total = jnp.sum(raised, 0, keepdims=True)
    weights = (raised / total).astype(BF16)
    mixed = lax.dot_general(weights, rows, TN, preferred_element_type=F32).astype(BF16)
    log_total = jnp.broadcast_to(top + jnp.log(total), (columns, columns))
    down = lax.broadcasted_iota(jnp.int32, (columns, columns), 0)
    across = lax.broadcasted_iota(jnp.int32, (columns, columns), 1)
    upright = jnp.sum(jnp.where(down == across, log_total, 0.0), 1, keepdims=True)
    high = upright.astype(BF16).astype(F32)
    middle = (upright - high).astype(BF16).astype(F32)
    low = upright - high - middle
    lane = lax.broadcasted_iota(jnp.int32, (columns, 128), 1)
    pieces = jnp.where(lane == 0, high, jnp.where(lane == 1, middle, jnp.where(lane == 2, low, 0.0)))
    pieces = pieces.astype(BF16)
    step = columns // 4
    for s, ref in enumerate((m0, m1, m2, m3)):
        ref[:, :width] = mixed[s * step : (s + 1) * step]
        ref[:, width:] = pieces[s * step : (s + 1) * step]


def embed_kernel(m0, m1, m2, m3, value_ref, final_ref, out_ref, *, heads):
    width = value_ref.shape[0]
    parts = (m0, m1, m2, m3)
    logs = [jnp.sum(ref[:, width:].astype(F32), -1, keepdims=True) for ref in parts]
    peak = jnp.maximum(jnp.maximum(logs[0], logs[1]), jnp.maximum(logs[2], logs[3]))
    shares = [jnp.exp(entry - peak) for entry in logs]
    whole = (shares[0] + shares[1]) + (shares[2] + shares[3])
    mixed = sum((s / whole) * ref[:, :width].astype(F32) for s, ref in zip(shares, parts))
    pooled = jnp.dot(mixed.astype(BF16), value_ref[...], preferred_element_type=F32)
    rows, columns = pooled.shape
    images = rows // heads
    row_head = lax.broadcasted_iota(jnp.int32, pooled.shape, 0) // images
    column_head = lax.broadcasted_iota(jnp.int32, pooled.shape, 1) // (columns // heads)
    kept = jnp.where(row_head == column_head, pooled, 0.0)
    pooled = sum(kept[h * images : (h + 1) * images] for h in range(heads))
    out_ref[...] = jnp.dot(pooled.astype(BF16), final_ref[...], preferred_element_type=F32)


def text_kernel(place_ref, captions_ref, order_ref, out_ref):
    core = place_ref[1] % 2
    unit = unit_rows(captions_ref[...]).astype(F32)
    first = jnp.concatenate([unit[0:2], unit[4:6]], 0)
    second = jnp.concatenate([unit[2:4], unit[6:8]], 0)
    chosen = jnp.where(core == 0, first, second).astype(BF16)
    out_ref[...] = jnp.broadcast_to(chosen[None], out_ref.shape)


def text_ids(shape, first_dp, images, head):
    column = lax.broadcasted_iota(jnp.int32, shape, 1)
    return (first_dp + column // 4) * images + column % 4 // 2 * 4 + head % 2 * 2 + column % 2


def unit_kernel(e0, e1, e2, e3, order1, order2, order3, unit_ref):
    embed = (e0[...] + e1[...]) + (e2[...] + e3[...])
    unit_ref[...] = unit_rows(embed)


def text_grad_kernel(place_ref, scalar_ref, u0, u1, u2, u3, text_ref, order_ref, part_ref, *, near):
    dp, head = place_ref[0], place_ref[1]
    multiplier, shift = scalar_ref[0], scalar_ref[1]
    images, width = u0.shape
    chunk = width // 4
    block = dp // near
    units = jnp.concatenate([ref[...].astype(F32) for ref in (u0, u1, u2, u3)], 0)
    logits = lax.dot_general(units.astype(BF16), text_ref[...], NT, preferred_element_type=F32)
    logits = logits * multiplier + shift
    row = lax.broadcasted_iota(jnp.int32, logits.shape, 0)
    image_id = ((block ^ (row // images)) * near + dp % near) * images + row % images
    text_id = text_ids(logits.shape, block * near, images, head)
    matched = jnp.where(image_id == text_id, 1.0, 0.0)
    coefficient = (multiplier * (jax.nn.sigmoid(logits) - matched)).astype(BF16)
    source = lax.broadcasted_iota(jnp.int32, (near * 4, near * 8), 0)
    target = lax.broadcasted_iota(jnp.int32, (near * 4, near * 8), 1)
    repeat = jnp.where(source == target // 8 * 4 + head // 2 * 2 + target % 8 // 4, 1.0, 0.0)
    wide = jnp.dot(coefficient, repeat.astype(BF16), preferred_element_type=F32)
    wide = jnp.concatenate([wide] * 4, 0)
    row_chunk = lax.broadcasted_iota(jnp.int32, wide.shape, 0) // (4 * images)
    column_chunk = lax.broadcasted_iota(jnp.int32, wide.shape, 1) % 4
    wide = jnp.where(row_chunk == column_chunk, wide, 0.0).astype(BF16)
    stacked = jnp.concatenate([units[:, c * chunk : (c + 1) * chunk] for c in range(4)], 0)
    part = lax.dot_general(wide, stacked.astype(BF16), TN, preferred_element_type=F32)
    part_ref[...] = part.reshape(part_ref.shape).astype(part_ref.dtype)


def image_grad_kernel(
    place_ref, scalar_ref, unit_ref, t0, t1, t2, t3, own_ref, other_ref, *, near
):
    dp, head = place_ref[0], place_ref[1]
    multiplier, shift = scalar_ref[0], scalar_ref[1]
    images, width = unit_ref.shape
    share = images // 4
    block = dp // near
    grads = jnp.zeros((images, width), F32)
    for s, ref in enumerate((t0, t1, t2, t3)):
        texts = ref[...]
        logits = lax.dot_general(unit_ref[...], texts, NT, preferred_element_type=F32)
        logits = logits * multiplier + shift
        image_id = dp * images + lax.broadcasted_iota(jnp.int32, logits.shape, 0)
        text_id = text_ids(logits.shape, (block ^ s) * near, images, head)
        matched = jnp.where(image_id == text_id, 1.0, 0.0)
        coefficient = (multiplier * (jax.nn.sigmoid(logits) - matched)).astype(BF16)
        grads = grads + jnp.dot(coefficient, texts, preferred_element_type=F32)
    for wanted, ref in ((head, own_ref), (head ^ 1, other_ref)):
        ref[...] = sum(
            jnp.where(wanted == k, grads[k * share : (k + 1) * share], 0.0) for k in range(4)
        )


def sum_kernel(part_ref, out_ref):
    share, width = out_ref.shape
    chunk = part_ref.shape[2]
    total = jnp.sum(part_ref[...].astype(F32), 0)
    for r in range(share):
        for c in range(4):
            out_ref[r : r + 1, c * chunk : (c + 1) * chunk] = total[r * 4 + c : r * 4 + c + 1]


def per_device(tokens, projector, queries, final, captions, multiplier, shift):
    images, here, width = tokens.shape
    heads, head_size = queries.shape
    n_dp = lax.axis_size("dp")
    near = n_dp // 4
    share = images // 4
    dp = lax.axis_index("dp")
    head = lax.axis_index("head")
    columns = heads * head_size

    both = projector.reshape(width, 2 * columns)
    own = (jnp.arange(columns) // head_size)[None, :] == jnp.arange(heads)[:, None]
    spread = jnp.where(own, jnp.tile(queries, (1, heads)), 0).astype(BF16)
    key_spec = pl.BlockSpec((width, columns), lambda i: (0, 0), memory_space=pltpu.VMEM)
    value_spec = pl.BlockSpec((width, columns), lambda i: (0, 1), memory_space=pltpu.VMEM)

    def f32(*shape):
        return jax.ShapeDtypeStruct(shape, F32)

    def bf16(*shape):
        return jax.ShapeDtypeStruct(shape, BF16)

    key_query = call(
        lambda *refs: key_query_kernel(*refs, scale=1.0 / math.sqrt(head_size)),
        f32(heads, width),
        [VMEM, key_spec],
        2 * heads * width * columns,
        2 * width * columns,
    )(spread, both)
    queried = peers([key_query] * 4)

    place = jnp.stack([dp, head]).astype(jnp.int32)
    groups = [[b * near + i for i in range(near)] for b in range(4)]

    def swap(pieces):
        return lax.all_to_all(pieces, "dp", 0, 0, axis_index_groups=groups, tiled=False)

    def across(pieces):
        return [pieces[0]] + [
            lax.ppermute(pieces[s], "dp", [(i, i ^ (s * near)) for i in range(n_dp)])
            for s in (1, 2, 3)
        ]

    text_copies = call(
        text_kernel, bf16(near, 4, width), [SMEM, VMEM, ANY], 6 << 30, 8 * n_dp * width
    )(place, captions, key_query)
    texts = swap(text_copies).reshape(near * 4, width)
    all_texts = across([texts] * 4)

    message = [bf16(heads * images, width + 128)] * 4
    mixes = call(
        lambda *refs: mix_kernel(*refs, images=images),
        message,
        [VMEM] * 5,
        64 << 30,
        3 * images * here * width,
    )(tokens, *queried)
    mixes = peers(mixes)

    embeds = call(
        lambda *refs: embed_kernel(*refs, heads=heads),
        f32(images, width),
        [VMEM] * 4 + [value_spec, VMEM],
        64 << 30,
        4 * width * columns,
    )(*mixes, both, final)
    embeds = peers([embeds] * 4)

    scalars = jnp.stack([multiplier, shift])
    unit = call(
        unit_kernel,
        bf16(images, width),
        [VMEM] * 4 + [ANY] * 3,
        8 * images * width,
        18 * images * width,
    )(*embeds, *all_texts[1:])
    units = across([unit] * 4)
    own_part, other_part = call(
        lambda *refs: image_grad_kernel(*refs, near=near),
        [f32(share, width)] * 2,
        [SMEM, SMEM] + [VMEM] * 5,
        2 * 64 * n_dp * width,
        16 * n_dp * width,
    )(place, scalars, unit, *all_texts)
    image_grad = own_part + lax.ppermute(other_part, "head", [(i, i ^ 1) for i in range(4)])
    text_part = call(
        lambda *refs: text_grad_kernel(*refs, near=near),
        bf16(near, 4 * share, width // 4),
        [SMEM, SMEM] + [VMEM] * 5 + [ANY],
        2 * 256 * near * width,
        8 * near * width,
    )(place, scalars, *units, texts, own_part)
    received = swap(text_part)
    text_grad = call(
        sum_kernel, f32(share, width), [VMEM], near * share * width, 2 * near * share * width
    )(received)
    return image_grad, text_grad


def solution(mesh):
    in_specs = (
        P("dp", "head", None),
        P(None, None, "head"),
        P("head", None),
        P("head", None),
        P("dp", None),
        P(),
        P(),
    )
    out_specs = (P(("dp", "head"), None), P(("dp", "head"), None))
    return jax.shard_map(
        per_device, mesh=mesh, in_specs=in_specs, out_specs=out_specs, check_vma=False
    )
```

time: 90.3 us -> 70.4 us (0.78)
  the two profiles are of different devices: /device:TPU:2 before, /device:TPU:8 now
where the time goes in v2:
time: 70.4 us; the launch traced here: 70 us
  starting transfers between devices  35.9 us (51%)
  waiting for transfers between devices  16.7 us (24%)
  Pallas kernels  8.77 us (12%)
  local copies, waits for them, and re-layouts  5.86 us (8%)
  between operations  2.11 us (3%)
  other arithmetic  0.77 us (1%)
    all_to_all x2, starting transfers between devices, swap(): lax.all_to_all(pieces, 'dp', 0, 0, axis_index_groups=groups, tiled=False)  16.6 us
    ppermute x9, starting transfers between devices, peers(): lax.ppermute(pieces[s], 'head', [(i, i ^ s) for i in range(4)])  10.2 us
    all_to_all x2, waiting for transfers between devices, swap(): lax.all_to_all(pieces, 'dp', 0, 0, axis_index_groups=groups, tiled=False)  10.2 us
    ppermute x6, starting transfers between devices, across(): lax.ppermute(pieces[s], 'dp', [(i, i ^ s * near) for i in range(n_dp)])  9.05 us
    unnamed x13, local copies, waits for them, and re-layouts  5.72 us
    ppermute x9, waiting for transfers between devices, peers(): lax.ppermute(pieces[s], 'head', [(i, i ^ s) for i in range(4)])  2.91 us
    ppermute x6, waiting for transfers between devices, across(): lax.ppermute(pieces[s], 'dp', [(i, i ^ s * near) for i in range(n_dp)])  2.36 us
    pallas_call x1, Pallas kernels, per_device(): call(lambda *refs: text_grad_kernel(*refs, near=near), bf16(near, 4 * sha...  1.74 us
  transfers between devices with their start and end apart: 18, of which 7 were waited for; matrix products, arithmetic and copies ran while one was open for 1% of the time, Pallas kernels for 8%

profile of v2, /device:TPU:8, one launch (start us, length us, event | category | flops | bytes accessed | tf_op | source)
XLA Modules:
  0.0 70.0 jit_solution(17369867734330381156)
XLA Ops:
  0.7 2.1 %copy.9 = bf16[192,8,2,384]{3,1,2,0:T(8,128)(2,1)S(1)} copy(bf16[192,8,2,384]{3,2,1,0:T(2,128)(2,1)} %bitcast.10) | data formatting | bytes 4718592
  3.4 2.4 %collective-permute-start.1 = (f32[4,1536]{1,0:T(4,128)S(1)}, f32[4,1536]{1,0:T(4,128)S(1)}, u32[]{:S(2)}, u32[]{:S(2)}) collective-permute-start(f32[4,1536]{1,0:T(4,128)S(1)} %shard_map.86.refs_1_.order_ref), channel_id=1, source_target_pairs={{0,2},{1,3},{2,0},{3,1},{4,6},{5,7},{6,4},{7,5},{8,10},{9,11},{10,... | collective-permute-start | bytes 73736 | tf_op jit(solution)/shard_map/ppermute | solution.py:38
  6.8 1.3 %shard_map.89 = bf16[16,4,1536]{2,1,0:T(4,128)(2,1)} custom-call(s32[2]{0:T(128)S(1)} %pad_add_fusion.place_ref.refs_0_, bf16[8,1536]{1,0:T(8,128)(2,1)S(1)} %copy-done.2, f32[4,1536]{1,0:T(4,128)S(1)} %shard_map.86.refs_1_.order_ref), custom_call_target="tpu_custom_call" | custom-call | flops 6442450944 | bytes 786432 | tf_op jit(solution)/shard_map/pallas_call | solution.py:229
  8.2 9.9 %all-to-all-start = ((bf16[16,4,1536]{2,1,0:T(4,128)(2,1)}), bf16[16,4,1536]{2,1,0:T(4,128)(2,1)S(1)}, u32[]{:S(2)}, u32[]{:S(2)}) async-start(bf16[16,4,1536]{2,1,0:T(4,128)(2,1)} %shard_map.89), calls=%async_computation | async-start | bytes 393216 | tf_op jit(solution)/shard_map/all_to_all | solution.py:221
  18.1 1.4 %copy-done = bf16[8,64,1536]{2,1,0:T(8,128)(2,1)S(1)} copy-done((bf16[8,64,1536]{2,1,0:T(8,128)(2,1)S(1)}, bf16[8,64,1536]{2,1,0:T(8,128)(2,1)}, u32[]{:S(2)}) %copy-start) | copy-done | bytes 1572888
  19.5 1.5 %shard_map.87 = (bf16[32,1664]{1,0:T(8,128)(2,1)S(1)}, bf16[32,1664]{1,0:T(8,128)(2,1)S(1)}, bf16[32,1664]{1,0:T(8,128)(2,1)S(1)}, bf16[32,1664]{1,0:T(8,128)(2,1)S(1)}) custom-call(bf16[8,64,1536]{2,1,0:T(8,128)(2,1)S(1)} %copy-done, f32[4,1536]{1,0:T(4,128)S(1)} %shard_map.86.refs_1_.order_ref, f32[4,1536]{1,0:T(4,128)S(1)} %collective-permute-done.refs_2_, ...), custom_call_target="tpu_custom_call" | custom-call | flops 68719476736 | bytes 2359296 | tf_op jit(solution)/shard_map/pallas_call | solution.py:236
  21.1 2.4 %collective-permute-start.4 = (bf16[32,1664]{1,0:T(8,128)(2,1)S(1)}, bf16[32,1664]{1,0:T(8,128)(2,1)}, u32[]{:S(2)}, u32[]{:S(2)}) collective-permute-start(bf16[32,1664]{1,0:T(8,128)(2,1)S(1)} %get-tuple-element.10), channel_id=1, source_target_pairs={{0,2},{1,3},{2,0},{3,1},{4,6},{5,7},{6,4},{7,5},{8,10},{9,11},{10,... | collective-permute-start | bytes 319496 | tf_op jit(solution)/shard_map/ppermute | solution.py:38
  24.5 3.9 %all-to-all-done = bf16[16,4,1536]{2,1,0:T(4,128)(2,1)S(1)} async-done(((bf16[16,4,1536]{2,1,0:T(4,128)(2,1)}), bf16[16,4,1536]{2,1,0:T(4,128)(2,1)S(1)}, u32[]{:S(2)}, u32[]{:S(2)}) %all-to-all-start) | async-done | bytes 196640 | tf_op jit(solution)/shard_map/all_to_all | solution.py:221
  28.4 3.1 %collective-permute-start.10 = (bf16[64,1536]{1,0:T(8,128)(2,1)S(1)}, bf16[64,1536]{1,0:T(8,128)(2,1)S(1)}, u32[]{:S(2)}, u32[]{:S(2)}) collective-permute-start(bf16[64,1536]{1,0:T(8,128)(2,1)S(1)} %reshape.28.refs_3_.refs_6_), channel_id=1, source_target_pairs={{0,128},{4,132},{8,136},{12,140},{16,144},{20,148},{24,152},{28,15... | collective-permute-start | bytes 589832 | tf_op jit(solution)/shard_map/ppermute | solution.py:225
  31.6 1.1 %collective-permute-start.11 = (bf16[64,1536]{1,0:T(8,128)(2,1)S(1)}, bf16[64,1536]{1,0:T(8,128)(2,1)S(1)}, u32[]{:S(2)}, u32[]{:S(2)}) collective-permute-start(bf16[64,1536]{1,0:T(8,128)(2,1)S(1)} %reshape.28.refs_3_.refs_6_), channel_id=1, source_target_pairs={{0,192},{4,196},{8,200},{12,204},{16,208},{20,212},{24,216},{28,22... | collective-permute-start | bytes 589832 | tf_op jit(solution)/shard_map/ppermute | solution.py:225
  32.7 1.3 %copy-done.1 = bf16[384,1536]{1,0:T(8,128)(2,1)S(1)} copy-done((bf16[384,1536]{1,0:T(8,128)(2,1)S(1)}, bf16[384,1536]{1,0:T(8,128)(2,1)}, u32[]{:S(2)}) %copy-start.1) | copy-done | bytes 1179672
  34.9 1.6 %shard_map.88.e0 = f32[8,1536]{1,0:T(8,128)S(1)} custom-call(bf16[32,1664]{1,0:T(8,128)(2,1)S(1)} %copy-done.4, bf16[32,1664]{1,0:T(8,128)(2,1)S(1)} %collective-permute-done.3.refs_1_, bf16[32,1664]{1,0:T(8,128)(2,1)} %collective-permute-done.4.refs_2_, bf16[32,1664]{1,0:T(8,128)(2,1)} %collective-permute-done.5.refs_3_, bf16[1536,768]{1,0:T(8,128)(2,1)S(1)} %bitcast.9, ...), custom_call_target="tpu_custom_call" | custom-call | flops 68719476736 | bytes 2359296 | tf_op jit(solution)/shard_map/pallas_call | solution.py:245
  36.5 2.4 %collective-permute-start.7 = (f32[8,1536]{1,0:T(8,128)S(1)}, f32[8,1536]{1,0:T(8,128)S(1)}, u32[]{:S(2)}, u32[]{:S(2)}) collective-permute-start(f32[8,1536]{1,0:T(8,128)S(1)} %shard_map.88.e0), channel_id=1, source_target_pairs={{0,2},{1,3},{2,0},{3,1},{4,6},{5,7},{6,4},{7,5},{8,10},{9,11},{10,... | collective-permute-start | bytes 147464 | tf_op jit(solution)/shard_map/ppermute | solution.py:38
  42.2 1.9 %collective-permute-done.8.e3 = f32[8,1536]{1,0:T(8,128)S(1)} collective-permute-done((f32[8,1536]{1,0:T(8,128)S(1)}, f32[8,1536]{1,0:T(8,128)S(1)}, u32[]{:S(2)}, u32[]{:S(2)}) %collective-permute-start.8) | collective-permute-done | bytes 49184 | tf_op jit(solution)/shard_map/ppermute | solution.py:38
  44.2 2.0 %collective-permute-start.13 = (bf16[8,1536]{1,0:T(8,128)(2,1)S(1)}, bf16[8,1536]{1,0:T(8,128)(2,1)S(1)}, u32[]{:S(2)}, u32[]{:S(2)}) collective-permute-start(bf16[8,1536]{1,0:T(8,128)(2,1)S(1)} %shard_map.90.refs_2_), channel_id=1, source_target_pairs={{0,64},{4,68},{8,72},{12,76},{16,80},{20,84},{24,88},{28,92},{32,9... | collective-permute-start | bytes 73736 | tf_op jit(solution)/shard_map/ppermute | solution.py:225
  46.3 1.6 %collective-permute-start.14 = (bf16[8,1536]{1,0:T(8,128)(2,1)S(1)}, bf16[8,1536]{1,0:T(8,128)(2,1)S(1)}, u32[]{:S(2)}, u32[]{:S(2)}) collective-permute-start(bf16[8,1536]{1,0:T(8,128)(2,1)S(1)} %shard_map.90.refs_2_), channel_id=1, source_target_pairs={{0,128},{4,132},{8,136},{12,140},{16,144},{20,148},{24,152},{28,15... | collective-permute-start | bytes 73736 | tf_op jit(solution)/shard_map/ppermute | solution.py:225
  47.9 1.1 %collective-permute-start.15 = (bf16[8,1536]{1,0:T(8,128)(2,1)S(1)}, bf16[8,1536]{1,0:T(8,128)(2,1)S(1)}, u32[]{:S(2)}, u32[]{:S(2)}) collective-permute-start(bf16[8,1536]{1,0:T(8,128)(2,1)S(1)} %shard_map.90.refs_2_), channel_id=1, source_target_pairs={{0,192},{4,196},{8,200},{12,204},{16,208},{20,212},{24,216},{28,22... | collective-permute-start | bytes 73736 | tf_op jit(solution)/shard_map/ppermute | solution.py:225
  49.1 1.5 %shard_map.91 = (f32[2,1536]{1,0:T(2,128)S(1)}, f32[2,1536]{1,0:T(2,128)S(1)}) custom-call(s32[2]{0:T(128)S(1)} %pad_add_fusion.place_ref.refs_0_, f32[2]{0:T(128)S(1)} %pad_maximum_fusion.refs_1_, bf16[8,1536]{1,0:T(8,128)(2,1)S(1)} %shard_map.90.refs_2_, bf16[64,1536]{1,0:T(8,128)(2,1)S(1)} %reshape.28.refs_3_.refs_6_, ...), custom_call_target="tpu_custom_call" | custom-call | flops 12582912 | bytes 1572864 | tf_op jit(solution)/shard_map/pallas_call | solution.py:263
  50.6 1.0 %collective-permute-done.14.refs_4_ = bf16[8,1536]{1,0:T(8,128)(2,1)S(1)} collective-permute-done((bf16[8,1536]{1,0:T(8,128)(2,1)S(1)}, bf16[8,1536]{1,0:T(8,128)(2,1)S(1)}, u32[]{:S(2)}, u32[]{:S(2)}) %collective-permute-start.14) | collective-permute-done | bytes 24608 | tf_op jit(solution)/shard_map/ppermute | solution.py:225
  51.6 1.3 %collective-permute-done.15.refs_5_ = bf16[8,1536]{1,0:T(8,128)(2,1)S(1)} collective-permute-done((bf16[8,1536]{1,0:T(8,128)(2,1)S(1)}, bf16[8,1536]{1,0:T(8,128)(2,1)S(1)}, u32[]{:S(2)}, u32[]{:S(2)}) %collective-permute-start.15) | collective-permute-done | bytes 24608 | tf_op jit(solution)/shard_map/ppermute | solution.py:225
  52.9 1.7 %shard_map.92 = bf16[16,8,384]{2,1,0:T(8,128)(2,1)} custom-call(s32[2]{0:T(128)S(1)} %pad_add_fusion.place_ref.refs_0_, f32[2]{0:T(128)S(1)} %pad_maximum_fusion.refs_1_, bf16[8,1536]{1,0:T(8,128)(2,1)S(1)} %shard_map.90.refs_2_, bf16[8,1536]{1,0:T(8,128)(2,1)S(1)} %collective-permute-done.13.refs_3_, bf16[8,1536]{1,0:T(8,128)(2,1)S(1)} %collective-permute-done.14.refs_4_, ...), custom_call_target="tpu_custom_call" | custom-call | flops 12582912 | bytes 196608 | tf_op jit(solution)/shard_map/pallas_call | solution.py:271
  54.7 6.6 %all-to-all-start.1 = ((bf16[16,8,384]{2,1,0:T(8,128)(2,1)}), bf16[16,8,384]{2,1,0:T(8,128)(2,1)S(1)}, u32[]{:S(2)}, u32[]{:S(2)}) async-start(bf16[16,8,384]{2,1,0:T(8,128)(2,1)} %shard_map.92), calls=%async_computation.1 | async-start | bytes 196608 | tf_op jit(solution)/shard_map/all_to_all | solution.py:221
  61.3 1.2 %collective-permute-done.12 = f32[2,1536]{1,0:T(2,128)S(1)} collective-permute-done((f32[2,1536]{1,0:T(2,128)S(1)}, f32[2,1536]{1,0:T(2,128)S(1)}, u32[]{:S(2)}, u32[]{:S(2)}) %collective-permute-start.12) | collective-permute-done | bytes 12320 | tf_op jit(solution)/shard_map/ppermute | solution.py:270
  63.1 6.3 %all-to-all-done.1.part_ref = bf16[16,8,384]{2,1,0:T(8,128)(2,1)S(1)} async-done(((bf16[16,8,384]{2,1,0:T(8,128)(2,1)}), bf16[16,8,384]{2,1,0:T(8,128)(2,1)S(1)}, u32[]{:S(2)}, u32[]{:S(2)}) %all-to-all-start.1) | async-done | bytes 98336 | tf_op jit(solution)/shard_map/all_to_all | solution.py:221
  (41 shorter events, 7.1 us)
Async XLA Ops:
  0.6 2.2 %copy-start.5 = (bf16[4,96]{1,0:T(4,128)(2,1)S(1)}, bf16[4,96]{1,0:T(4,128)(2,1)}, u32[]{:S(2)}) copy-start(bf16[4,96]{1,0:T(4,128)(2,1)} %param.9) | copy-start | bytes 2308
  2.8 4.0 %copy-start.2 = (bf16[8,1536]{1,0:T(8,128)(2,1)S(1)}, bf16[8,1536]{1,0:T(8,128)(2,1)}, u32[]{:S(2)}) copy-start(bf16[8,1536]{1,0:T(8,128)(2,1)} %captions_ref.1) | copy-start | bytes 73732
  3.3 14.8 %collective-permute-start = (f32[4,1536]{1,0:T(4,128)S(1)}, f32[4,1536]{1,0:T(4,128)S(1)}, u32[]{:S(2)}, u32[]{:S(2)}) collective-permute-start(f32[4,1536]{1,0:T(4,128)S(1)} %shard_map.86.refs_1_.order_ref), channel_id=1, source_target_pairs={{0,1},{1,0},{2,3},{3,2},{4,5},{5,4},{6,7},{7,6},{8,9},{9,8},{10,11... | collective-permute-start | bytes 73736 | tf_op jit(solution)/shard_map/ppermute | solution.py:38
  3.4 14.7 %collective-permute-start.1 = (f32[4,1536]{1,0:T(4,128)S(1)}, f32[4,1536]{1,0:T(4,128)S(1)}, u32[]{:S(2)}, u32[]{:S(2)}) collective-permute-start(f32[4,1536]{1,0:T(4,128)S(1)} %shard_map.86.refs_1_.order_ref), channel_id=1, source_target_pairs={{0,2},{1,3},{2,0},{3,1},{4,6},{5,7},{6,4},{7,5},{8,10},{9,11},{10,... | collective-permute-start | bytes 73736 | tf_op jit(solution)/shard_map/ppermute | solution.py:38
  5.7 12.4 %collective-permute-start.2 = (f32[4,1536]{1,0:T(4,128)S(1)}, f32[4,1536]{1,0:T(4,128)S(1)}, u32[]{:S(2)}, u32[]{:S(2)}) collective-permute-start(f32[4,1536]{1,0:T(4,128)S(1)} %shard_map.86.refs_1_.order_ref), channel_id=1, source_target_pairs={{0,3},{1,2},{2,1},{3,0},{4,7},{5,6},{6,5},{7,4},{8,11},{9,10},{10,... | collective-permute-start | bytes 73736 | tf_op jit(solution)/shard_map/ppermute | solution.py:38
  8.2 20.2 %all-to-all-start = ((bf16[16,4,1536]{2,1,0:T(4,128)(2,1)}), bf16[16,4,1536]{2,1,0:T(4,128)(2,1)S(1)}, u32[]{:S(2)}, u32[]{:S(2)}) async-start(bf16[16,4,1536]{2,1,0:T(4,128)(2,1)} %shard_map.89), calls=%async_computation | async-start | bytes 393216 | tf_op jit(solution)/shard_map/all_to_all | solution.py:221
  18.1 1.4 %copy-start = (bf16[8,64,1536]{2,1,0:T(8,128)(2,1)S(1)}, bf16[8,64,1536]{2,1,0:T(8,128)(2,1)}, u32[]{:S(2)}) copy-start(bf16[8,64,1536]{2,1,0:T(8,128)(2,1)} %refs_0_.1) | copy-start | bytes 4718596
  21.0 11.7 %copy-start.3 = (bf16[32,1664]{1,0:T(8,128)(2,1)}, bf16[32,1664]{1,0:T(8,128)(2,1)S(1)}, u32[]{:S(2)}) copy-start(bf16[32,1664]{1,0:T(8,128)(2,1)S(1)} %get-tuple-element.8.refs_0_) | copy-start | bytes 319492
  21.0 11.7 %collective-permute-start.3 = (bf16[32,1664]{1,0:T(8,128)(2,1)S(1)}, bf16[32,1664]{1,0:T(8,128)(2,1)S(1)}, u32[]{:S(2)}, u32[]{:S(2)}) collective-permute-start(bf16[32,1664]{1,0:T(8,128)(2,1)S(1)} %get-tuple-element.9), channel_id=1, source_target_pairs={{0,1},{1,0},{2,3},{3,2},{4,5},{5,4},{6,7},{7,6},{8,9},{9,8},{10,11... | collective-permute-start | bytes 319496 | tf_op jit(solution)/shard_map/ppermute | solution.py:38
  21.1 11.6 %collective-permute-start.4 = (bf16[32,1664]{1,0:T(8,128)(2,1)S(1)}, bf16[32,1664]{1,0:T(8,128)(2,1)}, u32[]{:S(2)}, u32[]{:S(2)}) collective-permute-start(bf16[32,1664]{1,0:T(8,128)(2,1)S(1)} %get-tuple-element.10), channel_id=1, source_target_pairs={{0,2},{1,3},{2,0},{3,1},{4,6},{5,7},{6,4},{7,5},{8,10},{9,11},{10,... | collective-permute-start | bytes 319496 | tf_op jit(solution)/shard_map/ppermute | solution.py:38
  23.5 9.2 %collective-permute-start.5 = (bf16[32,1664]{1,0:T(8,128)(2,1)S(1)}, bf16[32,1664]{1,0:T(8,128)(2,1)}, u32[]{:S(2)}, u32[]{:S(2)}) collective-permute-start(bf16[32,1664]{1,0:T(8,128)(2,1)S(1)} %get-tuple-element.11), channel_id=1, source_target_pairs={{0,3},{1,2},{2,1},{3,0},{4,7},{5,6},{6,5},{7,4},{8,11},{9,10},{10,... | collective-permute-start | bytes 319496 | tf_op jit(solution)/shard_map/ppermute | solution.py:38
  28.4 15.7 %collective-permute-start.10 = (bf16[64,1536]{1,0:T(8,128)(2,1)S(1)}, bf16[64,1536]{1,0:T(8,128)(2,1)S(1)}, u32[]{:S(2)}, u32[]{:S(2)}) collective-permute-start(bf16[64,1536]{1,0:T(8,128)(2,1)S(1)} %reshape.28.refs_3_.refs_6_), channel_id=1, source_target_pairs={{0,128},{4,132},{8,136},{12,140},{16,144},{20,148},{24,152},{28,15... | collective-permute-start | bytes 589832 | tf_op jit(solution)/shard_map/ppermute | solution.py:225
  31.6 12.6 %collective-permute-start.11 = (bf16[64,1536]{1,0:T(8,128)(2,1)S(1)}, bf16[64,1536]{1,0:T(8,128)(2,1)S(1)}, u32[]{:S(2)}, u32[]{:S(2)}) collective-permute-start(bf16[64,1536]{1,0:T(8,128)(2,1)S(1)} %reshape.28.refs_3_.refs_6_), channel_id=1, source_target_pairs={{0,192},{4,196},{8,200},{12,204},{16,208},{20,212},{24,216},{28,22... | collective-permute-start | bytes 589832 | tf_op jit(solution)/shard_map/ppermute | solution.py:225
  32.7 11.4 %collective-permute-start.9 = (bf16[64,1536]{1,0:T(8,128)(2,1)S(1)}, bf16[64,1536]{1,0:T(8,128)(2,1)S(1)}, u32[]{:S(2)}, u32[]{:S(2)}) collective-permute-start(bf16[64,1536]{1,0:T(8,128)(2,1)S(1)} %reshape.28.refs_3_.refs_6_), channel_id=1, source_target_pairs={{0,64},{4,68},{8,72},{12,76},{16,80},{20,84},{24,88},{28,92},{32,9... | collective-permute-start | bytes 589832 | tf_op jit(solution)/shard_map/ppermute | solution.py:225
  32.7 1.3 %copy-start.1 = (bf16[384,1536]{1,0:T(8,128)(2,1)S(1)}, bf16[384,1536]{1,0:T(8,128)(2,1)}, u32[]{:S(2)}) copy-start(bf16[384,1536]{1,0:T(8,128)(2,1)} %refs_5_.1) | copy-start | bytes 3538948
  34.0 0.9 %copy-start.4 = (bf16[32,1664]{1,0:T(8,128)(2,1)S(1)}, bf16[32,1664]{1,0:T(8,128)(2,1)}, u32[]{:S(2)}) copy-start(bf16[32,1664]{1,0:T(8,128)(2,1)} %copy-done.3) | copy-start | bytes 319492
  36.5 2.4 %collective-permute-start.6 = (f32[8,1536]{1,0:T(8,128)S(1)}, f32[8,1536]{1,0:T(8,128)S(1)}, u32[]{:S(2)}, u32[]{:S(2)}) collective-permute-start(f32[8,1536]{1,0:T(8,128)S(1)} %shard_map.88.e0), channel_id=1, source_target_pairs={{0,1},{1,0},{2,3},{3,2},{4,5},{5,4},{6,7},{7,6},{8,9},{9,8},{10,11... | collective-permute-start | bytes 147464 | tf_op jit(solution)/shard_map/ppermute | solution.py:38
  36.5 5.7 %collective-permute-start.7 = (f32[8,1536]{1,0:T(8,128)S(1)}, f32[8,1536]{1,0:T(8,128)S(1)}, u32[]{:S(2)}, u32[]{:S(2)}) collective-permute-start(f32[8,1536]{1,0:T(8,128)S(1)} %shard_map.88.e0), channel_id=1, source_target_pairs={{0,2},{1,3},{2,0},{3,1},{4,6},{5,7},{6,4},{7,5},{8,10},{9,11},{10,... | collective-permute-start | bytes 147464 | tf_op jit(solution)/shard_map/ppermute | solution.py:38
  38.9 5.2 %collective-permute-start.8 = (f32[8,1536]{1,0:T(8,128)S(1)}, f32[8,1536]{1,0:T(8,128)S(1)}, u32[]{:S(2)}, u32[]{:S(2)}) collective-permute-start(f32[8,1536]{1,0:T(8,128)S(1)} %shard_map.88.e0), channel_id=1, source_target_pairs={{0,3},{1,2},{2,1},{3,0},{4,7},{5,6},{6,5},{7,4},{8,11},{9,10},{10,... | collective-permute-start | bytes 147464 | tf_op jit(solution)/shard_map/ppermute | solution.py:38
  44.2 6.3 %collective-permute-start.13 = (bf16[8,1536]{1,0:T(8,128)(2,1)S(1)}, bf16[8,1536]{1,0:T(8,128)(2,1)S(1)}, u32[]{:S(2)}, u32[]{:S(2)}) collective-permute-start(bf16[8,1536]{1,0:T(8,128)(2,1)S(1)} %shard_map.90.refs_2_), channel_id=1, source_target_pairs={{0,64},{4,68},{8,72},{12,76},{16,80},{20,84},{24,88},{28,92},{32,9... | collective-permute-start | bytes 73736 | tf_op jit(solution)/shard_map/ppermute | solution.py:225
  46.3 5.3 %collective-permute-start.14 = (bf16[8,1536]{1,0:T(8,128)(2,1)S(1)}, bf16[8,1536]{1,0:T(8,128)(2,1)S(1)}, u32[]{:S(2)}, u32[]{:S(2)}) collective-permute-start(bf16[8,1536]{1,0:T(8,128)(2,1)S(1)} %shard_map.90.refs_2_), channel_id=1, source_target_pairs={{0,128},{4,132},{8,136},{12,140},{16,144},{20,148},{24,152},{28,15... | collective-permute-start | bytes 73736 | tf_op jit(solution)/shard_map/ppermute | solution.py:225
  47.9 5.0 %collective-permute-start.15 = (bf16[8,1536]{1,0:T(8,128)(2,1)S(1)}, bf16[8,1536]{1,0:T(8,128)(2,1)S(1)}, u32[]{:S(2)}, u32[]{:S(2)}) collective-permute-start(bf16[8,1536]{1,0:T(8,128)(2,1)S(1)} %shard_map.90.refs_2_), channel_id=1, source_target_pairs={{0,192},{4,196},{8,200},{12,204},{16,208},{20,212},{24,216},{28,22... | collective-permute-start | bytes 73736 | tf_op jit(solution)/shard_map/ppermute | solution.py:225
  54.7 14.7 %all-to-all-start.1 = ((bf16[16,8,384]{2,1,0:T(8,128)(2,1)}), bf16[16,8,384]{2,1,0:T(8,128)(2,1)S(1)}, u32[]{:S(2)}, u32[]{:S(2)}) async-start(bf16[16,8,384]{2,1,0:T(8,128)(2,1)} %shard_map.92), calls=%async_computation.1 | async-start | bytes 196608 | tf_op jit(solution)/shard_map/all_to_all | solution.py:221
  61.3 1.2 %collective-permute-start.12 = (f32[2,1536]{1,0:T(2,128)S(1)}, f32[2,1536]{1,0:T(2,128)S(1)}, u32[]{:S(2)}, u32[]{:S(2)}) collective-permute-start(f32[2,1536]{1,0:T(2,128)S(1)} %get-tuple-element.13), channel_id=1, source_target_pairs={{0,1},{1,0},{2,3},{3,2},{4,5},{5,4},{6,7},{7,6},{8,9},{9,8},{10,11... | collective-permute-start | bytes 36872 | tf_op jit(solution)/shard_map/ppermute | solution.py:270

commit v3 on v2

--- a/solution.py
+++ b/solution.py
@@ -13,17 +13,19 @@
 TN = (((0,), (0,)), ((), ()))
 VMEM = pl.BlockSpec(memory_space=pltpu.VMEM)
 ANY = pl.BlockSpec(memory_space=pl.ANY)
+HBM = pl.BlockSpec(memory_space=pltpu.HBM)
 SMEM = pl.BlockSpec(memory_space=pltpu.SMEM)
 
 
-def call(kernel, outs, specs, flops, moved):
+def call(kernel, outs, specs, flops, moved, scratch=(), out_specs=None):
     return pl.pallas_call(
         kernel,
         grid=(1,),
         out_shape=outs,
         in_specs=specs,
-        out_specs=jax.tree.map(lambda _: VMEM, outs),
-        compiler_params=pltpu.CompilerParams(vmem_limit_bytes=10 << 20),
+        out_specs=out_specs or jax.tree.map(lambda _: VMEM, outs),
+        scratch_shapes=scratch,
+        compiler_params=pltpu.CompilerParams(vmem_limit_bytes=12 << 20),
         cost_estimate=pl.CostEstimate(flops=flops, bytes_accessed=moved, transcendentals=0),
     )
 
@@ -33,10 +35,8 @@
     return (widened * lax.rsqrt(jnp.sum(widened * widened, -1, keepdims=True) + 1e-06)).astype(BF16)
 
 
-def peers(pieces):
-    return [pieces[0]] + [
-        lax.ppermute(pieces[s], "head", [(i, i ^ s) for i in range(4)]) for s in (1, 2, 3)
-    ]
+def peer(piece, step):
+    return lax.ppermute(piece, "head", [(i, i ^ step) for i in range(4)])
 
 
 def key_query_kernel(spread_ref, key_ref, out_ref, *, scale):
@@ -45,14 +45,22 @@
     )
 
 
-def mix_kernel(tokens_ref, q0, q1, q2, q3, m0, m1, m2, m3, *, images):
-    count, here, width = tokens_ref.shape
-    rows = tokens_ref[...].reshape(count * here, width)
+def mix_kernel(own_ref, other_ref, q0, q1, m0, m1, near_ref, done, *, images):
+    half = images // 2
+    copies = [
+        pltpu.make_async_copy(
+            other_ref.at[pl.ds(c * half, half)], near_ref.at[pl.ds(c * half, half)], done.at[c]
+        )
+        for c in range(2)
+    ]
+    for copy in copies:
+        copy.start()
+    here, width = own_ref.shape[1:]
     heads = q0.shape[0]
     spread = jnp.concatenate(
         [
             jnp.broadcast_to(ref[h : h + 1, :], (images, width))
-            for ref in (q0, q1, q2, q3)
+            for ref in (q0, q1)
             for h in range(heads)
         ],
         0,
@@ -60,39 +68,46 @@
     columns = spread.shape[0]
     high = spread.astype(BF16)
     low = (spread - high.astype(F32)).astype(BF16)
-    raw = lax.dot_general(rows, jnp.concatenate([high, low], 0), NT, preferred_element_type=F32)
-    scores = raw[:, :columns] + raw[:, columns:]
-    row_image = lax.broadcasted_iota(jnp.int32, scores.shape, 0) // here
-    column_image = lax.broadcasted_iota(jnp.int32, scores.shape, 1) % images
-    mine = row_image == column_image
-    top = jnp.max(jnp.where(mine, scores, -jnp.inf), 0, keepdims=True)
+    both = jnp.concatenate([high, low], 0)
+    own = own_ref[...].reshape(images * here, width)
+    raw = [lax.dot_general(both, own, NT, preferred_element_type=F32)]
+    for copy in copies:
+        copy.wait()
+    other = near_ref[...].reshape(images * here, width)
+    raw.append(lax.dot_general(both, other, NT, preferred_element_type=F32))
+    raw = jnp.concatenate(raw, 1)
+    scores = raw[:columns] + raw[columns:]
+    row_image = lax.broadcasted_iota(jnp.int32, scores.shape, 0) % images
+    token_image = lax.broadcasted_iota(jnp.int32, scores.shape, 1) // here % images
+    mine = row_image == token_image
+    top = jnp.max(jnp.where(mine, scores, -jnp.inf), 1, keepdims=True)
     raised = jnp.exp(jnp.where(mine, scores - top, -jnp.inf))
-    total = jnp.sum(raised, 0, keepdims=True)
+    total = jnp.sum(raised, 1, keepdims=True)
     weights = (raised / total).astype(BF16)
-    mixed = lax.dot_general(weights, rows, TN, preferred_element_type=F32).astype(BF16)
-    log_total = jnp.broadcast_to(top + jnp.log(total), (columns, columns))
-    down = lax.broadcasted_iota(jnp.int32, (columns, columns), 0)
-    across = lax.broadcasted_iota(jnp.int32, (columns, columns), 1)
-    upright = jnp.sum(jnp.where(down == across, log_total, 0.0), 1, keepdims=True)
-    high = upright.astype(BF16).astype(F32)
-    middle = (upright - high).astype(BF16).astype(F32)
-    low = upright - high - middle
+    split = images * here
+    mixed = jnp.dot(weights[:, :split], own, preferred_element_type=F32)
+    mixed = mixed + jnp.dot(weights[:, split:], other, preferred_element_type=F32)
+    mixed = mixed.astype(BF16)
+    log_total = top + jnp.log(total)
+    high = log_total.astype(BF16).astype(F32)
+    middle = (log_total - high).astype(BF16).astype(F32)
+    low = log_total - high - middle
     lane = lax.broadcasted_iota(jnp.int32, (columns, 128), 1)
     pieces = jnp.where(lane == 0, high, jnp.where(lane == 1, middle, jnp.where(lane == 2, low, 0.0)))
     pieces = pieces.astype(BF16)
-    step = columns // 4
-    for s, ref in enumerate((m0, m1, m2, m3)):
+    step = columns // 2
+    for s, ref in enumerate((m0, m1)):
         ref[:, :width] = mixed[s * step : (s + 1) * step]
         ref[:, width:] = pieces[s * step : (s + 1) * step]
 
 
-def embed_kernel(m0, m1, m2, m3, value_ref, final_ref, out_ref, *, heads):
+def embed_kernel(m0, m1, value_ref, final_ref, out_ref, *, heads):
     width = value_ref.shape[0]
-    parts = (m0, m1, m2, m3)
+    parts = (m0, m1)
     logs = [jnp.sum(ref[:, width:].astype(F32), -1, keepdims=True) for ref in parts]
-    peak = jnp.maximum(jnp.maximum(logs[0], logs[1]), jnp.maximum(logs[2], logs[3]))
+    peak = jnp.maximum(logs[0], logs[1])
     shares = [jnp.exp(entry - peak) for entry in logs]
-    whole = (shares[0] + shares[1]) + (shares[2] + shares[3])
+    whole = shares[0] + shares[1]
     mixed = sum((s / whole) * ref[:, :width].astype(F32) for s, ref in zip(shares, parts))
     pooled = jnp.dot(mixed.astype(BF16), value_ref[...], preferred_element_type=F32)
     rows, columns = pooled.shape
@@ -111,6 +126,11 @@
     second = jnp.concatenate([unit[2:4], unit[6:8]], 0)
     chosen = jnp.where(core == 0, first, second).astype(BF16)
     out_ref[...] = jnp.broadcast_to(chosen[None], out_ref.shape)
+
+
+def rows_kernel(text_ref, order_ref, final_ref, rows_ref):
+    texts = text_ref[...].astype(F32)
+    rows_ref[...] = jnp.concatenate([texts[i] for i in range(texts.shape[0])], 0).astype(BF16)
 
 
 def text_ids(shape, first_dp, images, head):
@@ -158,23 +178,31 @@
     images, width = unit_ref.shape
     share = images // 4
     block = dp // near
-    grads = jnp.zeros((images, width), F32)
-    for s, ref in enumerate((t0, t1, t2, t3)):
-        texts = ref[...]
-        logits = lax.dot_general(unit_ref[...], texts, NT, preferred_element_type=F32)
-        logits = logits * multiplier + shift
-        image_id = dp * images + lax.broadcasted_iota(jnp.int32, logits.shape, 0)
-        text_id = text_ids(logits.shape, (block ^ s) * near, images, head)
-        matched = jnp.where(image_id == text_id, 1.0, 0.0)
-        coefficient = (multiplier * (jax.nn.sigmoid(logits) - matched)).astype(BF16)
-        grads = grads + jnp.dot(coefficient, texts, preferred_element_type=F32)
+    texts = [ref[...] for ref in (t0, t1, t2, t3)]
+    count = texts[0].shape[0]
+    logits = [
+        lax.dot_general(unit_ref[...], part, NT, preferred_element_type=F32) for part in texts
+    ]
+    logits = jnp.concatenate(logits, 1) * multiplier + shift
+    image_id = dp * images + lax.broadcasted_iota(jnp.int32, logits.shape, 0)
+    column = lax.broadcasted_iota(jnp.int32, logits.shape, 1)
+    first_dp = ((column // count) ^ block) * near
+    text_id = (first_dp + column % count // 4) * images
+    text_id = text_id + column % 4 // 2 * 4 + head % 2 * 2 + column % 2
+    matched = jnp.where(image_id == text_id, 1.0, 0.0)
+    coefficient = (multiplier * (jax.nn.sigmoid(logits) - matched)).astype(BF16)
+    grads = sum(
+        jnp.dot(coefficient[:, s * count : (s + 1) * count], part, preferred_element_type=F32)
+        for s, part in enumerate(texts)
+    )
     for wanted, ref in ((head, own_ref), (head ^ 1, other_ref)):
         ref[...] = sum(
             jnp.where(wanted == k, grads[k * share : (k + 1) * share], 0.0) for k in range(4)
         )
 
 
-def sum_kernel(part_ref, out_ref):
+def sum_kernel(part_ref, own_ref, other_ref, image_ref, out_ref):
+    image_ref[...] = own_ref[...] + other_ref[...]
     share, width = out_ref.shape
     chunk = part_ref.shape[2]
     total = jnp.sum(part_ref[...].astype(F32), 0)
@@ -205,6 +233,7 @@
     def bf16(*shape):
         return jax.ShapeDtypeStruct(shape, BF16)
 
+    other_tokens = peer(tokens, 1)
     key_query = call(
         lambda *refs: key_query_kernel(*refs, scale=1.0 / math.sqrt(head_size)),
         f32(heads, width),
@@ -212,7 +241,6 @@
         2 * heads * width * columns,
         2 * width * columns,
     )(spread, both)
-    queried = peers([key_query] * 4)
 
     place = jnp.stack([dp, head]).astype(jnp.int32)
     groups = [[b * near + i for i in range(near)] for b in range(4)]
@@ -229,27 +257,28 @@
     text_copies = call(
         text_kernel, bf16(near, 4, width), [SMEM, VMEM, ANY], 6 << 30, 8 * n_dp * width
     )(place, captions, key_query)
-    texts = swap(text_copies).reshape(near * 4, width)
-    all_texts = across([texts] * 4)
-
-    message = [bf16(heads * images, width + 128)] * 4
+    copies = swap(text_copies)
+
     mixes = call(
         lambda *refs: mix_kernel(*refs, images=images),
-        message,
-        [VMEM] * 5,
+        [bf16(heads * images, width + 128)] * 2,
+        [VMEM, ANY, VMEM, VMEM],
         64 << 30,
-        3 * images * here * width,
-    )(tokens, *queried)
-    mixes = peers(mixes)
-
+        6 * images * here * width,
+        [pltpu.VMEM(tokens.shape, BF16), pltpu.SemaphoreType.DMA((2,))],
+    )(tokens, other_tokens, key_query, peer(key_query, 2))
+    texts = call(
+        rows_kernel, bf16(near * 4, width), [VMEM, ANY, ANY], near * 4 * width, 16 * near * width
+    )(copies, mixes[0], final)
+    all_texts = across([texts] * 4)
     embeds = call(
         lambda *refs: embed_kernel(*refs, heads=heads),
         f32(images, width),
-        [VMEM] * 4 + [value_spec, VMEM],
+        [VMEM, VMEM, value_spec, VMEM],
         64 << 30,
         4 * width * columns,
-    )(*mixes, both, final)
-    embeds = peers([embeds] * 4)
+    )(mixes[0], peer(mixes[1], 2), both, final)
+    embeds = [embeds] + [peer(embeds, s) for s in (1, 2, 3)]
 
     scalars = jnp.stack([multiplier, shift])
     unit = call(
@@ -267,7 +296,7 @@
         2 * 64 * n_dp * width,
         16 * n_dp * width,
     )(place, scalars, unit, *all_texts)
-    image_grad = own_part + lax.ppermute(other_part, "head", [(i, i ^ 1) for i in range(4)])
+    other_part = peer(other_part, 1)
     text_part = call(
         lambda *refs: text_grad_kernel(*refs, near=near),
         bf16(near, 4 * share, width // 4),
@@ -276,9 +305,9 @@
         8 * near * width,
     )(place, scalars, *units, texts, own_part)
     received = swap(text_part)
-    text_grad = call(
-        sum_kernel, f32(share, width), [VMEM], near * share * width, 2 * near * share * width
-    )(received)
+    image_grad, text_grad = call(
+        sum_kernel, [f32(share, width)] * 2, [VMEM] * 3, near * share * width, 2 * near * share * width
+    )(received, own_part, other_part)
     return image_grad, text_grad
 
 

time: 70.4 us -> 65.6 us (0.932)
  the two profiles are of different devices: /device:TPU:8 before, /device:TPU:2 now
where the time goes in v3:
time: 65.6 us; the launch traced here: 65.2 us
  starting transfers between devices  30.1 us (46%)
  waiting for transfers between devices  18.6 us (28%)
  Pallas kernels  9.41 us (14%)
  local copies, waits for them, and re-layouts  4.92 us (8%)
  between operations  2.08 us (3%)
    all_to_all x2, starting transfers between devices, swap(): lax.all_to_all(pieces, 'dp', 0, 0, axis_index_groups=groups, tiled=False)  13 us
    all_to_all x2, waiting for transfers between devices, swap(): lax.all_to_all(pieces, 'dp', 0, 0, axis_index_groups=groups, tiled=False)  12.5 us
    ppermute x7, starting transfers between devices, peer(): return lax.ppermute(piece, 'head', [(i, i ^ step) for i in range(4)])  8.72 us
    ppermute x6, starting transfers between devices, across(): lax.ppermute(pieces[s], 'dp', [(i, i ^ s * near) for i in range(n_dp)])  8.29 us
    unnamed x9, local copies, waits for them, and re-layouts  4.83 us
    ppermute x7, waiting for transfers between devices, peer(): return lax.ppermute(piece, 'head', [(i, i ^ step) for i in range(4)])  3.62 us
    pallas_call x1, Pallas kernels, per_device(): call(lambda *refs: mix_kernel(*refs, images=images), [bf16(heads * images...  3.3 us
    ppermute x6, waiting for transfers between devices, across(): lax.ppermute(pieces[s], 'dp', [(i, i ^ s * near) for i in range(n_dp)])  2.45 us
  transfers between devices with their start and end apart: 15, of which 8 were waited for; matrix products, arithmetic and copies ran while one was open for 4% of the time, Pallas kernels for 11%

profile of v3, /device:TPU:2, one launch (start us, length us, event | category | flops | bytes accessed | tf_op | source)
XLA Modules:
  0.0 65.2 jit_solution(15363982573465396728)
XLA Ops:
  0.7 2.1 %copy.9 = bf16[192,8,2,384]{3,1,2,0:T(8,128)(2,1)S(1)} copy(bf16[192,8,2,384]{3,2,1,0:T(2,128)(2,1)} %bitcast.10) | data formatting | bytes 4718592
  3.4 3.2 %collective-permute-start.1 = (f32[4,1536]{1,0:T(4,128)S(1)}, f32[4,1536]{1,0:T(4,128)S(1)}, u32[]{:S(2)}, u32[]{:S(2)}) collective-permute-start(f32[4,1536]{1,0:T(4,128)S(1)} %shard_map.86.refs_2_.order_ref), channel_id=1, source_target_pairs={{0,2},{1,3},{2,0},{3,1},{4,6},{5,7},{6,4},{7,5},{8,10},{9,11},{10,... | collective-permute-start | bytes 73736 | tf_op jit(solution)/shard_map/ppermute | solution.py:39
  6.7 1.3 %shard_map.89 = bf16[16,4,1536]{2,1,0:T(4,128)(2,1)} custom-call(s32[2]{0:T(128)S(1)} %pad_add_fusion.place_ref.refs_0_, bf16[8,1536]{1,0:T(8,128)(2,1)S(1)} %copy-done.2, f32[4,1536]{1,0:T(4,128)S(1)} %shard_map.86.refs_2_.order_ref), custom_call_target="tpu_custom_call" | custom-call | flops 6442450944 | bytes 786432 | tf_op jit(solution)/shard_map/pallas_call | solution.py:257
  8.1 8.7 %all-to-all-start = ((bf16[16,4,1536]{2,1,0:T(4,128)(2,1)}), bf16[16,4,1536]{2,1,0:T(4,128)(2,1)S(1)}, u32[]{:S(2)}, u32[]{:S(2)}) async-start(bf16[16,4,1536]{2,1,0:T(4,128)(2,1)} %shard_map.89), calls=%async_computation | async-start | bytes 393216 | tf_op jit(solution)/shard_map/all_to_all | solution.py:249
  16.8 1.4 %copy-done.1 = bf16[8,64,1536]{2,1,0:T(8,128)(2,1)S(1)} copy-done((bf16[8,64,1536]{2,1,0:T(8,128)(2,1)S(1)}, bf16[8,64,1536]{2,1,0:T(8,128)(2,1)}, u32[]{:S(2)}) %copy-start.1) | copy-done | bytes 1572888
  18.2 3.3 %shard_map.87 = (bf16[32,1664]{1,0:T(8,128)(2,1)S(1)}, bf16[32,1664]{1,0:T(8,128)(2,1)S(1)}) custom-call(bf16[8,64,1536]{2,1,0:T(8,128)(2,1)S(1)} %copy-done.1, bf16[8,64,1536]{2,1,0:T(8,128)(2,1)} %collective-permute-done.refs_1_, f32[4,1536]{1,0:T(4,128)S(1)} %shard_map.86.refs_2_.order_ref, f32[4,1536]{1,0:T(4,128)S(1)} %collective-permute-done.1.refs_3_), custom_call_target="tpu_custom_call" | custom-call | flops 68719476736 | bytes 4718592 | tf_op jit(solution)/shard_map/pallas_call | solution.py:262
  21.5 1.9 %collective-permute-start.2 = (bf16[32,1664]{1,0:T(8,128)(2,1)S(1)}, bf16[32,1664]{1,0:T(8,128)(2,1)S(1)}, u32[]{:S(2)}, u32[]{:S(2)}) collective-permute-start(bf16[32,1664]{1,0:T(8,128)(2,1)S(1)} %get-tuple-element.7), channel_id=1, source_target_pairs={{0,2},{1,3},{2,0},{3,1},{4,6},{5,7},{6,4},{7,5},{8,10},{9,11},{10,... | collective-permute-start | bytes 319496 | tf_op jit(solution)/shard_map/ppermute | solution.py:39
  23.4 4.5 %all-to-all-done.text_ref = bf16[16,4,1536]{2,1,0:T(4,128)(2,1)S(1)} async-done(((bf16[16,4,1536]{2,1,0:T(4,128)(2,1)}), bf16[16,4,1536]{2,1,0:T(4,128)(2,1)S(1)}, u32[]{:S(2)}, u32[]{:S(2)}) %all-to-all-start) | async-done | bytes 196640 | tf_op jit(solution)/shard_map/all_to_all | solution.py:249
  27.9 1.3 %copy-done = bf16[384,1536]{1,0:T(8,128)(2,1)S(1)} copy-done((bf16[384,1536]{1,0:T(8,128)(2,1)S(1)}, bf16[384,1536]{1,0:T(8,128)(2,1)}, u32[]{:S(2)}) %copy-start) | copy-done | bytes 1179672
  29.8 2.4 %collective-permute-start.7 = (bf16[64,1536]{1,0:T(8,128)(2,1)S(1)}, bf16[64,1536]{1,0:T(8,128)(2,1)S(1)}, u32[]{:S(2)}, u32[]{:S(2)}) collective-permute-start(bf16[64,1536]{1,0:T(8,128)(2,1)S(1)} %shard_map.90.refs_3_.refs_6_), channel_id=1, source_target_pairs={{0,128},{4,132},{8,136},{12,140},{16,144},{20,148},{24,152},{28,15... | collective-permute-start | bytes 589832 | tf_op jit(solution)/shard_map/ppermute | solution.py:253
  32.8 0.7 %shard_map.88.e0 = f32[8,1536]{1,0:T(8,128)S(1)} custom-call(bf16[32,1664]{1,0:T(8,128)(2,1)S(1)} %get-tuple-element.6.refs_0_.order_ref, bf16[32,1664]{1,0:T(8,128)(2,1)S(1)} %collective-permute-done.2.refs_1_, bf16[1536,768]{1,0:T(8,128)(2,1)S(1)} %bitcast.9, bf16[384,1536]{1,0:T(8,128)(2,1)S(1)} %copy-done), custom_call_target="tpu_custom_call" | custom-call | flops 68719476736 | bytes 2359296 | tf_op jit(solution)/shard_map/pallas_call | solution.py:274
  33.5 1.9 %collective-permute-start.4 = (f32[8,1536]{1,0:T(8,128)S(1)}, f32[8,1536]{1,0:T(8,128)S(1)}, u32[]{:S(2)}, u32[]{:S(2)}) collective-permute-start(f32[8,1536]{1,0:T(8,128)S(1)} %shard_map.88.e0), channel_id=1, source_target_pairs={{0,2},{1,3},{2,0},{3,1},{4,6},{5,7},{6,4},{7,5},{8,10},{9,11},{10,... | collective-permute-start | bytes 147464 | tf_op jit(solution)/shard_map/ppermute | solution.py:39
  35.4 1.5 %collective-permute-start.5 = (f32[8,1536]{1,0:T(8,128)S(1)}, f32[8,1536]{1,0:T(8,128)S(1)}, u32[]{:S(2)}, u32[]{:S(2)}) collective-permute-start(f32[8,1536]{1,0:T(8,128)S(1)} %shard_map.88.e0), channel_id=1, source_target_pairs={{0,3},{1,2},{2,1},{3,0},{4,7},{5,6},{6,5},{7,4},{8,11},{9,10},{10,... | collective-permute-start | bytes 147464 | tf_op jit(solution)/shard_map/ppermute | solution.py:39
  38.2 1.0 %collective-permute-done.4.e2 = f32[8,1536]{1,0:T(8,128)S(1)} collective-permute-done((f32[8,1536]{1,0:T(8,128)S(1)}, f32[8,1536]{1,0:T(8,128)S(1)}, u32[]{:S(2)}, u32[]{:S(2)}) %collective-permute-start.4) | collective-permute-done | bytes 49184 | tf_op jit(solution)/shard_map/ppermute | solution.py:39
  39.2 1.4 %collective-permute-done.5.e3 = f32[8,1536]{1,0:T(8,128)S(1)} collective-permute-done((f32[8,1536]{1,0:T(8,128)S(1)}, f32[8,1536]{1,0:T(8,128)S(1)}, u32[]{:S(2)}, u32[]{:S(2)}) %collective-permute-start.5) | collective-permute-done | bytes 49184 | tf_op jit(solution)/shard_map/ppermute | solution.py:39
  41.3 2.8 %collective-permute-start.10 = (bf16[8,1536]{1,0:T(8,128)(2,1)S(1)}, bf16[8,1536]{1,0:T(8,128)(2,1)S(1)}, u32[]{:S(2)}, u32[]{:S(2)}) collective-permute-start(bf16[8,1536]{1,0:T(8,128)(2,1)S(1)} %shard_map.91.refs_2_), channel_id=1, source_target_pairs={{0,128},{4,132},{8,136},{12,140},{16,144},{20,148},{24,152},{28,15... | collective-permute-start | bytes 73736 | tf_op jit(solution)/shard_map/ppermute | solution.py:253
  44.1 1.2 %collective-permute-start.11 = (bf16[8,1536]{1,0:T(8,128)(2,1)S(1)}, bf16[8,1536]{1,0:T(8,128)(2,1)S(1)}, u32[]{:S(2)}, u32[]{:S(2)}) collective-permute-start(bf16[8,1536]{1,0:T(8,128)(2,1)S(1)} %shard_map.91.refs_2_), channel_id=1, source_target_pairs={{0,192},{4,196},{8,200},{12,204},{16,208},{20,212},{24,216},{28,22... | collective-permute-start | bytes 73736 | tf_op jit(solution)/shard_map/ppermute | solution.py:253
  45.3 0.7 %collective-permute-start.9 = (bf16[8,1536]{1,0:T(8,128)(2,1)S(1)}, bf16[8,1536]{1,0:T(8,128)(2,1)S(1)}, u32[]{:S(2)}, u32[]{:S(2)}) collective-permute-start(bf16[8,1536]{1,0:T(8,128)(2,1)S(1)} %shard_map.91.refs_2_), channel_id=1, source_target_pairs={{0,64},{4,68},{8,72},{12,76},{16,80},{20,84},{24,88},{28,92},{32,9... | collective-permute-start | bytes 73736 | tf_op jit(solution)/shard_map/ppermute | solution.py:253
  46.1 1.2 %shard_map.92 = (f32[2,1536]{1,0:T(2,128)S(1)}, f32[2,1536]{1,0:T(2,128)S(1)}) custom-call(s32[2]{0:T(128)S(1)} %pad_add_fusion.place_ref.refs_0_, f32[2]{0:T(128)S(1)} %pad_maximum_fusion.refs_1_, bf16[8,1536]{1,0:T(8,128)(2,1)S(1)} %shard_map.91.refs_2_, bf16[64,1536]{1,0:T(8,128)(2,1)S(1)} %shard_map.90.refs_3_.refs_6_, ...), custom_call_target="tpu_custom_call" | custom-call | flops 12582912 | bytes 1572864 | tf_op jit(solution)/shard_map/pallas_call | solution.py:292
  47.9 1.2 %collective-permute-done.9.refs_3_ = bf16[8,1536]{1,0:T(8,128)(2,1)S(1)} collective-permute-done((bf16[8,1536]{1,0:T(8,128)(2,1)S(1)}, bf16[8,1536]{1,0:T(8,128)(2,1)S(1)}, u32[]{:S(2)}, u32[]{:S(2)}) %collective-permute-start.9) | collective-permute-done | bytes 24608 | tf_op jit(solution)/shard_map/ppermute | solution.py:253
  49.1 1.7 %shard_map.93 = bf16[16,8,384]{2,1,0:T(8,128)(2,1)} custom-call(s32[2]{0:T(128)S(1)} %pad_add_fusion.place_ref.refs_0_, f32[2]{0:T(128)S(1)} %pad_maximum_fusion.refs_1_, bf16[8,1536]{1,0:T(8,128)(2,1)S(1)} %shard_map.91.refs_2_, bf16[8,1536]{1,0:T(8,128)(2,1)S(1)} %collective-permute-done.9.refs_3_, bf16[8,1536]{1,0:T(8,128)(2,1)S(1)} %collective-permute-done.10.refs_4_, ...), custom_call_target="tpu_custom_call" | custom-call | flops 12582912 | bytes 196608 | tf_op jit(solution)/shard_map/pallas_call | solution.py:300
  50.9 4.4 %all-to-all-start.1 = ((bf16[16,8,384]{2,1,0:T(8,128)(2,1)}), bf16[16,8,384]{2,1,0:T(8,128)(2,1)S(1)}, u32[]{:S(2)}, u32[]{:S(2)}) async-start(bf16[16,8,384]{2,1,0:T(8,128)(2,1)} %shard_map.93), calls=%async_computation.1 | async-start | bytes 196608 | tf_op jit(solution)/shard_map/all_to_all | solution.py:249
  55.4 1.2 %collective-permute-done.12.other_ref = f32[2,1536]{1,0:T(2,128)S(1)} collective-permute-done((f32[2,1536]{1,0:T(2,128)S(1)}, f32[2,1536]{1,0:T(2,128)S(1)}, u32[]{:S(2)}, u32[]{:S(2)}) %collective-permute-start.12) | collective-permute-done | bytes 12320 | tf_op jit(solution)/shard_map/ppermute | solution.py:39
  56.5 8.1 %all-to-all-done.1.part_ref = bf16[16,8,384]{2,1,0:T(8,128)(2,1)S(1)} async-done(((bf16[16,8,384]{2,1,0:T(8,128)(2,1)}), bf16[16,8,384]{2,1,0:T(8,128)(2,1)S(1)}, u32[]{:S(2)}, u32[]{:S(2)}) %all-to-all-start.1) | async-done | bytes 98336 | tf_op jit(solution)/shard_map/all_to_all | solution.py:249
  (30 shorter events, 4.0 us)
Async XLA Ops:
  0.6 16.1 %collective-permute-start = (bf16[8,64,1536]{2,1,0:T(8,128)(2,1)}, bf16[8,64,1536]{2,1,0:T(8,128)(2,1)}, u32[]{:S(2)}, u32[]{:S(2)}) collective-permute-start(bf16[8,64,1536]{2,1,0:T(8,128)(2,1)} %refs_0_.1), channel_id=1, source_target_pairs={{0,1},{1,0},{2,3},{3,2},{4,5},{5,4},{6,7},{7,6},{8,9},{9,8},{10,11... | collective-permute-start | bytes 4718600 | tf_op jit(solution)/shard_map/ppermute | solution.py:39
  0.7 2.2 %copy-start.3 = (bf16[4,96]{1,0:T(4,128)(2,1)S(1)}, bf16[4,96]{1,0:T(4,128)(2,1)}, u32[]{:S(2)}) copy-start(bf16[4,96]{1,0:T(4,128)(2,1)} %param.9) | copy-start | bytes 2308
  2.9 3.8 %copy-start.2 = (bf16[8,1536]{1,0:T(8,128)(2,1)S(1)}, bf16[8,1536]{1,0:T(8,128)(2,1)}, u32[]{:S(2)}) copy-start(bf16[8,1536]{1,0:T(8,128)(2,1)} %captions_ref.1) | copy-start | bytes 73732
  3.4 13.3 %collective-permute-start.1 = (f32[4,1536]{1,0:T(4,128)S(1)}, f32[4,1536]{1,0:T(4,128)S(1)}, u32[]{:S(2)}, u32[]{:S(2)}) collective-permute-start(f32[4,1536]{1,0:T(4,128)S(1)} %shard_map.86.refs_2_.order_ref), channel_id=1, source_target_pairs={{0,2},{1,3},{2,0},{3,1},{4,6},{5,7},{6,4},{7,5},{8,10},{9,11},{10,... | collective-permute-start | bytes 73736 | tf_op jit(solution)/shard_map/ppermute | solution.py:39
  8.1 19.8 %all-to-all-start = ((bf16[16,4,1536]{2,1,0:T(4,128)(2,1)}), bf16[16,4,1536]{2,1,0:T(4,128)(2,1)S(1)}, u32[]{:S(2)}, u32[]{:S(2)}) async-start(bf16[16,4,1536]{2,1,0:T(4,128)(2,1)} %shard_map.89), calls=%async_computation | async-start | bytes 393216 | tf_op jit(solution)/shard_map/all_to_all | solution.py:249
  16.8 1.4 %copy-start.1 = (bf16[8,64,1536]{2,1,0:T(8,128)(2,1)S(1)}, bf16[8,64,1536]{2,1,0:T(8,128)(2,1)}, u32[]{:S(2)}) copy-start(bf16[8,64,1536]{2,1,0:T(8,128)(2,1)} %refs_0_.1) | copy-start | bytes 4718596
  21.5 11.3 %collective-permute-start.2 = (bf16[32,1664]{1,0:T(8,128)(2,1)S(1)}, bf16[32,1664]{1,0:T(8,128)(2,1)S(1)}, u32[]{:S(2)}, u32[]{:S(2)}) collective-permute-start(bf16[32,1664]{1,0:T(8,128)(2,1)S(1)} %get-tuple-element.7), channel_id=1, source_target_pairs={{0,2},{1,3},{2,0},{3,1},{4,6},{5,7},{6,4},{7,5},{8,10},{9,11},{10,... | collective-permute-start | bytes 319496 | tf_op jit(solution)/shard_map/ppermute | solution.py:39
  27.9 1.3 %copy-start = (bf16[384,1536]{1,0:T(8,128)(2,1)S(1)}, bf16[384,1536]{1,0:T(8,128)(2,1)}, u32[]{:S(2)}) copy-start(bf16[384,1536]{1,0:T(8,128)(2,1)} %final_ref.1) | copy-start | bytes 3538948
  29.2 11.4 %collective-permute-start.6 = (bf16[64,1536]{1,0:T(8,128)(2,1)S(1)}, bf16[64,1536]{1,0:T(8,128)(2,1)S(1)}, u32[]{:S(2)}, u32[]{:S(2)}) collective-permute-start(bf16[64,1536]{1,0:T(8,128)(2,1)S(1)} %shard_map.90.refs_3_.refs_6_), channel_id=1, source_target_pairs={{0,64},{4,68},{8,72},{12,76},{16,80},{20,84},{24,88},{28,92},{32,9... | collective-permute-start | bytes 589832 | tf_op jit(solution)/shard_map/ppermute | solution.py:253
  29.8 10.8 %collective-permute-start.7 = (bf16[64,1536]{1,0:T(8,128)(2,1)S(1)}, bf16[64,1536]{1,0:T(8,128)(2,1)S(1)}, u32[]{:S(2)}, u32[]{:S(2)}) collective-permute-start(bf16[64,1536]{1,0:T(8,128)(2,1)S(1)} %shard_map.90.refs_3_.refs_6_), channel_id=1, source_target_pairs={{0,128},{4,132},{8,136},{12,140},{16,144},{20,148},{24,152},{28,15... | collective-permute-start | bytes 589832 | tf_op jit(solution)/shard_map/ppermute | solution.py:253
  32.2 9.0 %collective-permute-start.8 = (bf16[64,1536]{1,0:T(8,128)(2,1)S(1)}, bf16[64,1536]{1,0:T(8,128)(2,1)S(1)}, u32[]{:S(2)}, u32[]{:S(2)}) collective-permute-start(bf16[64,1536]{1,0:T(8,128)(2,1)S(1)} %shard_map.90.refs_3_.refs_6_), channel_id=1, source_target_pairs={{0,192},{4,196},{8,200},{12,204},{16,208},{20,212},{24,216},{28,22... | collective-permute-start | bytes 589832 | tf_op jit(solution)/shard_map/ppermute | solution.py:253
  33.5 1.9 %collective-permute-start.3 = (f32[8,1536]{1,0:T(8,128)S(1)}, f32[8,1536]{1,0:T(8,128)S(1)}, u32[]{:S(2)}, u32[]{:S(2)}) collective-permute-start(f32[8,1536]{1,0:T(8,128)S(1)} %shard_map.88.e0), channel_id=1, source_target_pairs={{0,1},{1,0},{2,3},{3,2},{4,5},{5,4},{6,7},{7,6},{8,9},{9,8},{10,11... | collective-permute-start | bytes 147464 | tf_op jit(solution)/shard_map/ppermute | solution.py:39
  33.5 5.7 %collective-permute-start.4 = (f32[8,1536]{1,0:T(8,128)S(1)}, f32[8,1536]{1,0:T(8,128)S(1)}, u32[]{:S(2)}, u32[]{:S(2)}) collective-permute-start(f32[8,1536]{1,0:T(8,128)S(1)} %shard_map.88.e0), channel_id=1, source_target_pairs={{0,2},{1,3},{2,0},{3,1},{4,6},{5,7},{6,4},{7,5},{8,10},{9,11},{10,... | collective-permute-start | bytes 147464 | tf_op jit(solution)/shard_map/ppermute | solution.py:39
  35.4 5.2 %collective-permute-start.5 = (f32[8,1536]{1,0:T(8,128)S(1)}, f32[8,1536]{1,0:T(8,128)S(1)}, u32[]{:S(2)}, u32[]{:S(2)}) collective-permute-start(f32[8,1536]{1,0:T(8,128)S(1)} %shard_map.88.e0), channel_id=1, source_target_pairs={{0,3},{1,2},{2,1},{3,0},{4,7},{5,6},{6,5},{7,4},{8,11},{9,10},{10,... | collective-permute-start | bytes 147464 | tf_op jit(solution)/shard_map/ppermute | solution.py:39
  41.3 6.0 %collective-permute-start.10 = (bf16[8,1536]{1,0:T(8,128)(2,1)S(1)}, bf16[8,1536]{1,0:T(8,128)(2,1)S(1)}, u32[]{:S(2)}, u32[]{:S(2)}) collective-permute-start(bf16[8,1536]{1,0:T(8,128)(2,1)S(1)} %shard_map.91.refs_2_), channel_id=1, source_target_pairs={{0,128},{4,132},{8,136},{12,140},{16,144},{20,148},{24,152},{28,15... | collective-permute-start | bytes 73736 | tf_op jit(solution)/shard_map/ppermute | solution.py:253
  44.1 3.8 %collective-permute-start.11 = (bf16[8,1536]{1,0:T(8,128)(2,1)S(1)}, bf16[8,1536]{1,0:T(8,128)(2,1)S(1)}, u32[]{:S(2)}, u32[]{:S(2)}) collective-permute-start(bf16[8,1536]{1,0:T(8,128)(2,1)S(1)} %shard_map.91.refs_2_), channel_id=1, source_target_pairs={{0,192},{4,196},{8,200},{12,204},{16,208},{20,212},{24,216},{28,22... | collective-permute-start | bytes 73736 | tf_op jit(solution)/shard_map/ppermute | solution.py:253
  45.3 3.8 %collective-permute-start.9 = (bf16[8,1536]{1,0:T(8,128)(2,1)S(1)}, bf16[8,1536]{1,0:T(8,128)(2,1)S(1)}, u32[]{:S(2)}, u32[]{:S(2)}) collective-permute-start(bf16[8,1536]{1,0:T(8,128)(2,1)S(1)} %shard_map.91.refs_2_), channel_id=1, source_target_pairs={{0,64},{4,68},{8,72},{12,76},{16,80},{20,84},{24,88},{28,92},{32,9... | collective-permute-start | bytes 73736 | tf_op jit(solution)/shard_map/ppermute | solution.py:253
  50.9 13.7 %all-to-all-start.1 = ((bf16[16,8,384]{2,1,0:T(8,128)(2,1)}), bf16[16,8,384]{2,1,0:T(8,128)(2,1)S(1)}, u32[]{:S(2)}, u32[]{:S(2)}) async-start(bf16[16,8,384]{2,1,0:T(8,128)(2,1)} %shard_map.93), calls=%async_computation.1 | async-start | bytes 196608 | tf_op jit(solution)/shard_map/all_to_all | solution.py:249
  55.3 1.3 %collective-permute-start.12 = (f32[2,1536]{1,0:T(2,128)S(1)}, f32[2,1536]{1,0:T(2,128)S(1)}, u32[]{:S(2)}, u32[]{:S(2)}) collective-permute-start(f32[2,1536]{1,0:T(2,128)S(1)} %get-tuple-element.9), channel_id=1, source_target_pairs={{0,1},{1,0},{2,3},{3,2},{4,5},{5,4},{6,7},{7,6},{8,9},{9,8},{10,11... | collective-permute-start | bytes 36872 | tf_op jit(solution)/shard_map/ppermute | solution.py:39

commit v4 on v3

--- a/solution.py
+++ b/solution.py
@@ -17,15 +17,15 @@
 SMEM = pl.BlockSpec(memory_space=pltpu.SMEM)
 
 
-def call(kernel, outs, specs, flops, moved, scratch=(), out_specs=None):
+def call(kernel, outs, specs, flops, moved, scratch=(), limit=12):
     return pl.pallas_call(
         kernel,
         grid=(1,),
         out_shape=outs,
         in_specs=specs,
-        out_specs=out_specs or jax.tree.map(lambda _: VMEM, outs),
+        out_specs=jax.tree.map(lambda _: VMEM, outs),
         scratch_shapes=scratch,
-        compiler_params=pltpu.CompilerParams(vmem_limit_bytes=12 << 20),
+        compiler_params=pltpu.CompilerParams(vmem_limit_bytes=limit << 20),
         cost_estimate=pl.CostEstimate(flops=flops, bytes_accessed=moved, transcendentals=0),
     )
 
@@ -46,12 +46,9 @@
 
 
 def mix_kernel(own_ref, other_ref, q0, q1, m0, m1, near_ref, done, *, images):
-    half = images // 2
     copies = [
-        pltpu.make_async_copy(
-            other_ref.at[pl.ds(c * half, half)], near_ref.at[pl.ds(c * half, half)], done.at[c]
-        )
-        for c in range(2)
+        pltpu.make_async_copy(ref, near_ref.at[i], done.at[i])
+        for i, ref in enumerate((own_ref, other_ref))
     ]
     for copy in copies:
         copy.start()
@@ -69,12 +66,11 @@
     high = spread.astype(BF16)
     low = (spread - high.astype(F32)).astype(BF16)
     both = jnp.concatenate([high, low], 0)
-    own = own_ref[...].reshape(images * here, width)
-    raw = [lax.dot_general(both, own, NT, preferred_element_type=F32)]
-    for copy in copies:
+    sides, raw = [], []
+    for i, copy in enumerate(copies):
         copy.wait()
-    other = near_ref[...].reshape(images * here, width)
-    raw.append(lax.dot_general(both, other, NT, preferred_element_type=F32))
+        sides.append(near_ref[i].reshape(images * here, width))
+        raw.append(lax.dot_general(both, sides[i], NT, preferred_element_type=F32))
     raw = jnp.concatenate(raw, 1)
     scores = raw[:columns] + raw[columns:]
     row_image = lax.broadcasted_iota(jnp.int32, scores.shape, 0) % images
@@ -85,8 +81,8 @@
     total = jnp.sum(raised, 1, keepdims=True)
     weights = (raised / total).astype(BF16)
     split = images * here
-    mixed = jnp.dot(weights[:, :split], own, preferred_element_type=F32)
-    mixed = mixed + jnp.dot(weights[:, split:], other, preferred_element_type=F32)
+    mixed = jnp.dot(weights[:, :split], sides[0], preferred_element_type=F32)
+    mixed = mixed + jnp.dot(weights[:, split:], sides[1], preferred_element_type=F32)
     mixed = mixed.astype(BF16)
     log_total = top + jnp.log(total)
     high = log_total.astype(BF16).astype(F32)
@@ -101,7 +97,9 @@
         ref[:, width:] = pieces[s * step : (s + 1) * step]
 
 
-def embed_kernel(m0, m1, value_ref, final_ref, out_ref, *, heads):
+def embed_kernel(m0, m1, value_ref, final_ref, out_ref, near_ref, done, *, heads):
+    copy = pltpu.make_async_copy(final_ref, near_ref, done)
+    copy.start()
     width = value_ref.shape[0]
     parts = (m0, m1)
     logs = [jnp.sum(ref[:, width:].astype(F32), -1, keepdims=True) for ref in parts]
@@ -116,7 +114,8 @@
     column_head = lax.broadcasted_iota(jnp.int32, pooled.shape, 1) // (columns // heads)
     kept = jnp.where(row_head == column_head, pooled, 0.0)
     pooled = sum(kept[h * images : (h + 1) * images] for h in range(heads))
-    out_ref[...] = jnp.dot(pooled.astype(BF16), final_ref[...], preferred_element_type=F32)
+    copy.wait()
+    out_ref[...] = jnp.dot(pooled.astype(BF16), near_ref[...], preferred_element_type=F32)
 
 
 def text_kernel(place_ref, captions_ref, order_ref, out_ref):
@@ -128,7 +127,7 @@
     out_ref[...] = jnp.broadcast_to(chosen[None], out_ref.shape)
 
 
-def rows_kernel(text_ref, order_ref, final_ref, rows_ref):
+def rows_kernel(text_ref, order_ref, rows_ref):
     texts = text_ref[...].astype(F32)
     rows_ref[...] = jnp.concatenate([texts[i] for i in range(texts.shape[0])], 0).astype(BF16)
 
@@ -262,21 +261,24 @@
     mixes = call(
         lambda *refs: mix_kernel(*refs, images=images),
         [bf16(heads * images, width + 128)] * 2,
-        [VMEM, ANY, VMEM, VMEM],
+        [ANY, ANY, VMEM, VMEM],
         64 << 30,
         6 * images * here * width,
-        [pltpu.VMEM(tokens.shape, BF16), pltpu.SemaphoreType.DMA((2,))],
+        [pltpu.VMEM((2, *tokens.shape), BF16), pltpu.SemaphoreType.DMA((2,))],
+        53,
     )(tokens, other_tokens, key_query, peer(key_query, 2))
     texts = call(
-        rows_kernel, bf16(near * 4, width), [VMEM, ANY, ANY], near * 4 * width, 16 * near * width
-    )(copies, mixes[0], final)
+        rows_kernel, bf16(near * 4, width), [VMEM, ANY], near * 4 * width, 16 * near * width
+    )(copies, mixes[0])
     all_texts = across([texts] * 4)
     embeds = call(
         lambda *refs: embed_kernel(*refs, heads=heads),
         f32(images, width),
-        [VMEM, VMEM, value_spec, VMEM],
+        [VMEM, VMEM, value_spec, ANY],
         64 << 30,
         4 * width * columns,
+        [pltpu.VMEM(final.shape, BF16), pltpu.SemaphoreType.DMA],
+        52,
     )(mixes[0], peer(mixes[1], 2), both, final)
     embeds = [embeds] + [peer(embeds, s) for s in (1, 2, 3)]
 
@@ -303,7 +305,7 @@
         [SMEM, SMEM] + [VMEM] * 5 + [ANY],
         2 * 256 * near * width,
         8 * near * width,
-    )(place, scalars, *units, texts, own_part)
+    )(place, scalars, *units, texts, other_part)
     received = swap(text_part)
     image_grad, text_grad = call(
         sum_kernel, [f32(share, width)] * 2, [VMEM] * 3, near * share * width, 2 * near * share * width

time: 65.6 us -> 63 us (0.960)
  blocking collectives: 0 us -> 12.4 us
  waiting for transfers between devices: 18.6 us -> 9.24 us
  starting transfers between devices: 30.1 us -> 25.8 us
  local copies, waits for them, and re-layouts: 4.92 us -> 2.25 us
  Pallas kernels: 9.41 us -> 10.6 us
    all_to_all x0 -> x1, blocking collectives: none -> 12.4 us  [swap(): lax.all_to_all(pieces, 'dp', 0, 0, axis_index_groups=groups, tiled=False)]
    all_to_all x2 -> x1, waiting for transfers between devices: 12.5 us -> 5.57 us  [swap(): lax.all_to_all(pieces, 'dp', 0, 0, axis_index_groups=groups, tiled=False)]
    all_to_all x2 -> x1, starting transfers between devices: 13 us -> 8.68 us  [swap(): lax.all_to_all(pieces, 'dp', 0, 0, axis_index_groups=groups, tiled=False)]
    unnamed x9, local copies, waits for them, and re-layouts: 4.83 us -> 2.16 us
    ppermute x6, waiting for transfers between devices: 2.45 us -> 0.02 us  [across(): lax.ppermute(pieces[s], 'dp', [(i, i ^ s * near) for i in range(n_dp)])]
    pallas_call x1, Pallas kernels: 0.68 us -> 2.24 us  [per_device(): call(lambda *refs: embed_kernel(*refs, heads=heads), f32(images, width),...]
  transfers between devices with their start and end apart: 15 -> 14, of which waited for: 8 -> 4; matrix products, arithmetic and copies ran while one was open for 4% -> 4% of each run, Pallas kernels for 11% -> 14%
where the time goes in v4:
time: 63 us; the launch traced here: 62.5 us
  starting transfers between devices  25.8 us (41%)
  blocking collectives  12.4 us (20%)
  Pallas kernels  10.6 us (17%)
  waiting for transfers between devices  9.24 us (15%)
  local copies, waits for them, and re-layouts  2.25 us (4%)
  between operations  2.09 us (3%)
    all_to_all x1, blocking collectives, swap(): lax.all_to_all(pieces, 'dp', 0, 0, axis_index_groups=groups, tiled=False)  12.4 us
    ppermute x7, starting transfers between devices, peer(): return lax.ppermute(piece, 'head', [(i, i ^ step) for i in range(4)])  8.79 us
    all_to_all x1, starting transfers between devices, swap(): lax.all_to_all(pieces, 'dp', 0, 0, axis_index_groups=groups, tiled=False)  8.68 us
    ppermute x6, starting transfers between devices, across(): lax.ppermute(pieces[s], 'dp', [(i, i ^ s * near) for i in range(n_dp)])  8.29 us
    all_to_all x1, waiting for transfers between devices, swap(): lax.all_to_all(pieces, 'dp', 0, 0, axis_index_groups=groups, tiled=False)  5.57 us
    ppermute x7, waiting for transfers between devices, peer(): return lax.ppermute(piece, 'head', [(i, i ^ step) for i in range(4)])  3.65 us
    pallas_call x1, Pallas kernels, per_device(): call(lambda *refs: mix_kernel(*refs, images=images), [bf16(heads * images...  3.58 us
    pallas_call x1, Pallas kernels, per_device(): call(lambda *refs: embed_kernel(*refs, heads=heads), f32(images, width),...  2.24 us
  transfers between devices with their start and end apart: 14, of which 4 were waited for; matrix products, arithmetic and copies ran while one was open for 4% of the time, Pallas kernels for 14%

profile of v4, /device:TPU:2, one launch (start us, length us, event | category | flops | bytes accessed | tf_op | source)
XLA Modules:
  0.0 62.5 jit_solution(8251007455196203138)
XLA Ops:
  0.7 2.1 %copy.9 = bf16[192,8,2,384]{3,1,2,0:T(8,128)(2,1)S(1)} copy(bf16[192,8,2,384]{3,2,1,0:T(2,128)(2,1)} %bitcast.10) | data formatting | bytes 4718592
  3.0 0.4 shard_map.86.refs_2_.order_ref
  3.5 3.2 %collective-permute-start.1 = (f32[4,1536]{1,0:T(4,128)S(1)}, f32[4,1536]{1,0:T(4,128)S(1)}, u32[]{:S(2)}, u32[]{:S(2)}) collective-permute-start(f32[4,1536]{1,0:T(4,128)S(1)} %shard_map.86.refs_2_.order_ref), channel_id=1, source_target_pairs={{0,2},{1,3},{2,0},{3,1},{4,6},{5,7},{6,4},{7,5},{8,10},{9,11},{10,... | collective-permute-start | bytes 73736 | tf_op jit(solution)/shard_map/ppermute | solution.py:39
  6.7 1.3 %shard_map.89 = bf16[16,4,1536]{2,1,0:T(4,128)(2,1)} custom-call(s32[2]{0:T(128)S(1)} %pad_add_fusion.place_ref.refs_0_, bf16[8,1536]{1,0:T(8,128)(2,1)S(1)} %copy-done.2, f32[4,1536]{1,0:T(4,128)S(1)} %shard_map.86.refs_2_.order_ref), custom_call_target="tpu_custom_call" | custom-call | flops 6442450944 | bytes 786432 | tf_op jit(solution)/shard_map/pallas_call | solution.py:256
  8.1 8.7 %all-to-all-start = ((bf16[16,4,1536]{2,1,0:T(4,128)(2,1)}), bf16[16,4,1536]{2,1,0:T(4,128)(2,1)S(1)}, u32[]{:S(2)}, u32[]{:S(2)}) async-start(bf16[16,4,1536]{2,1,0:T(4,128)(2,1)} %shard_map.89), calls=%async_computation | async-start | bytes 393216 | tf_op jit(solution)/shard_map/all_to_all | solution.py:248
  16.8 3.6 %shard_map.87 = (bf16[32,1664]{1,0:T(8,128)(2,1)S(1)}, bf16[32,1664]{1,0:T(8,128)(2,1)S(1)}) custom-call(bf16[8,64,1536]{2,1,0:T(8,128)(2,1)} %refs_0_.1, bf16[8,64,1536]{2,1,0:T(8,128)(2,1)} %collective-permute-done.refs_1_, f32[4,1536]{1,0:T(4,128)S(1)} %shard_map.86.refs_2_.order_ref, f32[4,1536]{1,0:T(4,128)S(1)} %collective-permute-done.1.refs_3_), custom_call_target="tpu_custom_call" | custom-call | flops 68719476736 | bytes 4718592 | tf_op jit(solution)/shard_map/pallas_call | solution.py:261
  20.4 1.9 %collective-permute-start.2 = (bf16[32,1664]{1,0:T(8,128)(2,1)S(1)}, bf16[32,1664]{1,0:T(8,128)(2,1)S(1)}, u32[]{:S(2)}, u32[]{:S(2)}) collective-permute-start(bf16[32,1664]{1,0:T(8,128)(2,1)S(1)} %get-tuple-element.7), channel_id=1, source_target_pairs={{0,2},{1,3},{2,0},{3,1},{4,6},{5,7},{6,4},{7,5},{8,10},{9,11},{10,... | collective-permute-start | bytes 319496 | tf_op jit(solution)/shard_map/ppermute | solution.py:39
  22.3 5.6 %all-to-all-done.text_ref = bf16[16,4,1536]{2,1,0:T(4,128)(2,1)S(1)} async-done(((bf16[16,4,1536]{2,1,0:T(4,128)(2,1)}), bf16[16,4,1536]{2,1,0:T(4,128)(2,1)S(1)}, u32[]{:S(2)}, u32[]{:S(2)}) %all-to-all-start) | async-done | bytes 196640 | tf_op jit(solution)/shard_map/all_to_all | solution.py:248
  27.9 0.6 collective-permute-start.6
  28.6 2.4 %collective-permute-start.7 = (bf16[64,1536]{1,0:T(8,128)(2,1)S(1)}, bf16[64,1536]{1,0:T(8,128)(2,1)S(1)}, u32[]{:S(2)}, u32[]{:S(2)}) collective-permute-start(bf16[64,1536]{1,0:T(8,128)(2,1)S(1)} %shard_map.90.refs_3_.refs_6_), channel_id=1, source_target_pairs={{0,128},{4,132},{8,136},{12,140},{16,144},{20,148},{24,152},{28,15... | collective-permute-start | bytes 589832 | tf_op jit(solution)/shard_map/ppermute | solution.py:252
  31.0 0.5 collective-permute-start.8
  31.5 2.2 %shard_map.88.e0 = f32[8,1536]{1,0:T(8,128)S(1)} custom-call(bf16[32,1664]{1,0:T(8,128)(2,1)S(1)} %get-tuple-element.6.refs_0_.order_ref, bf16[32,1664]{1,0:T(8,128)(2,1)S(1)} %collective-permute-done.2.refs_1_, bf16[1536,768]{1,0:T(8,128)(2,1)} %bitcast.9, bf16[384,1536]{1,0:T(8,128)(2,1)S(1)} %copy-done.1), custom_call_target="tpu_custom_call" | custom-call | flops 68719476736 | bytes 2359296 | tf_op jit(solution)/shard_map/pallas_call | solution.py:274
  33.9 1.9 %collective-permute-start.4 = (f32[8,1536]{1,0:T(8,128)S(1)}, f32[8,1536]{1,0:T(8,128)S(1)}, u32[]{:S(2)}, u32[]{:S(2)}) collective-permute-start(f32[8,1536]{1,0:T(8,128)S(1)} %shard_map.88.e0), channel_id=1, source_target_pairs={{0,2},{1,3},{2,0},{3,1},{4,6},{5,7},{6,4},{7,5},{8,10},{9,11},{10,... | collective-permute-start | bytes 147464 | tf_op jit(solution)/shard_map/ppermute | solution.py:39
  35.8 1.4 %collective-permute-start.5 = (f32[8,1536]{1,0:T(8,128)S(1)}, f32[8,1536]{1,0:T(8,128)S(1)}, u32[]{:S(2)}, u32[]{:S(2)}) collective-permute-start(f32[8,1536]{1,0:T(8,128)S(1)} %shard_map.88.e0), channel_id=1, source_target_pairs={{0,3},{1,2},{2,1},{3,0},{4,7},{5,6},{6,5},{7,4},{8,11},{9,10},{10,... | collective-permute-start | bytes 147464 | tf_op jit(solution)/shard_map/ppermute | solution.py:39
  38.5 1.0 %collective-permute-done.4.e2 = f32[8,1536]{1,0:T(8,128)S(1)} collective-permute-done((f32[8,1536]{1,0:T(8,128)S(1)}, f32[8,1536]{1,0:T(8,128)S(1)}, u32[]{:S(2)}, u32[]{:S(2)}) %collective-permute-start.4) | collective-permute-done | bytes 49184 | tf_op jit(solution)/shard_map/ppermute | solution.py:39
  39.6 1.5 %collective-permute-done.5.e3 = f32[8,1536]{1,0:T(8,128)S(1)} collective-permute-done((f32[8,1536]{1,0:T(8,128)S(1)}, f32[8,1536]{1,0:T(8,128)S(1)}, u32[]{:S(2)}, u32[]{:S(2)}) %collective-permute-start.5) | collective-permute-done | bytes 49184 | tf_op jit(solution)/shard_map/ppermute | solution.py:39
  41.0 0.1 shard_map.91.refs_2_
  41.1 3.3 %collective-permute-start.10 = (bf16[8,1536]{1,0:T(8,128)(2,1)S(1)}, bf16[8,1536]{1,0:T(8,128)(2,1)S(1)}, u32[]{:S(2)}, u32[]{:S(2)}) collective-permute-start(bf16[8,1536]{1,0:T(8,128)(2,1)S(1)} %shard_map.91.refs_2_), channel_id=1, source_target_pairs={{0,128},{4,132},{8,136},{12,140},{16,144},{20,148},{24,152},{28,15... | collective-permute-start | bytes 73736 | tf_op jit(solution)/shard_map/ppermute | solution.py:252
  44.5 1.4 %collective-permute-start.9 = (bf16[8,1536]{1,0:T(8,128)(2,1)S(1)}, bf16[8,1536]{1,0:T(8,128)(2,1)S(1)}, u32[]{:S(2)}, u32[]{:S(2)}) collective-permute-start(bf16[8,1536]{1,0:T(8,128)(2,1)S(1)} %shard_map.91.refs_2_), channel_id=1, source_target_pairs={{0,64},{4,68},{8,72},{12,76},{16,80},{20,84},{24,88},{28,92},{32,9... | collective-permute-start | bytes 73736 | tf_op jit(solution)/shard_map/ppermute | solution.py:252
  45.9 1.2 %shard_map.92 = (f32[2,1536]{1,0:T(2,128)S(1)}, f32[2,1536]{1,0:T(2,128)S(1)}) custom-call(s32[2]{0:T(128)S(1)} %pad_add_fusion.place_ref.refs_0_, f32[2]{0:T(128)S(1)} %pad_maximum_fusion.refs_1_, bf16[8,1536]{1,0:T(8,128)(2,1)S(1)} %shard_map.91.refs_2_, bf16[64,1536]{1,0:T(8,128)(2,1)S(1)} %shard_map.90.refs_3_.refs_6_, ...), custom_call_target="tpu_custom_call" | custom-call | flops 12582912 | bytes 1572864 | tf_op jit(solution)/shard_map/pallas_call | solution.py:294
  47.2 1.2 %collective-permute-done.12.refs_7_.other_ref = f32[2,1536]{1,0:T(2,128)S(1)} collective-permute-done((f32[2,1536]{1,0:T(2,128)S(1)}, f32[2,1536]{1,0:T(2,128)S(1)}, u32[]{:S(2)}, u32[]{:S(2)}) %collective-permute-start.12) | collective-permute-done | bytes 12320 | tf_op jit(solution)/shard_map/ppermute | solution.py:39
  48.4 1.1 %shard_map.93 = bf16[16,8,384]{2,1,0:T(8,128)(2,1)S(1)} custom-call(s32[2]{0:T(128)S(1)} %pad_add_fusion.place_ref.refs_0_, f32[2]{0:T(128)S(1)} %pad_maximum_fusion.refs_1_, bf16[8,1536]{1,0:T(8,128)(2,1)S(1)} %shard_map.91.refs_2_, bf16[8,1536]{1,0:T(8,128)(2,1)S(1)} %collective-permute-done.9.refs_3_, ...), custom_call_target="tpu_custom_call" | custom-call | flops 12582912 | bytes 196608 | tf_op jit(solution)/shard_map/pallas_call | solution.py:302
  49.5 12.4 %all_to_all.10.part_ref = bf16[16,8,384]{2,1,0:T(8,128)(2,1)S(1)} all-to-all(bf16[16,8,384]{2,1,0:T(8,128)(2,1)S(1)} %shard_map.93), channel_id=1, replica_groups={{0,4,8,12,16,20,24,28,32,36,40,44,48,52,56,60},{64,68,72,76,80,84,88,92..., dimensions={0} | all-to-all | bytes 196608 | tf_op jit(solution)/shard_map/all_to_all | solution.py:248
  61.9 0.6 %shard_map.94 = (f32[2,1536]{1,0:T(2,128)}, f32[2,1536]{1,0:T(2,128)}) custom-call(bf16[16,8,384]{2,1,0:T(8,128)(2,1)S(1)} %all_to_all.10.part_ref, f32[2,1536]{1,0:T(2,128)S(1)} %get-tuple-element.9.own_ref, f32[2,1536]{1,0:T(2,128)S(1)} %collective-permute-done.12.refs_7_.other_ref), custom_call_target="tpu_custom_call" | custom-call | flops 49152 | bytes 98304 | tf_op jit(solution)/shard_map/pallas_call | solution.py:310
  (29 shorter events, 0.6 us)
Async XLA Ops:
  0.6 16.2 %collective-permute-start = (bf16[8,64,1536]{2,1,0:T(8,128)(2,1)}, bf16[8,64,1536]{2,1,0:T(8,128)(2,1)}, u32[]{:S(2)}, u32[]{:S(2)}) collective-permute-start(bf16[8,64,1536]{2,1,0:T(8,128)(2,1)} %refs_0_.1), channel_id=1, source_target_pairs={{0,1},{1,0},{2,3},{3,2},{4,5},{5,4},{6,7},{7,6},{8,9},{9,8},{10,11... | collective-permute-start | bytes 4718600 | tf_op jit(solution)/shard_map/ppermute | solution.py:39
  0.7 2.2 %copy-start.3 = (bf16[4,96]{1,0:T(4,128)(2,1)S(1)}, bf16[4,96]{1,0:T(4,128)(2,1)}, u32[]{:S(2)}) copy-start(bf16[4,96]{1,0:T(4,128)(2,1)} %param.9) | copy-start | bytes 2308
  2.9 5.2 %copy-start = (bf16[192,8,2,384]{3,1,2,0:T(8,128)(2,1)}, bf16[192,8,2,384]{3,1,2,0:T(8,128)(2,1)S(1)}, u32[]{:S(2)}) copy-start(bf16[192,8,2,384]{3,1,2,0:T(8,128)(2,1)S(1)} %copy.9) | copy-start | bytes 7077892
  2.9 3.8 %copy-start.2 = (bf16[8,1536]{1,0:T(8,128)(2,1)S(1)}, bf16[8,1536]{1,0:T(8,128)(2,1)}, u32[]{:S(2)}) copy-start(bf16[8,1536]{1,0:T(8,128)(2,1)} %captions_ref.1) | copy-start | bytes 73732
  3.5 13.3 %collective-permute-start.1 = (f32[4,1536]{1,0:T(4,128)S(1)}, f32[4,1536]{1,0:T(4,128)S(1)}, u32[]{:S(2)}, u32[]{:S(2)}) collective-permute-start(f32[4,1536]{1,0:T(4,128)S(1)} %shard_map.86.refs_2_.order_ref), channel_id=1, source_target_pairs={{0,2},{1,3},{2,0},{3,1},{4,6},{5,7},{6,4},{7,5},{8,10},{9,11},{10,... | collective-permute-start | bytes 73736 | tf_op jit(solution)/shard_map/ppermute | solution.py:39
  8.1 19.8 %all-to-all-start = ((bf16[16,4,1536]{2,1,0:T(4,128)(2,1)}), bf16[16,4,1536]{2,1,0:T(4,128)(2,1)S(1)}, u32[]{:S(2)}, u32[]{:S(2)}) async-start(bf16[16,4,1536]{2,1,0:T(4,128)(2,1)} %shard_map.89), calls=%async_computation | async-start | bytes 393216 | tf_op jit(solution)/shard_map/all_to_all | solution.py:248
  16.8 14.8 %copy-start.1 = (bf16[384,1536]{1,0:T(8,128)(2,1)S(1)}, bf16[384,1536]{1,0:T(8,128)(2,1)}, u32[]{:S(2)}) copy-start(bf16[384,1536]{1,0:T(8,128)(2,1)} %refs_3_.1) | copy-start | bytes 3538948
  20.4 11.1 %collective-permute-start.2 = (bf16[32,1664]{1,0:T(8,128)(2,1)S(1)}, bf16[32,1664]{1,0:T(8,128)(2,1)S(1)}, u32[]{:S(2)}, u32[]{:S(2)}) collective-permute-start(bf16[32,1664]{1,0:T(8,128)(2,1)S(1)} %get-tuple-element.7), channel_id=1, source_target_pairs={{0,2},{1,3},{2,0},{3,1},{4,6},{5,7},{6,4},{7,5},{8,10},{9,11},{10,... | collective-permute-start | bytes 319496 | tf_op jit(solution)/shard_map/ppermute | solution.py:39
  27.9 13.1 %collective-permute-start.6 = (bf16[64,1536]{1,0:T(8,128)(2,1)S(1)}, bf16[64,1536]{1,0:T(8,128)(2,1)S(1)}, u32[]{:S(2)}, u32[]{:S(2)}) collective-permute-start(bf16[64,1536]{1,0:T(8,128)(2,1)S(1)} %shard_map.90.refs_3_.refs_6_), channel_id=1, source_target_pairs={{0,64},{4,68},{8,72},{12,76},{16,80},{20,84},{24,88},{28,92},{32,9... | collective-permute-start | bytes 589832 | tf_op jit(solution)/shard_map/ppermute | solution.py:252
  28.6 12.5 %collective-permute-start.7 = (bf16[64,1536]{1,0:T(8,128)(2,1)S(1)}, bf16[64,1536]{1,0:T(8,128)(2,1)S(1)}, u32[]{:S(2)}, u32[]{:S(2)}) collective-permute-start(bf16[64,1536]{1,0:T(8,128)(2,1)S(1)} %shard_map.90.refs_3_.refs_6_), channel_id=1, source_target_pairs={{0,128},{4,132},{8,136},{12,140},{16,144},{20,148},{24,152},{28,15... | collective-permute-start | bytes 589832 | tf_op jit(solution)/shard_map/ppermute | solution.py:252
  31.0 10.0 %collective-permute-start.8 = (bf16[64,1536]{1,0:T(8,128)(2,1)S(1)}, bf16[64,1536]{1,0:T(8,128)(2,1)S(1)}, u32[]{:S(2)}, u32[]{:S(2)}) collective-permute-start(bf16[64,1536]{1,0:T(8,128)(2,1)S(1)} %shard_map.90.refs_3_.refs_6_), channel_id=1, source_target_pairs={{0,192},{4,196},{8,200},{12,204},{16,208},{20,212},{24,216},{28,22... | collective-permute-start | bytes 589832 | tf_op jit(solution)/shard_map/ppermute | solution.py:252
  33.8 2.0 %collective-permute-start.3 = (f32[8,1536]{1,0:T(8,128)S(1)}, f32[8,1536]{1,0:T(8,128)S(1)}, u32[]{:S(2)}, u32[]{:S(2)}) collective-permute-start(f32[8,1536]{1,0:T(8,128)S(1)} %shard_map.88.e0), channel_id=1, source_target_pairs={{0,1},{1,0},{2,3},{3,2},{4,5},{5,4},{6,7},{7,6},{8,9},{9,8},{10,11... | collective-permute-start | bytes 147464 | tf_op jit(solution)/shard_map/ppermute | solution.py:39
  33.9 5.7 %collective-permute-start.4 = (f32[8,1536]{1,0:T(8,128)S(1)}, f32[8,1536]{1,0:T(8,128)S(1)}, u32[]{:S(2)}, u32[]{:S(2)}) collective-permute-start(f32[8,1536]{1,0:T(8,128)S(1)} %shard_map.88.e0), channel_id=1, source_target_pairs={{0,2},{1,3},{2,0},{3,1},{4,6},{5,7},{6,4},{7,5},{8,10},{9,11},{10,... | collective-permute-start | bytes 147464 | tf_op jit(solution)/shard_map/ppermute | solution.py:39
  35.8 5.2 %collective-permute-start.5 = (f32[8,1536]{1,0:T(8,128)S(1)}, f32[8,1536]{1,0:T(8,128)S(1)}, u32[]{:S(2)}, u32[]{:S(2)}) collective-permute-start(f32[8,1536]{1,0:T(8,128)S(1)} %shard_map.88.e0), channel_id=1, source_target_pairs={{0,3},{1,2},{2,1},{3,0},{4,7},{5,6},{6,5},{7,4},{8,11},{9,10},{10,... | collective-permute-start | bytes 147464 | tf_op jit(solution)/shard_map/ppermute | solution.py:39
  41.1 7.2 %collective-permute-start.10 = (bf16[8,1536]{1,0:T(8,128)(2,1)S(1)}, bf16[8,1536]{1,0:T(8,128)(2,1)S(1)}, u32[]{:S(2)}, u32[]{:S(2)}) collective-permute-start(bf16[8,1536]{1,0:T(8,128)(2,1)S(1)} %shard_map.91.refs_2_), channel_id=1, source_target_pairs={{0,128},{4,132},{8,136},{12,140},{16,144},{20,148},{24,152},{28,15... | collective-permute-start | bytes 73736 | tf_op jit(solution)/shard_map/ppermute | solution.py:252
  44.5 3.9 %collective-permute-start.11 = (bf16[8,1536]{1,0:T(8,128)(2,1)S(1)}, bf16[8,1536]{1,0:T(8,128)(2,1)S(1)}, u32[]{:S(2)}, u32[]{:S(2)}) collective-permute-start(bf16[8,1536]{1,0:T(8,128)(2,1)S(1)} %shard_map.91.refs_2_), channel_id=1, source_target_pairs={{0,192},{4,196},{8,200},{12,204},{16,208},{20,212},{24,216},{28,22... | collective-permute-start | bytes 73736 | tf_op jit(solution)/shard_map/ppermute | solution.py:252
  44.5 3.9 %collective-permute-start.9 = (bf16[8,1536]{1,0:T(8,128)(2,1)S(1)}, bf16[8,1536]{1,0:T(8,128)(2,1)S(1)}, u32[]{:S(2)}, u32[]{:S(2)}) collective-permute-start(bf16[8,1536]{1,0:T(8,128)(2,1)S(1)} %shard_map.91.refs_2_), channel_id=1, source_target_pairs={{0,64},{4,68},{8,72},{12,76},{16,80},{20,84},{24,88},{28,92},{32,9... | collective-permute-start | bytes 73736 | tf_op jit(solution)/shard_map/ppermute | solution.py:252
  47.1 1.3 %collective-permute-start.12 = (f32[2,1536]{1,0:T(2,128)S(1)}, f32[2,1536]{1,0:T(2,128)S(1)}, u32[]{:S(2)}, u32[]{:S(2)}) collective-permute-start(f32[2,1536]{1,0:T(2,128)S(1)} %get-tuple-element.8), channel_id=1, source_target_pairs={{0,1},{1,0},{2,3},{3,2},{4,5},{5,4},{6,7},{7,6},{8,9},{9,8},{10,11... | collective-permute-start | bytes 36872 | tf_op jit(solution)/shard_map/ppermute | solution.py:39

commit v5 on v4

--- a/solution.py
+++ b/solution.py
@@ -97,9 +97,7 @@
         ref[:, width:] = pieces[s * step : (s + 1) * step]
 
 
-def embed_kernel(m0, m1, value_ref, final_ref, out_ref, near_ref, done, *, heads):
-    copy = pltpu.make_async_copy(final_ref, near_ref, done)
-    copy.start()
+def embed_kernel(m0, m1, value_ref, final_ref, out_ref, *, heads):
     width = value_ref.shape[0]
     parts = (m0, m1)
     logs = [jnp.sum(ref[:, width:].astype(F32), -1, keepdims=True) for ref in parts]
@@ -114,8 +112,7 @@
     column_head = lax.broadcasted_iota(jnp.int32, pooled.shape, 1) // (columns // heads)
     kept = jnp.where(row_head == column_head, pooled, 0.0)
     pooled = sum(kept[h * images : (h + 1) * images] for h in range(heads))
-    copy.wait()
-    out_ref[...] = jnp.dot(pooled.astype(BF16), near_ref[...], preferred_element_type=F32)
+    out_ref[...] = jnp.dot(pooled.astype(BF16), final_ref[...], preferred_element_type=F32)
 
 
 def text_kernel(place_ref, captions_ref, order_ref, out_ref):
@@ -134,7 +131,8 @@
 
 def text_ids(shape, first_dp, images, head):
     column = lax.broadcasted_iota(jnp.int32, shape, 1)
-    return (first_dp + column // 4) * images + column % 4 // 2 * 4 + head % 2 * 2 + column % 2
+    local = column // 4 * 7 % 16
+    return (first_dp + local) * images + column % 4 // 2 * 4 + head % 2 * 2 + column % 2
 
 
 def unit_kernel(e0, e1, e2, e3, order1, order2, order3, unit_ref):
@@ -186,7 +184,7 @@
     image_id = dp * images + lax.broadcasted_iota(jnp.int32, logits.shape, 0)
     column = lax.broadcasted_iota(jnp.int32, logits.shape, 1)
     first_dp = ((column // count) ^ block) * near
-    text_id = (first_dp + column % count // 4) * images
+    text_id = (first_dp + column % count // 4 * 7 % near) * images
     text_id = text_id + column % 4 // 2 * 4 + head % 2 * 2 + column % 2
     matched = jnp.where(image_id == text_id, 1.0, 0.0)
     coefficient = (multiplier * (jax.nn.sigmoid(logits) - matched)).astype(BF16)
@@ -242,7 +240,7 @@
     )(spread, both)
 
     place = jnp.stack([dp, head]).astype(jnp.int32)
-    groups = [[b * near + i for i in range(near)] for b in range(4)]
+    groups = [[b * near + i * 7 % near for i in range(near)] for b in range(4)]
 
     def swap(pieces):
         return lax.all_to_all(pieces, "dp", 0, 0, axis_index_groups=groups, tiled=False)
@@ -274,11 +272,9 @@
     embeds = call(
         lambda *refs: embed_kernel(*refs, heads=heads),
         f32(images, width),
-        [VMEM, VMEM, value_spec, ANY],
+        [VMEM, VMEM, value_spec, VMEM],
         64 << 30,
         4 * width * columns,
-        [pltpu.VMEM(final.shape, BF16), pltpu.SemaphoreType.DMA],
-        52,
     )(mixes[0], peer(mixes[1], 2), both, final)
     embeds = [embeds] + [peer(embeds, s) for s in (1, 2, 3)]
 

time: 63 us -> 62.8 us (level)
  Pallas kernels: 10.6 us -> 8.97 us
  local copies, waits for them, and re-layouts: 2.25 us -> 3.51 us
  blocking collectives: 12.4 us -> 13.1 us
    pallas_call x1, Pallas kernels: 2.24 us -> 0.68 us  [per_device(): call(lambda *refs: embed_kernel(*refs, heads=heads), f32(images, width),...]
    unnamed x9 -> x7, local copies, waits for them, and re-layouts: 2.16 us -> 3.42 us
    all_to_all x1, blocking collectives: 12.4 us -> 13.1 us  [swap(): lax.all_to_all(pieces, 'dp', 0, 0, axis_index_groups=groups, tiled=False)]
  transfers between devices with their start and end apart: 14 -> 14, of which waited for: 4 -> 4; matrix products, arithmetic and copies ran while one was open for 4% -> 4% of each run, Pallas kernels for 14% -> 11%
where the time goes in v5:
time: 62.8 us; the launch traced here: 62.5 us
  starting transfers between devices  25.7 us (41%)
  blocking collectives  13.1 us (21%)
  Pallas kernels  8.97 us (14%)
  waiting for transfers between devices  8.97 us (14%)
  local copies, waits for them, and re-layouts  3.51 us (6%)
  between operations  2.07 us (3%)
    all_to_all x1, blocking collectives, swap(): lax.all_to_all(pieces, 'dp', 0, 0, axis_index_groups=groups, tiled=False)  13.1 us
    ppermute x7, starting transfers between devices, peer(): return lax.ppermute(piece, 'head', [(i, i ^ step) for i in range(4)])  8.73 us
    all_to_all x1, starting transfers between devices, swap(): lax.all_to_all(pieces, 'dp', 0, 0, axis_index_groups=groups, tiled=False)  8.68 us
    ppermute x6, starting transfers between devices, across(): lax.ppermute(pieces[s], 'dp', [(i, i ^ s * near) for i in range(n_dp)])  8.29 us
    all_to_all x1, waiting for transfers between devices, swap(): lax.all_to_all(pieces, 'dp', 0, 0, axis_index_groups=groups, tiled=False)  5.28 us
    ppermute x7, waiting for transfers between devices, peer(): return lax.ppermute(piece, 'head', [(i, i ^ step) for i in range(4)])  3.67 us
    pallas_call x1, Pallas kernels, per_device(): call(lambda *refs: mix_kernel(*refs, images=images), [bf16(heads * images...  3.48 us
    unnamed x7, local copies, waits for them, and re-layouts  3.42 us
  transfers between devices with their start and end apart: 14, of which 4 were waited for; matrix products, arithmetic and copies ran while one was open for 4% of the time, Pallas kernels for 11%

profile of v5, /device:TPU:2, one launch (start us, length us, event | category | flops | bytes accessed | tf_op | source)
XLA Modules:
  0.0 62.5 jit_solution(1509780086605415783)
XLA Ops:
  0.7 2.1 %copy.9 = bf16[192,8,2,384]{3,1,2,0:T(8,128)(2,1)S(1)} copy(bf16[192,8,2,384]{3,2,1,0:T(2,128)(2,1)} %bitcast.10) | data formatting | bytes 4718592
  3.0 0.4 shard_map.86.refs_2_.order_ref
  3.4 3.2 %collective-permute-start.1 = (f32[4,1536]{1,0:T(4,128)S(1)}, f32[4,1536]{1,0:T(4,128)S(1)}, u32[]{:S(2)}, u32[]{:S(2)}) collective-permute-start(f32[4,1536]{1,0:T(4,128)S(1)} %shard_map.86.refs_2_.order_ref), channel_id=1, source_target_pairs={{0,2},{1,3},{2,0},{3,1},{4,6},{5,7},{6,4},{7,5},{8,10},{9,11},{10,... | collective-permute-start | bytes 73736 | tf_op jit(solution)/shard_map/ppermute | solution.py:39
  6.7 1.3 %shard_map.89 = bf16[16,4,1536]{2,1,0:T(4,128)(2,1)} custom-call(s32[2]{0:T(128)S(1)} %pad_add_fusion.place_ref.refs_0_, bf16[8,1536]{1,0:T(8,128)(2,1)S(1)} %copy-done.1, f32[4,1536]{1,0:T(4,128)S(1)} %shard_map.86.refs_2_.order_ref), custom_call_target="tpu_custom_call" | custom-call | flops 6442450944 | bytes 786432 | tf_op jit(solution)/shard_map/pallas_call | solution.py:254
  8.1 8.7 %all-to-all-start = ((bf16[16,4,1536]{2,1,0:T(4,128)(2,1)}), bf16[16,4,1536]{2,1,0:T(4,128)(2,1)S(1)}, u32[]{:S(2)}, u32[]{:S(2)}) async-start(bf16[16,4,1536]{2,1,0:T(4,128)(2,1)} %shard_map.89), calls=%async_computation | async-start | bytes 393216 | tf_op jit(solution)/shard_map/all_to_all | solution.py:246
  16.8 3.5 %shard_map.87 = (bf16[32,1664]{1,0:T(8,128)(2,1)S(1)}, bf16[32,1664]{1,0:T(8,128)(2,1)S(1)}) custom-call(bf16[8,64,1536]{2,1,0:T(8,128)(2,1)} %refs_0_.1, bf16[8,64,1536]{2,1,0:T(8,128)(2,1)} %collective-permute-done.refs_1_, f32[4,1536]{1,0:T(4,128)S(1)} %shard_map.86.refs_2_.order_ref, f32[4,1536]{1,0:T(4,128)S(1)} %collective-permute-done.1.refs_3_), custom_call_target="tpu_custom_call" | custom-call | flops 68719476736 | bytes 4718592 | tf_op jit(solution)/shard_map/pallas_call | solution.py:259
  20.3 1.9 %collective-permute-start.2 = (bf16[32,1664]{1,0:T(8,128)(2,1)S(1)}, bf16[32,1664]{1,0:T(8,128)(2,1)S(1)}, u32[]{:S(2)}, u32[]{:S(2)}) collective-permute-start(bf16[32,1664]{1,0:T(8,128)(2,1)S(1)} %get-tuple-element.7), channel_id=1, source_target_pairs={{0,2},{1,3},{2,0},{3,1},{4,6},{5,7},{6,4},{7,5},{8,10},{9,11},{10,... | collective-permute-start | bytes 319496 | tf_op jit(solution)/shard_map/ppermute | solution.py:39
  22.2 5.3 %all-to-all-done.text_ref = bf16[16,4,1536]{2,1,0:T(4,128)(2,1)S(1)} async-done(((bf16[16,4,1536]{2,1,0:T(4,128)(2,1)}), bf16[16,4,1536]{2,1,0:T(4,128)(2,1)S(1)}, u32[]{:S(2)}, u32[]{:S(2)}) %all-to-all-start) | async-done | bytes 196640 | tf_op jit(solution)/shard_map/all_to_all | solution.py:246
  27.6 0.6 collective-permute-start.6
  28.2 2.4 %collective-permute-start.7 = (bf16[64,1536]{1,0:T(8,128)(2,1)S(1)}, bf16[64,1536]{1,0:T(8,128)(2,1)S(1)}, u32[]{:S(2)}, u32[]{:S(2)}) collective-permute-start(bf16[64,1536]{1,0:T(8,128)(2,1)S(1)} %shard_map.90.refs_3_.refs_6_), channel_id=1, source_target_pairs={{0,128},{4,132},{8,136},{12,140},{16,144},{20,148},{24,152},{28,15... | collective-permute-start | bytes 589832 | tf_op jit(solution)/shard_map/ppermute | solution.py:250
  30.6 0.5 collective-permute-start.8
  31.1 1.3 %copy-done = bf16[384,1536]{1,0:T(8,128)(2,1)S(1)} copy-done((bf16[384,1536]{1,0:T(8,128)(2,1)S(1)}, bf16[384,1536]{1,0:T(8,128)(2,1)}, u32[]{:S(2)}) %copy-start) | copy-done | bytes 1179672
  32.4 0.7 %shard_map.88.e0 = f32[8,1536]{1,0:T(8,128)S(1)} custom-call(bf16[32,1664]{1,0:T(8,128)(2,1)S(1)} %get-tuple-element.6.refs_0_.order_ref, bf16[32,1664]{1,0:T(8,128)(2,1)S(1)} %collective-permute-done.2.refs_1_, bf16[1536,768]{1,0:T(8,128)(2,1)S(1)} %bitcast.9, bf16[384,1536]{1,0:T(8,128)(2,1)S(1)} %copy-done), custom_call_target="tpu_custom_call" | custom-call | flops 68719476736 | bytes 2359296 | tf_op jit(solution)/shard_map/pallas_call | solution.py:272
  33.1 2.0 %collective-permute-start.4 = (f32[8,1536]{1,0:T(8,128)S(1)}, f32[8,1536]{1,0:T(8,128)S(1)}, u32[]{:S(2)}, u32[]{:S(2)}) collective-permute-start(f32[8,1536]{1,0:T(8,128)S(1)} %shard_map.88.e0), channel_id=1, source_target_pairs={{0,2},{1,3},{2,0},{3,1},{4,6},{5,7},{6,4},{7,5},{8,10},{9,11},{10,... | collective-permute-start | bytes 147464 | tf_op jit(solution)/shard_map/ppermute | solution.py:39
  35.1 1.4 %collective-permute-start.5 = (f32[8,1536]{1,0:T(8,128)S(1)}, f32[8,1536]{1,0:T(8,128)S(1)}, u32[]{:S(2)}, u32[]{:S(2)}) collective-permute-start(f32[8,1536]{1,0:T(8,128)S(1)} %shard_map.88.e0), channel_id=1, source_target_pairs={{0,3},{1,2},{2,1},{3,0},{4,7},{5,6},{6,5},{7,4},{8,11},{9,10},{10,... | collective-permute-start | bytes 147464 | tf_op jit(solution)/shard_map/ppermute | solution.py:39
  37.8 1.0 %collective-permute-done.4.e2 = f32[8,1536]{1,0:T(8,128)S(1)} collective-permute-done((f32[8,1536]{1,0:T(8,128)S(1)}, f32[8,1536]{1,0:T(8,128)S(1)}, u32[]{:S(2)}, u32[]{:S(2)}) %collective-permute-start.4) | collective-permute-done | bytes 49184 | tf_op jit(solution)/shard_map/ppermute | solution.py:39
  38.8 1.5 %collective-permute-done.5.e3 = f32[8,1536]{1,0:T(8,128)S(1)} collective-permute-done((f32[8,1536]{1,0:T(8,128)S(1)}, f32[8,1536]{1,0:T(8,128)S(1)}, u32[]{:S(2)}, u32[]{:S(2)}) %collective-permute-start.5) | collective-permute-done | bytes 49184 | tf_op jit(solution)/shard_map/ppermute | solution.py:39
  40.4 3.3 %collective-permute-start.10 = (bf16[8,1536]{1,0:T(8,128)(2,1)S(1)}, bf16[8,1536]{1,0:T(8,128)(2,1)S(1)}, u32[]{:S(2)}, u32[]{:S(2)}) collective-permute-start(bf16[8,1536]{1,0:T(8,128)(2,1)S(1)} %shard_map.91.refs_2_), channel_id=1, source_target_pairs={{0,128},{4,132},{8,136},{12,140},{16,144},{20,148},{24,152},{28,15... | collective-permute-start | bytes 73736 | tf_op jit(solution)/shard_map/ppermute | solution.py:250
  43.8 1.4 %collective-permute-start.9 = (bf16[8,1536]{1,0:T(8,128)(2,1)S(1)}, bf16[8,1536]{1,0:T(8,128)(2,1)S(1)}, u32[]{:S(2)}, u32[]{:S(2)}) collective-permute-start(bf16[8,1536]{1,0:T(8,128)(2,1)S(1)} %shard_map.91.refs_2_), channel_id=1, source_target_pairs={{0,64},{4,68},{8,72},{12,76},{16,80},{20,84},{24,88},{28,92},{32,9... | collective-permute-start | bytes 73736 | tf_op jit(solution)/shard_map/ppermute | solution.py:250
  45.2 1.2 %shard_map.92 = (f32[2,1536]{1,0:T(2,128)S(1)}, f32[2,1536]{1,0:T(2,128)S(1)}) custom-call(s32[2]{0:T(128)S(1)} %pad_add_fusion.place_ref.refs_0_, f32[2]{0:T(128)S(1)} %pad_maximum_fusion.refs_1_, bf16[8,1536]{1,0:T(8,128)(2,1)S(1)} %shard_map.91.refs_2_, bf16[64,1536]{1,0:T(8,128)(2,1)S(1)} %shard_map.90.refs_3_.refs_6_, ...), custom_call_target="tpu_custom_call" | custom-call | flops 12582912 | bytes 1572864 | tf_op jit(solution)/shard_map/pallas_call | solution.py:290
  46.5 1.2 %collective-permute-done.12.refs_7_.other_ref = f32[2,1536]{1,0:T(2,128)S(1)} collective-permute-done((f32[2,1536]{1,0:T(2,128)S(1)}, f32[2,1536]{1,0:T(2,128)S(1)}, u32[]{:S(2)}, u32[]{:S(2)}) %collective-permute-start.12) | collective-permute-done | bytes 12320 | tf_op jit(solution)/shard_map/ppermute | solution.py:39
  47.7 1.1 %shard_map.93 = bf16[16,8,384]{2,1,0:T(8,128)(2,1)S(1)} custom-call(s32[2]{0:T(128)S(1)} %pad_add_fusion.place_ref.refs_0_, f32[2]{0:T(128)S(1)} %pad_maximum_fusion.refs_1_, bf16[8,1536]{1,0:T(8,128)(2,1)S(1)} %shard_map.91.refs_2_, bf16[8,1536]{1,0:T(8,128)(2,1)S(1)} %collective-permute-done.9.refs_3_, ...), custom_call_target="tpu_custom_call" | custom-call | flops 12582912 | bytes 196608 | tf_op jit(solution)/shard_map/pallas_call | solution.py:298
  48.8 13.1 %all_to_all.10.part_ref = bf16[16,8,384]{2,1,0:T(8,128)(2,1)S(1)} all-to-all(bf16[16,8,384]{2,1,0:T(8,128)(2,1)S(1)} %shard_map.93), channel_id=1, replica_groups={{0,28,56,20,48,12,40,4,32,60,24,52,16,44,8,36},{64,92,120,84,112,76,104..., dimensions={0} | all-to-all | bytes 196608 | tf_op jit(solution)/shard_map/all_to_all | solution.py:246
  61.9 0.6 %shard_map.94 = (f32[2,1536]{1,0:T(2,128)}, f32[2,1536]{1,0:T(2,128)}) custom-call(bf16[16,8,384]{2,1,0:T(8,128)(2,1)S(1)} %all_to_all.10.part_ref, f32[2,1536]{1,0:T(2,128)S(1)} %get-tuple-element.9.own_ref, f32[2,1536]{1,0:T(2,128)S(1)} %collective-permute-done.12.refs_7_.other_ref), custom_call_target="tpu_custom_call" | custom-call | flops 49152 | bytes 98304 | tf_op jit(solution)/shard_map/pallas_call | solution.py:306
  (27 shorter events, 0.6 us)
Async XLA Ops:
  0.6 16.2 %collective-permute-start = (bf16[8,64,1536]{2,1,0:T(8,128)(2,1)}, bf16[8,64,1536]{2,1,0:T(8,128)(2,1)}, u32[]{:S(2)}, u32[]{:S(2)}) collective-permute-start(bf16[8,64,1536]{2,1,0:T(8,128)(2,1)} %refs_0_.1), channel_id=1, source_target_pairs={{0,1},{1,0},{2,3},{3,2},{4,5},{5,4},{6,7},{7,6},{8,9},{9,8},{10,11... | collective-permute-start | bytes 4718600 | tf_op jit(solution)/shard_map/ppermute | solution.py:39
  0.7 2.2 %copy-start.2 = (bf16[4,96]{1,0:T(4,128)(2,1)S(1)}, bf16[4,96]{1,0:T(4,128)(2,1)}, u32[]{:S(2)}) copy-start(bf16[4,96]{1,0:T(4,128)(2,1)} %param.9) | copy-start | bytes 2308
  2.9 3.8 %copy-start.1 = (bf16[8,1536]{1,0:T(8,128)(2,1)S(1)}, bf16[8,1536]{1,0:T(8,128)(2,1)}, u32[]{:S(2)}) copy-start(bf16[8,1536]{1,0:T(8,128)(2,1)} %captions_ref.1) | copy-start | bytes 73732
  3.4 13.3 %collective-permute-start.1 = (f32[4,1536]{1,0:T(4,128)S(1)}, f32[4,1536]{1,0:T(4,128)S(1)}, u32[]{:S(2)}, u32[]{:S(2)}) collective-permute-start(f32[4,1536]{1,0:T(4,128)S(1)} %shard_map.86.refs_2_.order_ref), channel_id=1, source_target_pairs={{0,2},{1,3},{2,0},{3,1},{4,6},{5,7},{6,4},{7,5},{8,10},{9,11},{10,... | collective-permute-start | bytes 73736 | tf_op jit(solution)/shard_map/ppermute | solution.py:39
  8.1 19.4 %all-to-all-start = ((bf16[16,4,1536]{2,1,0:T(4,128)(2,1)}), bf16[16,4,1536]{2,1,0:T(4,128)(2,1)S(1)}, u32[]{:S(2)}, u32[]{:S(2)}) async-start(bf16[16,4,1536]{2,1,0:T(4,128)(2,1)} %shard_map.89), calls=%async_computation | async-start | bytes 393216 | tf_op jit(solution)/shard_map/all_to_all | solution.py:246
  20.3 10.9 %collective-permute-start.2 = (bf16[32,1664]{1,0:T(8,128)(2,1)S(1)}, bf16[32,1664]{1,0:T(8,128)(2,1)S(1)}, u32[]{:S(2)}, u32[]{:S(2)}) collective-permute-start(bf16[32,1664]{1,0:T(8,128)(2,1)S(1)} %get-tuple-element.7), channel_id=1, source_target_pairs={{0,2},{1,3},{2,0},{3,1},{4,6},{5,7},{6,4},{7,5},{8,10},{9,11},{10,... | collective-permute-start | bytes 319496 | tf_op jit(solution)/shard_map/ppermute | solution.py:39
  27.6 12.7 %collective-permute-start.6 = (bf16[64,1536]{1,0:T(8,128)(2,1)S(1)}, bf16[64,1536]{1,0:T(8,128)(2,1)S(1)}, u32[]{:S(2)}, u32[]{:S(2)}) collective-permute-start(bf16[64,1536]{1,0:T(8,128)(2,1)S(1)} %shard_map.90.refs_3_.refs_6_), channel_id=1, source_target_pairs={{0,64},{4,68},{8,72},{12,76},{16,80},{20,84},{24,88},{28,92},{32,9... | collective-permute-start | bytes 589832 | tf_op jit(solution)/shard_map/ppermute | solution.py:250
  28.2 12.1 %collective-permute-start.7 = (bf16[64,1536]{1,0:T(8,128)(2,1)S(1)}, bf16[64,1536]{1,0:T(8,128)(2,1)S(1)}, u32[]{:S(2)}, u32[]{:S(2)}) collective-permute-start(bf16[64,1536]{1,0:T(8,128)(2,1)S(1)} %shard_map.90.refs_3_.refs_6_), channel_id=1, source_target_pairs={{0,128},{4,132},{8,136},{12,140},{16,144},{20,148},{24,152},{28,15... | collective-permute-start | bytes 589832 | tf_op jit(solution)/shard_map/ppermute | solution.py:250
  30.6 9.7 %collective-permute-start.8 = (bf16[64,1536]{1,0:T(8,128)(2,1)S(1)}, bf16[64,1536]{1,0:T(8,128)(2,1)S(1)}, u32[]{:S(2)}, u32[]{:S(2)}) collective-permute-start(bf16[64,1536]{1,0:T(8,128)(2,1)S(1)} %shard_map.90.refs_3_.refs_6_), channel_id=1, source_target_pairs={{0,192},{4,196},{8,200},{12,204},{16,208},{20,212},{24,216},{28,22... | collective-permute-start | bytes 589832 | tf_op jit(solution)/shard_map/ppermute | solution.py:250
  31.1 1.3 %copy-start = (bf16[384,1536]{1,0:T(8,128)(2,1)S(1)}, bf16[384,1536]{1,0:T(8,128)(2,1)}, u32[]{:S(2)}) copy-start(bf16[384,1536]{1,0:T(8,128)(2,1)} %refs_3_.1) | copy-start | bytes 3538948
  33.1 2.0 %collective-permute-start.3 = (f32[8,1536]{1,0:T(8,128)S(1)}, f32[8,1536]{1,0:T(8,128)S(1)}, u32[]{:S(2)}, u32[]{:S(2)}) collective-permute-start(f32[8,1536]{1,0:T(8,128)S(1)} %shard_map.88.e0), channel_id=1, source_target_pairs={{0,1},{1,0},{2,3},{3,2},{4,5},{5,4},{6,7},{7,6},{8,9},{9,8},{10,11... | collective-permute-start | bytes 147464 | tf_op jit(solution)/shard_map/ppermute | solution.py:39
  33.1 5.7 %collective-permute-start.4 = (f32[8,1536]{1,0:T(8,128)S(1)}, f32[8,1536]{1,0:T(8,128)S(1)}, u32[]{:S(2)}, u32[]{:S(2)}) collective-permute-start(f32[8,1536]{1,0:T(8,128)S(1)} %shard_map.88.e0), channel_id=1, source_target_pairs={{0,2},{1,3},{2,0},{3,1},{4,6},{5,7},{6,4},{7,5},{8,10},{9,11},{10,... | collective-permute-start | bytes 147464 | tf_op jit(solution)/shard_map/ppermute | solution.py:39
  35.1 5.2 %collective-permute-start.5 = (f32[8,1536]{1,0:T(8,128)S(1)}, f32[8,1536]{1,0:T(8,128)S(1)}, u32[]{:S(2)}, u32[]{:S(2)}) collective-permute-start(f32[8,1536]{1,0:T(8,128)S(1)} %shard_map.88.e0), channel_id=1, source_target_pairs={{0,3},{1,2},{2,1},{3,0},{4,7},{5,6},{6,5},{7,4},{8,11},{9,10},{10,... | collective-permute-start | bytes 147464 | tf_op jit(solution)/shard_map/ppermute | solution.py:39
  40.4 7.2 %collective-permute-start.10 = (bf16[8,1536]{1,0:T(8,128)(2,1)S(1)}, bf16[8,1536]{1,0:T(8,128)(2,1)S(1)}, u32[]{:S(2)}, u32[]{:S(2)}) collective-permute-start(bf16[8,1536]{1,0:T(8,128)(2,1)S(1)} %shard_map.91.refs_2_), channel_id=1, source_target_pairs={{0,128},{4,132},{8,136},{12,140},{16,144},{20,148},{24,152},{28,15... | collective-permute-start | bytes 73736 | tf_op jit(solution)/shard_map/ppermute | solution.py:250
  43.8 3.9 %collective-permute-start.11 = (bf16[8,1536]{1,0:T(8,128)(2,1)S(1)}, bf16[8,1536]{1,0:T(8,128)(2,1)S(1)}, u32[]{:S(2)}, u32[]{:S(2)}) collective-permute-start(bf16[8,1536]{1,0:T(8,128)(2,1)S(1)} %shard_map.91.refs_2_), channel_id=1, source_target_pairs={{0,192},{4,196},{8,200},{12,204},{16,208},{20,212},{24,216},{28,22... | collective-permute-start | bytes 73736 | tf_op jit(solution)/shard_map/ppermute | solution.py:250
  43.8 3.9 %collective-permute-start.9 = (bf16[8,1536]{1,0:T(8,128)(2,1)S(1)}, bf16[8,1536]{1,0:T(8,128)(2,1)S(1)}, u32[]{:S(2)}, u32[]{:S(2)}) collective-permute-start(bf16[8,1536]{1,0:T(8,128)(2,1)S(1)} %shard_map.91.refs_2_), channel_id=1, source_target_pairs={{0,64},{4,68},{8,72},{12,76},{16,80},{20,84},{24,88},{28,92},{32,9... | collective-permute-start | bytes 73736 | tf_op jit(solution)/shard_map/ppermute | solution.py:250
  46.4 1.3 %collective-permute-start.12 = (f32[2,1536]{1,0:T(2,128)S(1)}, f32[2,1536]{1,0:T(2,128)S(1)}, u32[]{:S(2)}, u32[]{:S(2)}) collective-permute-start(f32[2,1536]{1,0:T(2,128)S(1)} %get-tuple-element.8), channel_id=1, source_target_pairs={{0,1},{1,0},{2,3},{3,2},{4,5},{5,4},{6,7},{7,6},{8,9},{9,8},{10,11... | collective-permute-start | bytes 36872 | tf_op jit(solution)/shard_map/ppermute | solution.py:39

commit v6 on v5

--- a/solution.py
+++ b/solution.py
@@ -17,13 +17,13 @@
 SMEM = pl.BlockSpec(memory_space=pltpu.SMEM)
 
 
-def call(kernel, outs, specs, flops, moved, scratch=(), limit=12):
+def call(kernel, outs, specs, flops, moved, scratch=(), limit=12, out_specs=None):
     return pl.pallas_call(
         kernel,
         grid=(1,),
         out_shape=outs,
         in_specs=specs,
-        out_specs=jax.tree.map(lambda _: VMEM, outs),
+        out_specs=out_specs or jax.tree.map(lambda _: VMEM, outs),
         scratch_shapes=scratch,
         compiler_params=pltpu.CompilerParams(vmem_limit_bytes=limit << 20),
         cost_estimate=pl.CostEstimate(flops=flops, bytes_accessed=moved, transcendentals=0),
@@ -39,10 +39,39 @@
     return lax.ppermute(piece, "head", [(i, i ^ step) for i in range(4)])
 
 
-def key_query_kernel(spread_ref, key_ref, out_ref, *, scale):
-    out_ref[...] = (
+def first_kernel(
+    place_ref, spread_ref, key_ref, captions_ref, query_ref, text_ref, copies_ref, done, *, scale
+):
+    core = place_ref[1] % 2
+    unit = unit_rows(captions_ref[...]).astype(F32)
+    first = jnp.concatenate([unit[0:2], unit[4:6]], 0)
+    second = jnp.concatenate([unit[2:4], unit[6:8]], 0)
+    chosen = jnp.where(core == 0, first, second)
+    half = chosen.shape[1] // 2
+    chosen = jnp.concatenate([chosen[:, :half], chosen[:, half:]], 0).astype(BF16)
+    copies_ref[...] = jnp.broadcast_to(chosen[None], copies_ref.shape)
+    copy = pltpu.make_async_copy(copies_ref, text_ref, done)
+    copy.start()
+    query_ref[...] = (
         lax.dot_general(spread_ref[...], key_ref[...], NT, preferred_element_type=F32) * scale
     )
+    copy.wait()
+
+
+def halves_product(units, texts):
+    half = texts.shape[1]
+    low = lax.dot_general(units[:, :half], texts, NT, preferred_element_type=F32)
+    high = lax.dot_general(units[:, half:], texts, NT, preferred_element_type=F32)
+    upper = lax.broadcasted_iota(jnp.int32, low.shape, 1) % 8 // 4 == 1
+    own = jnp.where(upper, high, low)
+    count = own.shape[1]
+    return own + jnp.where(upper, pltpu.roll(own, 4, 1), pltpu.roll(own, count - 4, 1))
+
+
+def text_ids(shape, first_dp, images, head):
+    column = lax.broadcasted_iota(jnp.int32, shape, 1)
+    local = column // 8 * 7 % 16
+    return (first_dp + local) * images + column % 4 // 2 * 4 + head % 2 * 2 + column % 2
 
 
 def mix_kernel(own_ref, other_ref, q0, q1, m0, m1, near_ref, done, *, images):
@@ -115,26 +144,6 @@
     out_ref[...] = jnp.dot(pooled.astype(BF16), final_ref[...], preferred_element_type=F32)
 
 
-def text_kernel(place_ref, captions_ref, order_ref, out_ref):
-    core = place_ref[1] % 2
-    unit = unit_rows(captions_ref[...]).astype(F32)
-    first = jnp.concatenate([unit[0:2], unit[4:6]], 0)
-    second = jnp.concatenate([unit[2:4], unit[6:8]], 0)
-    chosen = jnp.where(core == 0, first, second).astype(BF16)
-    out_ref[...] = jnp.broadcast_to(chosen[None], out_ref.shape)
-
-
-def rows_kernel(text_ref, order_ref, rows_ref):
-    texts = text_ref[...].astype(F32)
-    rows_ref[...] = jnp.concatenate([texts[i] for i in range(texts.shape[0])], 0).astype(BF16)
-
-
-def text_ids(shape, first_dp, images, head):
-    column = lax.broadcasted_iota(jnp.int32, shape, 1)
-    local = column // 4 * 7 % 16
-    return (first_dp + local) * images + column % 4 // 2 * 4 + head % 2 * 2 + column % 2
-
-
 def unit_kernel(e0, e1, e2, e3, order1, order2, order3, unit_ref):
     embed = (e0[...] + e1[...]) + (e2[...] + e3[...])
     unit_ref[...] = unit_rows(embed)
@@ -147,16 +156,15 @@
     chunk = width // 4
     block = dp // near
     units = jnp.concatenate([ref[...].astype(F32) for ref in (u0, u1, u2, u3)], 0)
-    logits = lax.dot_general(units.astype(BF16), text_ref[...], NT, preferred_element_type=F32)
-    logits = logits * multiplier + shift
+    logits = halves_product(units.astype(BF16), text_ref[...]) * multiplier + shift
     row = lax.broadcasted_iota(jnp.int32, logits.shape, 0)
     image_id = ((block ^ (row // images)) * near + dp % near) * images + row % images
     text_id = text_ids(logits.shape, block * near, images, head)
     matched = jnp.where(image_id == text_id, 1.0, 0.0)
     coefficient = (multiplier * (jax.nn.sigmoid(logits) - matched)).astype(BF16)
-    source = lax.broadcasted_iota(jnp.int32, (near * 4, near * 8), 0)
-    target = lax.broadcasted_iota(jnp.int32, (near * 4, near * 8), 1)
-    repeat = jnp.where(source == target // 8 * 4 + head // 2 * 2 + target % 8 // 4, 1.0, 0.0)
+    source = lax.broadcasted_iota(jnp.int32, (near * 8, near * 8), 0)
+    target = lax.broadcasted_iota(jnp.int32, (near * 8, near * 8), 1)
+    repeat = jnp.where(source == target // 8 * 8 + head // 2 * 2 + target % 8 // 4, 1.0, 0.0)
     wide = jnp.dot(coefficient, repeat.astype(BF16), preferred_element_type=F32)
     wide = jnp.concatenate([wide] * 4, 0)
     row_chunk = lax.broadcasted_iota(jnp.int32, wide.shape, 0) // (4 * images)
@@ -177,21 +185,24 @@
     block = dp // near
     texts = [ref[...] for ref in (t0, t1, t2, t3)]
     count = texts[0].shape[0]
-    logits = [
-        lax.dot_general(unit_ref[...], part, NT, preferred_element_type=F32) for part in texts
-    ]
-    logits = jnp.concatenate(logits, 1) * multiplier + shift
+    logits = jnp.concatenate([halves_product(unit_ref[...], part) for part in texts], 1)
+    logits = logits * multiplier + shift
     image_id = dp * images + lax.broadcasted_iota(jnp.int32, logits.shape, 0)
     column = lax.broadcasted_iota(jnp.int32, logits.shape, 1)
     first_dp = ((column // count) ^ block) * near
-    text_id = (first_dp + column % count // 4 * 7 % near) * images
+    text_id = (first_dp + column % count // 8 * 7 % near) * images
     text_id = text_id + column % 4 // 2 * 4 + head % 2 * 2 + column % 2
     matched = jnp.where(image_id == text_id, 1.0, 0.0)
-    coefficient = (multiplier * (jax.nn.sigmoid(logits) - matched)).astype(BF16)
+    coefficient = multiplier * (jax.nn.sigmoid(logits) - matched)
+    upper = column % 8 // 4 == 1
+    sides = jnp.concatenate(
+        [jnp.where(upper, 0.0, coefficient), jnp.where(upper, coefficient, 0.0)], 0
+    ).astype(BF16)
     grads = sum(
-        jnp.dot(coefficient[:, s * count : (s + 1) * count], part, preferred_element_type=F32)
+        jnp.dot(sides[:, s * count : (s + 1) * count], part, preferred_element_type=F32)
         for s, part in enumerate(texts)
     )
+    grads = jnp.concatenate([grads[:images], grads[images:]], 1)
     for wanted, ref in ((head, own_ref), (head ^ 1, other_ref)):
         ref[...] = sum(
             jnp.where(wanted == k, grads[k * share : (k + 1) * share], 0.0) for k in range(4)
@@ -231,15 +242,17 @@
         return jax.ShapeDtypeStruct(shape, BF16)
 
     other_tokens = peer(tokens, 1)
-    key_query = call(
-        lambda *refs: key_query_kernel(*refs, scale=1.0 / math.sqrt(head_size)),
-        f32(heads, width),
-        [VMEM, key_spec],
+    place = jnp.stack([dp, head]).astype(jnp.int32)
+    key_query, text_copies = call(
+        lambda *refs: first_kernel(*refs, scale=1.0 / math.sqrt(head_size)),
+        [f32(heads, width), bf16(near, images, width // 2)],
+        [SMEM, VMEM, key_spec, VMEM],
         2 * heads * width * columns,
         2 * width * columns,
-    )(spread, both)
-
-    place = jnp.stack([dp, head]).astype(jnp.int32)
+        [pltpu.VMEM((near, images, width // 2), BF16), pltpu.SemaphoreType.DMA],
+        out_specs=[VMEM, ANY],
+    )(place, spread, both, captions)
+
     groups = [[b * near + i * 7 % near for i in range(near)] for b in range(4)]
 
     def swap(pieces):
@@ -251,10 +264,8 @@
             for s in (1, 2, 3)
         ]
 
-    text_copies = call(
-        text_kernel, bf16(near, 4, width), [SMEM, VMEM, ANY], 6 << 30, 8 * n_dp * width
-    )(place, captions, key_query)
-    copies = swap(text_copies)
+    texts = swap(text_copies).reshape(near * images, width // 2)
+    all_texts = across([texts] * 4)
 
     mixes = call(
         lambda *refs: mix_kernel(*refs, images=images),
@@ -265,10 +276,6 @@
         [pltpu.VMEM((2, *tokens.shape), BF16), pltpu.SemaphoreType.DMA((2,))],
         53,
     )(tokens, other_tokens, key_query, peer(key_query, 2))
-    texts = call(
-        rows_kernel, bf16(near * 4, width), [VMEM, ANY], near * 4 * width, 16 * near * width
-    )(copies, mixes[0])
-    all_texts = across([texts] * 4)
     embeds = call(
         lambda *refs: embed_kernel(*refs, heads=heads),
         f32(images, width),

time: 62.8 us -> 62.7 us (level)
    ppermute x7, waiting for transfers between devices: 3.67 us -> 2.36 us  [peer(): return lax.ppermute(piece, 'head', [(i, i ^ step) for i in range(4)])]
    ppermute x6, waiting for transfers between devices: 0.02 us -> 1.32 us  [across(): lax.ppermute(pieces[s], 'dp', [(i, i ^ s * near) for i in range(n_dp)])]
    pallas_call x3 -> x1, Pallas kernels: 1.8 us -> 1.58 us  [per_device(): call(lambda *refs: first_kernel(*refs, scale=1.0 / math.sqrt(head_size)),...]
where the time goes in v6:
time: 62.7 us; the launch traced here: 62.4 us
  starting transfers between devices  25.6 us (41%)
  blocking collectives  13 us (21%)
  Pallas kernels  9.01 us (14%)
  waiting for transfers between devices  8.96 us (14%)
  local copies, waits for them, and re-layouts  3.52 us (6%)
  between operations  2.08 us (3%)
    all_to_all x1, blocking collectives, swap(): lax.all_to_all(pieces, 'dp', 0, 0, axis_index_groups=groups, tiled=False)  13 us
    ppermute x7, starting transfers between devices, peer(): return lax.ppermute(piece, 'head', [(i, i ^ step) for i in range(4)])  8.76 us
    all_to_all x1, starting transfers between devices, swap(): lax.all_to_all(pieces, 'dp', 0, 0, axis_index_groups=groups, tiled=False)  8.68 us
    ppermute x6, starting transfers between devices, across(): lax.ppermute(pieces[s], 'dp', [(i, i ^ s * near) for i in range(n_dp)])  8.2 us
    all_to_all x1, waiting for transfers between devices, swap(): lax.all_to_all(pieces, 'dp', 0, 0, axis_index_groups=groups, tiled=False)  5.28 us
    pallas_call x1, Pallas kernels, per_device(): call(lambda *refs: mix_kernel(*refs, images=images), [bf16(heads * images...  3.51 us
    unnamed x7, local copies, waits for them, and re-layouts  3.43 us
    ppermute x7, waiting for transfers between devices, peer(): return lax.ppermute(piece, 'head', [(i, i ^ step) for i in range(4)])  2.36 us
  transfers between devices with their start and end apart: 14, of which 4 were waited for; matrix products, arithmetic and copies ran while one was open for 4% of the time, Pallas kernels for 11%

profile of v6, /device:TPU:2, one launch (start us, length us, event | category | flops | bytes accessed | tf_op | source)
XLA Modules:
  0.0 62.4 jit_solution(2255713787375340137)
XLA Ops:
  0.8 2.1 %copy.9 = bf16[192,8,2,384]{3,1,2,0:T(8,128)(2,1)S(1)} copy(bf16[192,8,2,384]{3,2,1,0:T(2,128)(2,1)} %bitcast.16) | data formatting | bytes 4718592
  3.1 1.6 %shard_map.86 = (f32[4,1536]{1,0:T(4,128)S(1)}, bf16[16,8,768]{2,1,0:T(8,128)(2,1)}) custom-call(s32[2]{0:T(128)S(1)} %pad_add_fusion.refs_0_, bf16[4,384]{1,0:T(4,128)(2,1)S(1)} %fusion.refs_1_, bf16[1536,768]{1,0:T(8,128)(2,1)S(1)} %bitcast.9, bf16[8,1536]{1,0:T(8,128)(2,1)S(1)} %copy-done), custom_call_target="tpu_custom_call" | custom-call | flops 4718592 | bytes 1179648 | tf_op jit(solution)/shard_map/pallas_call | solution.py:246
  4.7 3.3 %collective-permute-start.1 = (f32[4,1536]{1,0:T(4,128)S(1)}, f32[4,1536]{1,0:T(4,128)S(1)}, u32[]{:S(2)}, u32[]{:S(2)}) collective-permute-start(f32[4,1536]{1,0:T(4,128)S(1)} %get-tuple-element.8.refs_2_), channel_id=1, source_target_pairs={{0,2},{1,3},{2,0},{3,1},{4,6},{5,7},{6,4},{7,5},{8,10},{9,11},{10,... | collective-permute-start | bytes 73736 | tf_op jit(solution)/shard_map/ppermute | solution.py:39
  8.0 8.7 %all-to-all-start = ((bf16[16,8,768]{2,1,0:T(8,128)(2,1)}), bf16[16,8,768]{2,1,0:T(8,128)(2,1)S(1)}, u32[]{:S(2)}, u32[]{:S(2)}) async-start(bf16[16,8,768]{2,1,0:T(8,128)(2,1)} %get-tuple-element.11), calls=%async_computation | async-start | bytes 393216 | tf_op jit(solution)/shard_map/all_to_all | solution.py:259
  16.7 3.5 %shard_map.87 = (bf16[32,1664]{1,0:T(8,128)(2,1)S(1)}, bf16[32,1664]{1,0:T(8,128)(2,1)S(1)}) custom-call(bf16[8,64,1536]{2,1,0:T(8,128)(2,1)} %refs_0_.1, bf16[8,64,1536]{2,1,0:T(8,128)(2,1)} %collective-permute-done.refs_1_, f32[4,1536]{1,0:T(4,128)S(1)} %get-tuple-element.8.refs_2_, f32[4,1536]{1,0:T(4,128)S(1)} %collective-permute-done.1.refs_3_), custom_call_target="tpu_custom_call" | custom-call | flops 68719476736 | bytes 4718592 | tf_op jit(solution)/shard_map/pallas_call | solution.py:270
  20.2 1.9 %collective-permute-start.2 = (bf16[32,1664]{1,0:T(8,128)(2,1)S(1)}, bf16[32,1664]{1,0:T(8,128)(2,1)S(1)}, u32[]{:S(2)}, u32[]{:S(2)}) collective-permute-start(bf16[32,1664]{1,0:T(8,128)(2,1)S(1)} %get-tuple-element.10), channel_id=1, source_target_pairs={{0,2},{1,3},{2,0},{3,1},{4,6},{5,7},{6,4},{7,5},{8,10},{9,11},{10,... | collective-permute-start | bytes 319496 | tf_op jit(solution)/shard_map/ppermute | solution.py:39
  22.1 5.3 %all-to-all-done = bf16[16,8,768]{2,1,0:T(8,128)(2,1)S(1)} async-done(((bf16[16,8,768]{2,1,0:T(8,128)(2,1)}), bf16[16,8,768]{2,1,0:T(8,128)(2,1)S(1)}, u32[]{:S(2)}, u32[]{:S(2)}) %all-to-all-start) | async-done | bytes 196640 | tf_op jit(solution)/shard_map/all_to_all | solution.py:259
  27.4 0.5 collective-permute-start.6
  27.9 2.4 %collective-permute-start.7 = (bf16[128,768]{1,0:T(8,128)(2,1)S(1)}, bf16[128,768]{1,0:T(8,128)(2,1)S(1)}, u32[]{:S(2)}, u32[]{:S(2)}) collective-permute-start(bf16[128,768]{1,0:T(8,128)(2,1)S(1)} %bitcast.12), channel_id=1, source_target_pairs={{0,128},{4,132},{8,136},{12,140},{16,144},{20,148},{24,152},{28,15... | collective-permute-start | bytes 589832 | tf_op jit(solution)/shard_map/ppermute | solution.py:263
  30.4 0.5 collective-permute-start.8
  30.9 1.3 %copy-done.1 = bf16[384,1536]{1,0:T(8,128)(2,1)S(1)} copy-done((bf16[384,1536]{1,0:T(8,128)(2,1)S(1)}, bf16[384,1536]{1,0:T(8,128)(2,1)}, u32[]{:S(2)}) %copy-start.1) | copy-done | bytes 1179672
  32.2 0.7 %shard_map.88.e0 = f32[8,1536]{1,0:T(8,128)S(1)} custom-call(bf16[32,1664]{1,0:T(8,128)(2,1)S(1)} %get-tuple-element.9.refs_0_, bf16[32,1664]{1,0:T(8,128)(2,1)S(1)} %collective-permute-done.2.refs_1_, bf16[1536,768]{1,0:T(8,128)(2,1)S(1)} %bitcast.10, bf16[384,1536]{1,0:T(8,128)(2,1)S(1)} %copy-done.1), custom_call_target="tpu_custom_call" | custom-call | flops 68719476736 | bytes 2359296 | tf_op jit(solution)/shard_map/pallas_call | solution.py:279
  32.9 2.0 %collective-permute-start.4 = (f32[8,1536]{1,0:T(8,128)S(1)}, f32[8,1536]{1,0:T(8,128)S(1)}, u32[]{:S(2)}, u32[]{:S(2)}) collective-permute-start(f32[8,1536]{1,0:T(8,128)S(1)} %shard_map.88.e0), channel_id=1, source_target_pairs={{0,2},{1,3},{2,0},{3,1},{4,6},{5,7},{6,4},{7,5},{8,10},{9,11},{10,... | collective-permute-start | bytes 147464 | tf_op jit(solution)/shard_map/ppermute | solution.py:39
  34.9 1.4 %collective-permute-start.5 = (f32[8,1536]{1,0:T(8,128)S(1)}, f32[8,1536]{1,0:T(8,128)S(1)}, u32[]{:S(2)}, u32[]{:S(2)}) collective-permute-start(f32[8,1536]{1,0:T(8,128)S(1)} %shard_map.88.e0), channel_id=1, source_target_pairs={{0,3},{1,2},{2,1},{3,0},{4,7},{5,6},{6,5},{7,4},{8,11},{9,10},{10,... | collective-permute-start | bytes 147464 | tf_op jit(solution)/shard_map/ppermute | solution.py:39
  37.6 1.3 %collective-permute-done.8.order3.refs_6_ = bf16[128,768]{1,0:T(8,128)(2,1)S(1)} collective-permute-done((bf16[128,768]{1,0:T(8,128)(2,1)S(1)}, bf16[128,768]{1,0:T(8,128)(2,1)S(1)}, u32[]{:S(2)}, u32[]{:S(2)}) %collective-permute-start.8) | collective-permute-done | bytes 196640 | tf_op jit(solution)/shard_map/ppermute | solution.py:263
  38.9 1.2 %collective-permute-done.5.e3 = f32[8,1536]{1,0:T(8,128)S(1)} collective-permute-done((f32[8,1536]{1,0:T(8,128)S(1)}, f32[8,1536]{1,0:T(8,128)S(1)}, u32[]{:S(2)}, u32[]{:S(2)}) %collective-permute-start.5) | collective-permute-done | bytes 49184 | tf_op jit(solution)/shard_map/ppermute | solution.py:39
  40.1 0.1 shard_map.89.refs_2_
  40.2 3.3 %collective-permute-start.10 = (bf16[8,1536]{1,0:T(8,128)(2,1)S(1)}, bf16[8,1536]{1,0:T(8,128)(2,1)S(1)}, u32[]{:S(2)}, u32[]{:S(2)}) collective-permute-start(bf16[8,1536]{1,0:T(8,128)(2,1)S(1)} %shard_map.89.refs_2_), channel_id=1, source_target_pairs={{0,128},{4,132},{8,136},{12,140},{16,144},{20,148},{24,152},{28,15... | collective-permute-start | bytes 73736 | tf_op jit(solution)/shard_map/ppermute | solution.py:263
  43.5 1.4 %collective-permute-start.9 = (bf16[8,1536]{1,0:T(8,128)(2,1)S(1)}, bf16[8,1536]{1,0:T(8,128)(2,1)S(1)}, u32[]{:S(2)}, u32[]{:S(2)}) collective-permute-start(bf16[8,1536]{1,0:T(8,128)(2,1)S(1)} %shard_map.89.refs_2_), channel_id=1, source_target_pairs={{0,64},{4,68},{8,72},{12,76},{16,80},{20,84},{24,88},{28,92},{32,9... | collective-permute-start | bytes 73736 | tf_op jit(solution)/shard_map/ppermute | solution.py:263
  44.9 1.3 %shard_map.90 = (f32[2,1536]{1,0:T(2,128)S(1)}, f32[2,1536]{1,0:T(2,128)S(1)}) custom-call(s32[2]{0:T(128)S(1)} %pad_add_fusion.refs_0_, f32[2]{0:T(128)S(1)} %pad_maximum_fusion.refs_1_, bf16[8,1536]{1,0:T(8,128)(2,1)S(1)} %shard_map.89.refs_2_, bf16[128,768]{1,0:T(8,128)(2,1)S(1)} %bitcast.14, bf16[128,768]{1,0:T(8,128)(2,1)S(1)} %collective-permute-done.6.order1.refs_4_, ...), custom_call_target="tpu_custom_call" | custom-call | flops 12582912 | bytes 1572864 | tf_op jit(solution)/shard_map/pallas_call | solution.py:297
  46.4 1.2 %collective-permute-done.12.refs_7_.other_ref = f32[2,1536]{1,0:T(2,128)S(1)} collective-permute-done((f32[2,1536]{1,0:T(2,128)S(1)}, f32[2,1536]{1,0:T(2,128)S(1)}, u32[]{:S(2)}, u32[]{:S(2)}) %collective-permute-start.12) | collective-permute-done | bytes 12320 | tf_op jit(solution)/shard_map/ppermute | solution.py:39
  47.6 1.2 %shard_map.91 = bf16[16,8,384]{2,1,0:T(8,128)(2,1)S(1)} custom-call(s32[2]{0:T(128)S(1)} %pad_add_fusion.refs_0_, f32[2]{0:T(128)S(1)} %pad_maximum_fusion.refs_1_, bf16[8,1536]{1,0:T(8,128)(2,1)S(1)} %shard_map.89.refs_2_, bf16[8,1536]{1,0:T(8,128)(2,1)S(1)} %collective-permute-done.9.refs_3_, bf16[8,1536]{1,0:T(8,128)(2,1)S(1)} %collective-permute-done.10.refs_4_, ...), custom_call_target="tpu_custom_call" | custom-call | flops 12582912 | bytes 196608 | tf_op jit(solution)/shard_map/pallas_call | solution.py:305
  48.8 13.0 %all_to_all.10.part_ref = bf16[16,8,384]{2,1,0:T(8,128)(2,1)S(1)} all-to-all(bf16[16,8,384]{2,1,0:T(8,128)(2,1)S(1)} %shard_map.91), channel_id=1, replica_groups={{0,28,56,20,48,12,40,4,32,60,24,52,16,44,8,36},{64,92,120,84,112,76,104..., dimensions={0} | all-to-all | bytes 196608 | tf_op jit(solution)/shard_map/all_to_all | solution.py:259
  61.7 0.6 %shard_map.92 = (f32[2,1536]{1,0:T(2,128)}, f32[2,1536]{1,0:T(2,128)}) custom-call(bf16[16,8,384]{2,1,0:T(8,128)(2,1)S(1)} %all_to_all.10.part_ref, f32[2,1536]{1,0:T(2,128)S(1)} %get-tuple-element.13.own_ref, f32[2,1536]{1,0:T(2,128)S(1)} %collective-permute-done.12.refs_7_.other_ref), custom_call_target="tpu_custom_call" | custom-call | flops 49152 | bytes 98304 | tf_op jit(solution)/shard_map/pallas_call | solution.py:313
  (25 shorter events, 0.5 us)
Async XLA Ops:
  0.6 16.1 %collective-permute-start = (bf16[8,64,1536]{2,1,0:T(8,128)(2,1)}, bf16[8,64,1536]{2,1,0:T(8,128)(2,1)}, u32[]{:S(2)}, u32[]{:S(2)}) collective-permute-start(bf16[8,64,1536]{2,1,0:T(8,128)(2,1)} %refs_0_.1), channel_id=1, source_target_pairs={{0,1},{1,0},{2,3},{3,2},{4,5},{5,4},{6,7},{7,6},{8,9},{9,8},{10,11... | collective-permute-start | bytes 4718600 | tf_op jit(solution)/shard_map/ppermute | solution.py:39
  0.7 2.2 %copy-start.2 = (bf16[4,96]{1,0:T(4,128)(2,1)S(1)}, bf16[4,96]{1,0:T(4,128)(2,1)}, u32[]{:S(2)}) copy-start(bf16[4,96]{1,0:T(4,128)(2,1)} %param.9) | copy-start | bytes 2308
  0.7 2.4 %copy-start = (bf16[8,1536]{1,0:T(8,128)(2,1)S(1)}, bf16[8,1536]{1,0:T(8,128)(2,1)}, u32[]{:S(2)}) copy-start(bf16[8,1536]{1,0:T(8,128)(2,1)} %refs_3_.2) | copy-start | bytes 73732
  4.7 12.0 %collective-permute-start.1 = (f32[4,1536]{1,0:T(4,128)S(1)}, f32[4,1536]{1,0:T(4,128)S(1)}, u32[]{:S(2)}, u32[]{:S(2)}) collective-permute-start(f32[4,1536]{1,0:T(4,128)S(1)} %get-tuple-element.8.refs_2_), channel_id=1, source_target_pairs={{0,2},{1,3},{2,0},{3,1},{4,6},{5,7},{6,4},{7,5},{8,10},{9,11},{10,... | collective-permute-start | bytes 73736 | tf_op jit(solution)/shard_map/ppermute | solution.py:39
  8.0 19.4 %all-to-all-start = ((bf16[16,8,768]{2,1,0:T(8,128)(2,1)}), bf16[16,8,768]{2,1,0:T(8,128)(2,1)S(1)}, u32[]{:S(2)}, u32[]{:S(2)}) async-start(bf16[16,8,768]{2,1,0:T(8,128)(2,1)} %get-tuple-element.11), calls=%async_computation | async-start | bytes 393216 | tf_op jit(solution)/shard_map/all_to_all | solution.py:259
  20.2 10.7 %collective-permute-start.2 = (bf16[32,1664]{1,0:T(8,128)(2,1)S(1)}, bf16[32,1664]{1,0:T(8,128)(2,1)S(1)}, u32[]{:S(2)}, u32[]{:S(2)}) collective-permute-start(bf16[32,1664]{1,0:T(8,128)(2,1)S(1)} %get-tuple-element.10), channel_id=1, source_target_pairs={{0,2},{1,3},{2,0},{3,1},{4,6},{5,7},{6,4},{7,5},{8,10},{9,11},{10,... | collective-permute-start | bytes 319496 | tf_op jit(solution)/shard_map/ppermute | solution.py:39
  27.4 7.5 %collective-permute-start.6 = (bf16[128,768]{1,0:T(8,128)(2,1)S(1)}, bf16[128,768]{1,0:T(8,128)(2,1)S(1)}, u32[]{:S(2)}, u32[]{:S(2)}) collective-permute-start(bf16[128,768]{1,0:T(8,128)(2,1)S(1)} %bitcast.11), channel_id=1, source_target_pairs={{0,64},{4,68},{8,72},{12,76},{16,80},{20,84},{24,88},{28,92},{32,9... | collective-permute-start | bytes 589832 | tf_op jit(solution)/shard_map/ppermute | solution.py:263
  27.9 9.6 %collective-permute-start.7 = (bf16[128,768]{1,0:T(8,128)(2,1)S(1)}, bf16[128,768]{1,0:T(8,128)(2,1)S(1)}, u32[]{:S(2)}, u32[]{:S(2)}) collective-permute-start(bf16[128,768]{1,0:T(8,128)(2,1)S(1)} %bitcast.12), channel_id=1, source_target_pairs={{0,128},{4,132},{8,136},{12,140},{16,144},{20,148},{24,152},{28,15... | collective-permute-start | bytes 589832 | tf_op jit(solution)/shard_map/ppermute | solution.py:263
  30.4 8.5 %collective-permute-start.8 = (bf16[128,768]{1,0:T(8,128)(2,1)S(1)}, bf16[128,768]{1,0:T(8,128)(2,1)S(1)}, u32[]{:S(2)}, u32[]{:S(2)}) collective-permute-start(bf16[128,768]{1,0:T(8,128)(2,1)S(1)} %bitcast.13), channel_id=1, source_target_pairs={{0,192},{4,196},{8,200},{12,204},{16,208},{20,212},{24,216},{28,22... | collective-permute-start | bytes 589832 | tf_op jit(solution)/shard_map/ppermute | solution.py:263
  30.9 1.3 %copy-start.1 = (bf16[384,1536]{1,0:T(8,128)(2,1)S(1)}, bf16[384,1536]{1,0:T(8,128)(2,1)}, u32[]{:S(2)}) copy-start(bf16[384,1536]{1,0:T(8,128)(2,1)} %refs_3_.3) | copy-start | bytes 3538948
  32.9 6.0 %collective-permute-start.3 = (f32[8,1536]{1,0:T(8,128)S(1)}, f32[8,1536]{1,0:T(8,128)S(1)}, u32[]{:S(2)}, u32[]{:S(2)}) collective-permute-start(f32[8,1536]{1,0:T(8,128)S(1)} %shard_map.88.e0), channel_id=1, source_target_pairs={{0,1},{1,0},{2,3},{3,2},{4,5},{5,4},{6,7},{7,6},{8,9},{9,8},{10,11... | collective-permute-start | bytes 147464 | tf_op jit(solution)/shard_map/ppermute | solution.py:39
  32.9 6.0 %collective-permute-start.4 = (f32[8,1536]{1,0:T(8,128)S(1)}, f32[8,1536]{1,0:T(8,128)S(1)}, u32[]{:S(2)}, u32[]{:S(2)}) collective-permute-start(f32[8,1536]{1,0:T(8,128)S(1)} %shard_map.88.e0), channel_id=1, source_target_pairs={{0,2},{1,3},{2,0},{3,1},{4,6},{5,7},{6,4},{7,5},{8,10},{9,11},{10,... | collective-permute-start | bytes 147464 | tf_op jit(solution)/shard_map/ppermute | solution.py:39
  34.9 5.2 %collective-permute-start.5 = (f32[8,1536]{1,0:T(8,128)S(1)}, f32[8,1536]{1,0:T(8,128)S(1)}, u32[]{:S(2)}, u32[]{:S(2)}) collective-permute-start(f32[8,1536]{1,0:T(8,128)S(1)} %shard_map.88.e0), channel_id=1, source_target_pairs={{0,3},{1,2},{2,1},{3,0},{4,7},{5,6},{6,5},{7,4},{8,11},{9,10},{10,... | collective-permute-start | bytes 147464 | tf_op jit(solution)/shard_map/ppermute | solution.py:39
  40.2 7.4 %collective-permute-start.10 = (bf16[8,1536]{1,0:T(8,128)(2,1)S(1)}, bf16[8,1536]{1,0:T(8,128)(2,1)S(1)}, u32[]{:S(2)}, u32[]{:S(2)}) collective-permute-start(bf16[8,1536]{1,0:T(8,128)(2,1)S(1)} %shard_map.89.refs_2_), channel_id=1, source_target_pairs={{0,128},{4,132},{8,136},{12,140},{16,144},{20,148},{24,152},{28,15... | collective-permute-start | bytes 73736 | tf_op jit(solution)/shard_map/ppermute | solution.py:263
  43.5 4.0 %collective-permute-start.11 = (bf16[8,1536]{1,0:T(8,128)(2,1)S(1)}, bf16[8,1536]{1,0:T(8,128)(2,1)S(1)}, u32[]{:S(2)}, u32[]{:S(2)}) collective-permute-start(bf16[8,1536]{1,0:T(8,128)(2,1)S(1)} %shard_map.89.refs_2_), channel_id=1, source_target_pairs={{0,192},{4,196},{8,200},{12,204},{16,208},{20,212},{24,216},{28,22... | collective-permute-start | bytes 73736 | tf_op jit(solution)/shard_map/ppermute | solution.py:263
  43.5 4.0 %collective-permute-start.9 = (bf16[8,1536]{1,0:T(8,128)(2,1)S(1)}, bf16[8,1536]{1,0:T(8,128)(2,1)S(1)}, u32[]{:S(2)}, u32[]{:S(2)}) collective-permute-start(bf16[8,1536]{1,0:T(8,128)(2,1)S(1)} %shard_map.89.refs_2_), channel_id=1, source_target_pairs={{0,64},{4,68},{8,72},{12,76},{16,80},{20,84},{24,88},{28,92},{32,9... | collective-permute-start | bytes 73736 | tf_op jit(solution)/shard_map/ppermute | solution.py:263
  46.3 1.3 %collective-permute-start.12 = (f32[2,1536]{1,0:T(2,128)S(1)}, f32[2,1536]{1,0:T(2,128)S(1)}, u32[]{:S(2)}, u32[]{:S(2)}) collective-permute-start(f32[2,1536]{1,0:T(2,128)S(1)} %get-tuple-element.12), channel_id=1, source_target_pairs={{0,1},{1,0},{2,3},{3,2},{4,5},{5,4},{6,7},{7,6},{8,9},{9,8},{10,11... | collective-permute-start | bytes 36872 | tf_op jit(solution)/shard_map/ppermute | solution.py:39

commit v7 on v4

--- a/solution.py
+++ b/solution.py
@@ -97,7 +97,7 @@
         ref[:, width:] = pieces[s * step : (s + 1) * step]
 
 
-def embed_kernel(m0, m1, value_ref, final_ref, out_ref, near_ref, done, *, heads):
+def embed_kernel(m0, m1, value_ref, final_ref, out_ref, short_ref, near_ref, done, *, heads):
     copy = pltpu.make_async_copy(final_ref, near_ref, done)
     copy.start()
     width = value_ref.shape[0]
@@ -115,7 +115,9 @@
     kept = jnp.where(row_head == column_head, pooled, 0.0)
     pooled = sum(kept[h * images : (h + 1) * images] for h in range(heads))
     copy.wait()
-    out_ref[...] = jnp.dot(pooled.astype(BF16), near_ref[...], preferred_element_type=F32)
+    embed = jnp.dot(pooled.astype(BF16), near_ref[...], preferred_element_type=F32)
+    out_ref[...] = embed
+    short_ref[...] = embed.astype(BF16)
 
 
 def text_kernel(place_ref, captions_ref, order_ref, out_ref):
@@ -138,7 +140,8 @@
 
 
 def unit_kernel(e0, e1, e2, e3, order1, order2, order3, unit_ref):
-    embed = (e0[...] + e1[...]) + (e2[...] + e3[...])
+    parts = [ref[...].astype(F32) for ref in (e0, e1, e2, e3)]
+    embed = (parts[0] + parts[1]) + (parts[2] + parts[3])
     unit_ref[...] = unit_rows(embed)
 
 
@@ -271,16 +274,16 @@
         rows_kernel, bf16(near * 4, width), [VMEM, ANY], near * 4 * width, 16 * near * width
     )(copies, mixes[0])
     all_texts = across([texts] * 4)
-    embeds = call(
+    embeds, short_embeds = call(
         lambda *refs: embed_kernel(*refs, heads=heads),
-        f32(images, width),
+        [f32(images, width), bf16(images, width)],
         [VMEM, VMEM, value_spec, ANY],
         64 << 30,
         4 * width * columns,
         [pltpu.VMEM(final.shape, BF16), pltpu.SemaphoreType.DMA],
         52,
     )(mixes[0], peer(mixes[1], 2), both, final)
-    embeds = [embeds] + [peer(embeds, s) for s in (1, 2, 3)]
+    embeds = [embeds] + [peer(short_embeds, s) for s in (1, 2, 3)]
 
     scalars = jnp.stack([multiplier, shift])
     unit = call(

time: 63 us -> 62.9 us (level)
  no operation moved by 1% of the time
where the time goes in v7:
time: 62.9 us; the launch traced here: 62.5 us
  starting transfers between devices  25.8 us (41%)
  blocking collectives  12.9 us (21%)
  Pallas kernels  10.6 us (17%)
  waiting for transfers between devices  8.76 us (14%)
  local copies, waits for them, and re-layouts  2.25 us (4%)
  between operations  2.09 us (3%)
    all_to_all x1, blocking collectives, swap(): lax.all_to_all(pieces, 'dp', 0, 0, axis_index_groups=groups, tiled=False)  12.9 us
    ppermute x7, starting transfers between devices, peer(): return lax.ppermute(piece, 'head', [(i, i ^ step) for i in range(4)])  8.8 us
    all_to_all x1, starting transfers between devices, swap(): lax.all_to_all(pieces, 'dp', 0, 0, axis_index_groups=groups, tiled=False)  8.68 us
    ppermute x6, starting transfers between devices, across(): lax.ppermute(pieces[s], 'dp', [(i, i ^ s * near) for i in range(n_dp)])  8.29 us
    all_to_all x1, waiting for transfers between devices, swap(): lax.all_to_all(pieces, 'dp', 0, 0, axis_index_groups=groups, tiled=False)  5.55 us
    pallas_call x1, Pallas kernels, per_device(): call(lambda *refs: mix_kernel(*refs, images=images), [bf16(heads * images...  3.59 us
    ppermute x7, waiting for transfers between devices, peer(): return lax.ppermute(piece, 'head', [(i, i ^ step) for i in range(4)])  3.19 us
    pallas_call x1, Pallas kernels, per_device(): call(lambda *refs: embed_kernel(*refs, heads=heads), [f32(images, width),...  2.24 us
  transfers between devices with their start and end apart: 14, of which 4 were waited for; matrix products, arithmetic and copies ran while one was open for 4% of the time, Pallas kernels for 14%

profile of v7, /device:TPU:2, one launch (start us, length us, event | category | flops | bytes accessed | tf_op | source)
XLA Modules:
  0.0 62.5 jit_solution(15800214831594985753)
XLA Ops:
  0.7 2.1 %copy.9 = bf16[192,8,2,384]{3,1,2,0:T(8,128)(2,1)S(1)} copy(bf16[192,8,2,384]{3,2,1,0:T(2,128)(2,1)} %bitcast.10) | data formatting | bytes 4718592
  3.0 0.4 shard_map.86.refs_2_.order_ref
  3.5 3.2 %collective-permute-start.1 = (f32[4,1536]{1,0:T(4,128)S(1)}, f32[4,1536]{1,0:T(4,128)S(1)}, u32[]{:S(2)}, u32[]{:S(2)}) collective-permute-start(f32[4,1536]{1,0:T(4,128)S(1)} %shard_map.86.refs_2_.order_ref), channel_id=1, source_target_pairs={{0,2},{1,3},{2,0},{3,1},{4,6},{5,7},{6,4},{7,5},{8,10},{9,11},{10,... | collective-permute-start | bytes 73736 | tf_op jit(solution)/shard_map/ppermute | solution.py:39
  6.7 1.3 %shard_map.89 = bf16[16,4,1536]{2,1,0:T(4,128)(2,1)} custom-call(s32[2]{0:T(128)S(1)} %pad_add_fusion.place_ref.refs_0_, bf16[8,1536]{1,0:T(8,128)(2,1)S(1)} %copy-done.2, f32[4,1536]{1,0:T(4,128)S(1)} %shard_map.86.refs_2_.order_ref), custom_call_target="tpu_custom_call" | custom-call | flops 6442450944 | bytes 786432 | tf_op jit(solution)/shard_map/pallas_call | solution.py:259
  8.1 8.7 %all-to-all-start = ((bf16[16,4,1536]{2,1,0:T(4,128)(2,1)}), bf16[16,4,1536]{2,1,0:T(4,128)(2,1)S(1)}, u32[]{:S(2)}, u32[]{:S(2)}) async-start(bf16[16,4,1536]{2,1,0:T(4,128)(2,1)} %shard_map.89), calls=%async_computation | async-start | bytes 393216 | tf_op jit(solution)/shard_map/all_to_all | solution.py:251
  16.8 3.6 %shard_map.87 = (bf16[32,1664]{1,0:T(8,128)(2,1)S(1)}, bf16[32,1664]{1,0:T(8,128)(2,1)S(1)}) custom-call(bf16[8,64,1536]{2,1,0:T(8,128)(2,1)} %refs_0_.1, bf16[8,64,1536]{2,1,0:T(8,128)(2,1)} %collective-permute-done.refs_1_, f32[4,1536]{1,0:T(4,128)S(1)} %shard_map.86.refs_2_.order_ref, f32[4,1536]{1,0:T(4,128)S(1)} %collective-permute-done.1.refs_3_), custom_call_target="tpu_custom_call" | custom-call | flops 68719476736 | bytes 4718592 | tf_op jit(solution)/shard_map/pallas_call | solution.py:264
  20.4 1.9 %collective-permute-start.2 = (bf16[32,1664]{1,0:T(8,128)(2,1)S(1)}, bf16[32,1664]{1,0:T(8,128)(2,1)S(1)}, u32[]{:S(2)}, u32[]{:S(2)}) collective-permute-start(bf16[32,1664]{1,0:T(8,128)(2,1)S(1)} %get-tuple-element.9), channel_id=1, source_target_pairs={{0,2},{1,3},{2,0},{3,1},{4,6},{5,7},{6,4},{7,5},{8,10},{9,11},{10,... | collective-permute-start | bytes 319496 | tf_op jit(solution)/shard_map/ppermute | solution.py:39
  22.3 5.6 %all-to-all-done.text_ref = bf16[16,4,1536]{2,1,0:T(4,128)(2,1)S(1)} async-done(((bf16[16,4,1536]{2,1,0:T(4,128)(2,1)}), bf16[16,4,1536]{2,1,0:T(4,128)(2,1)S(1)}, u32[]{:S(2)}, u32[]{:S(2)}) %all-to-all-start) | async-done | bytes 196640 | tf_op jit(solution)/shard_map/all_to_all | solution.py:251
  27.9 0.6 collective-permute-start.6
  28.6 2.4 %collective-permute-start.7 = (bf16[64,1536]{1,0:T(8,128)(2,1)S(1)}, bf16[64,1536]{1,0:T(8,128)(2,1)S(1)}, u32[]{:S(2)}, u32[]{:S(2)}) collective-permute-start(bf16[64,1536]{1,0:T(8,128)(2,1)S(1)} %shard_map.90.refs_3_.refs_6_), channel_id=1, source_target_pairs={{0,128},{4,132},{8,136},{12,140},{16,144},{20,148},{24,152},{28,15... | collective-permute-start | bytes 589832 | tf_op jit(solution)/shard_map/ppermute | solution.py:255
  31.0 0.5 collective-permute-start.8
  31.5 2.2 %shard_map.88 = (f32[8,1536]{1,0:T(8,128)S(1)}, bf16[8,1536]{1,0:T(8,128)(2,1)S(1)}) custom-call(bf16[32,1664]{1,0:T(8,128)(2,1)S(1)} %get-tuple-element.8.refs_0_.order_ref, bf16[32,1664]{1,0:T(8,128)(2,1)S(1)} %collective-permute-done.2.refs_1_, bf16[1536,768]{1,0:T(8,128)(2,1)} %bitcast.9, bf16[384,1536]{1,0:T(8,128)(2,1)S(1)} %copy-done.1), custom_call_target="tpu_custom_call" | custom-call | flops 68719476736 | bytes 2359296 | tf_op jit(solution)/shard_map/pallas_call | solution.py:277
  33.9 1.9 %collective-permute-start.4 = (bf16[8,1536]{1,0:T(8,128)(2,1)S(1)}, bf16[8,1536]{1,0:T(8,128)(2,1)S(1)}, u32[]{:S(2)}, u32[]{:S(2)}) collective-permute-start(bf16[8,1536]{1,0:T(8,128)(2,1)S(1)} %get-tuple-element.11), channel_id=1, source_target_pairs={{0,2},{1,3},{2,0},{3,1},{4,6},{5,7},{6,4},{7,5},{8,10},{9,11},{10,... | collective-permute-start | bytes 73736 | tf_op jit(solution)/shard_map/ppermute | solution.py:39
  35.8 1.4 %collective-permute-start.5 = (bf16[8,1536]{1,0:T(8,128)(2,1)S(1)}, bf16[8,1536]{1,0:T(8,128)(2,1)S(1)}, u32[]{:S(2)}, u32[]{:S(2)}) collective-permute-start(bf16[8,1536]{1,0:T(8,128)(2,1)S(1)} %get-tuple-element.11), channel_id=1, source_target_pairs={{0,3},{1,2},{2,1},{3,0},{4,7},{5,6},{6,5},{7,4},{8,11},{9,10},{10,... | collective-permute-start | bytes 73736 | tf_op jit(solution)/shard_map/ppermute | solution.py:39
  38.5 0.7 %collective-permute-done.4.e2 = bf16[8,1536]{1,0:T(8,128)(2,1)S(1)} collective-permute-done((bf16[8,1536]{1,0:T(8,128)(2,1)S(1)}, bf16[8,1536]{1,0:T(8,128)(2,1)S(1)}, u32[]{:S(2)}, u32[]{:S(2)}) %collective-permute-start.4) | collective-permute-done | bytes 24608 | tf_op jit(solution)/shard_map/ppermute | solution.py:39
  39.3 1.3 %collective-permute-done.5.e3 = bf16[8,1536]{1,0:T(8,128)(2,1)S(1)} collective-permute-done((bf16[8,1536]{1,0:T(8,128)(2,1)S(1)}, bf16[8,1536]{1,0:T(8,128)(2,1)S(1)}, u32[]{:S(2)}, u32[]{:S(2)}) %collective-permute-start.5) | collective-permute-done | bytes 24608 | tf_op jit(solution)/shard_map/ppermute | solution.py:39
  40.6 0.1 shard_map.91.refs_2_
  40.7 3.3 %collective-permute-start.10 = (bf16[8,1536]{1,0:T(8,128)(2,1)S(1)}, bf16[8,1536]{1,0:T(8,128)(2,1)S(1)}, u32[]{:S(2)}, u32[]{:S(2)}) collective-permute-start(bf16[8,1536]{1,0:T(8,128)(2,1)S(1)} %shard_map.91.refs_2_), channel_id=1, source_target_pairs={{0,128},{4,132},{8,136},{12,140},{16,144},{20,148},{24,152},{28,15... | collective-permute-start | bytes 73736 | tf_op jit(solution)/shard_map/ppermute | solution.py:255
  44.1 1.3 %collective-permute-start.9 = (bf16[8,1536]{1,0:T(8,128)(2,1)S(1)}, bf16[8,1536]{1,0:T(8,128)(2,1)S(1)}, u32[]{:S(2)}, u32[]{:S(2)}) collective-permute-start(bf16[8,1536]{1,0:T(8,128)(2,1)S(1)} %shard_map.91.refs_2_), channel_id=1, source_target_pairs={{0,64},{4,68},{8,72},{12,76},{16,80},{20,84},{24,88},{28,92},{32,9... | collective-permute-start | bytes 73736 | tf_op jit(solution)/shard_map/ppermute | solution.py:255
  45.5 1.2 %shard_map.92 = (f32[2,1536]{1,0:T(2,128)S(1)}, f32[2,1536]{1,0:T(2,128)S(1)}) custom-call(s32[2]{0:T(128)S(1)} %pad_add_fusion.place_ref.refs_0_, f32[2]{0:T(128)S(1)} %pad_maximum_fusion.refs_1_, bf16[8,1536]{1,0:T(8,128)(2,1)S(1)} %shard_map.91.refs_2_, bf16[64,1536]{1,0:T(8,128)(2,1)S(1)} %shard_map.90.refs_3_.refs_6_, ...), custom_call_target="tpu_custom_call" | custom-call | flops 12582912 | bytes 1572864 | tf_op jit(solution)/shard_map/pallas_call | solution.py:297
  46.7 1.2 %collective-permute-done.12.refs_7_.other_ref = f32[2,1536]{1,0:T(2,128)S(1)} collective-permute-done((f32[2,1536]{1,0:T(2,128)S(1)}, f32[2,1536]{1,0:T(2,128)S(1)}, u32[]{:S(2)}, u32[]{:S(2)}) %collective-permute-start.12) | collective-permute-done | bytes 12320 | tf_op jit(solution)/shard_map/ppermute | solution.py:39
  47.9 1.1 %shard_map.93 = bf16[16,8,384]{2,1,0:T(8,128)(2,1)S(1)} custom-call(s32[2]{0:T(128)S(1)} %pad_add_fusion.place_ref.refs_0_, f32[2]{0:T(128)S(1)} %pad_maximum_fusion.refs_1_, bf16[8,1536]{1,0:T(8,128)(2,1)S(1)} %shard_map.91.refs_2_, bf16[8,1536]{1,0:T(8,128)(2,1)S(1)} %collective-permute-done.9.refs_3_, ...), custom_call_target="tpu_custom_call" | custom-call | flops 12582912 | bytes 196608 | tf_op jit(solution)/shard_map/pallas_call | solution.py:305
  49.0 12.9 %all_to_all.10.part_ref = bf16[16,8,384]{2,1,0:T(8,128)(2,1)S(1)} all-to-all(bf16[16,8,384]{2,1,0:T(8,128)(2,1)S(1)} %shard_map.93), channel_id=1, replica_groups={{0,4,8,12,16,20,24,28,32,36,40,44,48,52,56,60},{64,68,72,76,80,84,88,92..., dimensions={0} | all-to-all | bytes 196608 | tf_op jit(solution)/shard_map/all_to_all | solution.py:251
  61.9 0.6 %shard_map.94 = (f32[2,1536]{1,0:T(2,128)}, f32[2,1536]{1,0:T(2,128)}) custom-call(bf16[16,8,384]{2,1,0:T(8,128)(2,1)S(1)} %all_to_all.10.part_ref, f32[2,1536]{1,0:T(2,128)S(1)} %get-tuple-element.13.own_ref, f32[2,1536]{1,0:T(2,128)S(1)} %collective-permute-done.12.refs_7_.other_ref), custom_call_target="tpu_custom_call" | custom-call | flops 49152 | bytes 98304 | tf_op jit(solution)/shard_map/pallas_call | solution.py:313
  (29 shorter events, 0.7 us)
Async XLA Ops:
  0.6 16.2 %collective-permute-start = (bf16[8,64,1536]{2,1,0:T(8,128)(2,1)}, bf16[8,64,1536]{2,1,0:T(8,128)(2,1)}, u32[]{:S(2)}, u32[]{:S(2)}) collective-permute-start(bf16[8,64,1536]{2,1,0:T(8,128)(2,1)} %refs_0_.1), channel_id=1, source_target_pairs={{0,1},{1,0},{2,3},{3,2},{4,5},{5,4},{6,7},{7,6},{8,9},{9,8},{10,11... | collective-permute-start | bytes 4718600 | tf_op jit(solution)/shard_map/ppermute | solution.py:39
  0.7 2.2 %copy-start.3 = (bf16[4,96]{1,0:T(4,128)(2,1)S(1)}, bf16[4,96]{1,0:T(4,128)(2,1)}, u32[]{:S(2)}) copy-start(bf16[4,96]{1,0:T(4,128)(2,1)} %param.9) | copy-start | bytes 2308
  2.9 5.2 %copy-start = (bf16[192,8,2,384]{3,1,2,0:T(8,128)(2,1)}, bf16[192,8,2,384]{3,1,2,0:T(8,128)(2,1)S(1)}, u32[]{:S(2)}) copy-start(bf16[192,8,2,384]{3,1,2,0:T(8,128)(2,1)S(1)} %copy.9) | copy-start | bytes 7077892
  2.9 3.8 %copy-start.2 = (bf16[8,1536]{1,0:T(8,128)(2,1)S(1)}, bf16[8,1536]{1,0:T(8,128)(2,1)}, u32[]{:S(2)}) copy-start(bf16[8,1536]{1,0:T(8,128)(2,1)} %captions_ref.1) | copy-start | bytes 73732
  3.5 13.3 %collective-permute-start.1 = (f32[4,1536]{1,0:T(4,128)S(1)}, f32[4,1536]{1,0:T(4,128)S(1)}, u32[]{:S(2)}, u32[]{:S(2)}) collective-permute-start(f32[4,1536]{1,0:T(4,128)S(1)} %shard_map.86.refs_2_.order_ref), channel_id=1, source_target_pairs={{0,2},{1,3},{2,0},{3,1},{4,6},{5,7},{6,4},{7,5},{8,10},{9,11},{10,... | collective-permute-start | bytes 73736 | tf_op jit(solution)/shard_map/ppermute | solution.py:39
  8.1 19.8 %all-to-all-start = ((bf16[16,4,1536]{2,1,0:T(4,128)(2,1)}), bf16[16,4,1536]{2,1,0:T(4,128)(2,1)S(1)}, u32[]{:S(2)}, u32[]{:S(2)}) async-start(bf16[16,4,1536]{2,1,0:T(4,128)(2,1)} %shard_map.89), calls=%async_computation | async-start | bytes 393216 | tf_op jit(solution)/shard_map/all_to_all | solution.py:251
  16.8 14.8 %copy-start.1 = (bf16[384,1536]{1,0:T(8,128)(2,1)S(1)}, bf16[384,1536]{1,0:T(8,128)(2,1)}, u32[]{:S(2)}) copy-start(bf16[384,1536]{1,0:T(8,128)(2,1)} %refs_3_.1) | copy-start | bytes 3538948
  20.4 11.1 %collective-permute-start.2 = (bf16[32,1664]{1,0:T(8,128)(2,1)S(1)}, bf16[32,1664]{1,0:T(8,128)(2,1)S(1)}, u32[]{:S(2)}, u32[]{:S(2)}) collective-permute-start(bf16[32,1664]{1,0:T(8,128)(2,1)S(1)} %get-tuple-element.9), channel_id=1, source_target_pairs={{0,2},{1,3},{2,0},{3,1},{4,6},{5,7},{6,4},{7,5},{8,10},{9,11},{10,... | collective-permute-start | bytes 319496 | tf_op jit(solution)/shard_map/ppermute | solution.py:39
  27.9 12.6 %collective-permute-start.6 = (bf16[64,1536]{1,0:T(8,128)(2,1)S(1)}, bf16[64,1536]{1,0:T(8,128)(2,1)S(1)}, u32[]{:S(2)}, u32[]{:S(2)}) collective-permute-start(bf16[64,1536]{1,0:T(8,128)(2,1)S(1)} %shard_map.90.refs_3_.refs_6_), channel_id=1, source_target_pairs={{0,64},{4,68},{8,72},{12,76},{16,80},{20,84},{24,88},{28,92},{32,9... | collective-permute-start | bytes 589832 | tf_op jit(solution)/shard_map/ppermute | solution.py:255
  28.6 12.0 %collective-permute-start.7 = (bf16[64,1536]{1,0:T(8,128)(2,1)S(1)}, bf16[64,1536]{1,0:T(8,128)(2,1)S(1)}, u32[]{:S(2)}, u32[]{:S(2)}) collective-permute-start(bf16[64,1536]{1,0:T(8,128)(2,1)S(1)} %shard_map.90.refs_3_.refs_6_), channel_id=1, source_target_pairs={{0,128},{4,132},{8,136},{12,140},{16,144},{20,148},{24,152},{28,15... | collective-permute-start | bytes 589832 | tf_op jit(solution)/shard_map/ppermute | solution.py:255
  31.0 9.6 %collective-permute-start.8 = (bf16[64,1536]{1,0:T(8,128)(2,1)S(1)}, bf16[64,1536]{1,0:T(8,128)(2,1)S(1)}, u32[]{:S(2)}, u32[]{:S(2)}) collective-permute-start(bf16[64,1536]{1,0:T(8,128)(2,1)S(1)} %shard_map.90.refs_3_.refs_6_), channel_id=1, source_target_pairs={{0,192},{4,196},{8,200},{12,204},{16,208},{20,212},{24,216},{28,22... | collective-permute-start | bytes 589832 | tf_op jit(solution)/shard_map/ppermute | solution.py:255
  33.8 2.0 %collective-permute-start.3 = (bf16[8,1536]{1,0:T(8,128)(2,1)S(1)}, bf16[8,1536]{1,0:T(8,128)(2,1)S(1)}, u32[]{:S(2)}, u32[]{:S(2)}) collective-permute-start(bf16[8,1536]{1,0:T(8,128)(2,1)S(1)} %get-tuple-element.11), channel_id=1, source_target_pairs={{0,1},{1,0},{2,3},{3,2},{4,5},{5,4},{6,7},{7,6},{8,9},{9,8},{10,11... | collective-permute-start | bytes 73736 | tf_op jit(solution)/shard_map/ppermute | solution.py:39
  33.9 5.4 %collective-permute-start.4 = (bf16[8,1536]{1,0:T(8,128)(2,1)S(1)}, bf16[8,1536]{1,0:T(8,128)(2,1)S(1)}, u32[]{:S(2)}, u32[]{:S(2)}) collective-permute-start(bf16[8,1536]{1,0:T(8,128)(2,1)S(1)} %get-tuple-element.11), channel_id=1, source_target_pairs={{0,2},{1,3},{2,0},{3,1},{4,6},{5,7},{6,4},{7,5},{8,10},{9,11},{10,... | collective-permute-start | bytes 73736 | tf_op jit(solution)/shard_map/ppermute | solution.py:39
  35.8 4.8 %collective-permute-start.5 = (bf16[8,1536]{1,0:T(8,128)(2,1)S(1)}, bf16[8,1536]{1,0:T(8,128)(2,1)S(1)}, u32[]{:S(2)}, u32[]{:S(2)}) collective-permute-start(bf16[8,1536]{1,0:T(8,128)(2,1)S(1)} %get-tuple-element.11), channel_id=1, source_target_pairs={{0,3},{1,2},{2,1},{3,0},{4,7},{5,6},{6,5},{7,4},{8,11},{9,10},{10,... | collective-permute-start | bytes 73736 | tf_op jit(solution)/shard_map/ppermute | solution.py:39
  40.7 7.2 %collective-permute-start.10 = (bf16[8,1536]{1,0:T(8,128)(2,1)S(1)}, bf16[8,1536]{1,0:T(8,128)(2,1)S(1)}, u32[]{:S(2)}, u32[]{:S(2)}) collective-permute-start(bf16[8,1536]{1,0:T(8,128)(2,1)S(1)} %shard_map.91.refs_2_), channel_id=1, source_target_pairs={{0,128},{4,132},{8,136},{12,140},{16,144},{20,148},{24,152},{28,15... | collective-permute-start | bytes 73736 | tf_op jit(solution)/shard_map/ppermute | solution.py:255
  44.0 3.9 %collective-permute-start.11 = (bf16[8,1536]{1,0:T(8,128)(2,1)S(1)}, bf16[8,1536]{1,0:T(8,128)(2,1)S(1)}, u32[]{:S(2)}, u32[]{:S(2)}) collective-permute-start(bf16[8,1536]{1,0:T(8,128)(2,1)S(1)} %shard_map.91.refs_2_), channel_id=1, source_target_pairs={{0,192},{4,196},{8,200},{12,204},{16,208},{20,212},{24,216},{28,22... | collective-permute-start | bytes 73736 | tf_op jit(solution)/shard_map/ppermute | solution.py:255
  44.1 3.9 %collective-permute-start.9 = (bf16[8,1536]{1,0:T(8,128)(2,1)S(1)}, bf16[8,1536]{1,0:T(8,128)(2,1)S(1)}, u32[]{:S(2)}, u32[]{:S(2)}) collective-permute-start(bf16[8,1536]{1,0:T(8,128)(2,1)S(1)} %shard_map.91.refs_2_), channel_id=1, source_target_pairs={{0,64},{4,68},{8,72},{12,76},{16,80},{20,84},{24,88},{28,92},{32,9... | collective-permute-start | bytes 73736 | tf_op jit(solution)/shard_map/ppermute | solution.py:255
  46.6 1.3 %collective-permute-start.12 = (f32[2,1536]{1,0:T(2,128)S(1)}, f32[2,1536]{1,0:T(2,128)S(1)}, u32[]{:S(2)}, u32[]{:S(2)}) collective-permute-start(f32[2,1536]{1,0:T(2,128)S(1)} %get-tuple-element.12), channel_id=1, source_target_pairs={{0,1},{1,0},{2,3},{3,2},{4,5},{5,4},{6,7},{7,6},{8,9},{9,8},{10,11... | collective-permute-start | bytes 36872 | tf_op jit(solution)/shard_map/ppermute | solution.py:39
